TPU v7x, 32 devices: a whole 2x2x4 slice. The times are simulated.
32 devices in a mesh: dp: 4 (over y, x), fsdp: 8 (over z, core).
Axes of the slice: x: 2, y: 2, z: 4, core: 2. Of those that a mesh axis runs over, the one named last changes fastest.
Arguments:
- tokens: bfloat16 [4096, 8192], P(('dp', 'fsdp')), may hold values from -6 to 6
- frozen_key_matrix: bfloat16 [8192, 512], P('fsdp'), may hold values from -0.0625 to 0.0625
- adapter_down_factor: float32 [24, 8192, 16], P('fsdp', 'dp'), may hold values from -0.0625 to 0.0625
- adapter_up_factor: float32 [24, 16, 512], P('fsdp', None, 'dp'), may hold values from -1.5 to 1.5
- key_norm_gain: float32 [128], replicated, may hold values from 0.1 to 1.9
- adapter_offset: int32 [4, 8], P('dp', 'fsdp'), may hold values from 0 to 2, as said below
- loss_row_count: int32 [4, 8], P('dp', 'fsdp'), may hold values from 32 to 128, as said below
- cotangent: bfloat16 [4096, 512], P(('dp', 'fsdp')), may hold values from -6 to 6
Outputs:
- keys: bfloat16 [4096, 512], P(('dp', 'fsdp'))
- input_grad: bfloat16 [4096, 8192], P(('dp', 'fsdp'))
- down_grad: float32 [24, 8192, 16], P('fsdp', 'dp')
- up_factor_gradient: float32 [24, 16, 512], P('fsdp', None, 'dp')
Inputs may be any that keep to these rules, and one draw needn't show every extreme that they name: `adapter_offset`: in every column j, each offset 0 to 2 is named by at least one dp index. `loss_row_count`: some block has 128 live rows and some block 32.
All inputs are finite; a program needn't handle non-finite values.
Results may differ from a plain program's by a relative error of at most 0.0033.
Values may be sent and summed in bfloat16 or wider, within the bound.
No kernel may reach another device: no remote copies, remote signals or barrier semaphores. Data moves between devices by JAX's collectives and lax.ppermute only.
A program may use at most 64 MiB of HBM per device.

v0:
```python
import jax
import jax.numpy as jnp
from jax import lax
from jax.sharding import PartitionSpec as P

HD = 128


adapter_scale = 2.0
norm_eps = 1e-06


def on_device(
    tokens,
    frozen_key_matrix,
    adapter_down_factor,
    adapter_up_factor,
    key_norm_gain,
    adapter_offset,
    loss_row_count,
    cotangent,
):
    highest_precision = lax.Precision.HIGHEST
    row_count = tokens.shape[0]
    key_width = frozen_key_matrix.shape[1]
    stored_values = adapter_down_factor.shape[0]
    slot_value = adapter_offset[0, 0]
    live_count = loss_row_count[0, 0]
    selector = jnp.arange(stored_values, dtype=jnp.int32) == slot_value
    counted = jnp.where(selector, live_count, 0)
    summed_rows = lax.psum(counted, "dp")
    adapter_total = jnp.sum(jnp.where(selector, summed_rows, 0)).astype(jnp.float32)
    down_whole, up_whole = (
        lax.all_gather(adapter_down_factor, "dp", axis=1, tiled=True),
        lax.all_gather(adapter_up_factor, "dp", axis=2, tiled=True),
    )
    down_projection = lax.dynamic_index_in_dim(down_whole, slot_value, 0, keepdims=False)
    up_projection = lax.dynamic_index_in_dim(up_whole, slot_value, 0, keepdims=False)
    weight = lax.all_gather(frozen_key_matrix, "fsdp", axis=0, tiled=True)
    frozen_output = jnp.dot(tokens, weight, preferred_element_type=jnp.float32)
    tokens_float = tokens.astype(jnp.float32)
    lowrank_output = jnp.dot(tokens_float, down_projection, precision=highest_precision)
    projected_keys = frozen_output + adapter_scale * jnp.dot(
        lowrank_output, up_projection, precision=highest_precision
    )
    shaped = projected_keys.reshape(row_count, -1, HD)
    mean_square = jnp.mean(shaped * shaped, axis=-1, keepdims=True)
    inverse_rms = lax.rsqrt(mean_square + norm_eps)
    normed = shaped * inverse_rms
    keys = (normed * key_norm_gain).reshape(row_count, key_width).astype(jnp.bfloat16)
    row_mask = (jnp.arange(row_count, dtype=jnp.int32) < live_count).astype(jnp.float32)
    row_grad = cotangent.astype(jnp.float32) * row_mask[:, None] * (row_count / adapter_total)
    scaled_grad = row_grad.reshape(normed.shape) * key_norm_gain
    along_norm = jnp.mean(scaled_grad * normed, axis=-1, keepdims=True)
    prenorm_gradient = (inverse_rms * (scaled_grad - normed * along_norm)).reshape(
        row_count, key_width
    )
    pre_grad_low = prenorm_gradient.astype(jnp.bfloat16)
    lowrank_gradient = adapter_scale * jnp.dot(
        prenorm_gradient, up_projection.T, precision=highest_precision
    )
    input_base = lax.dot_general(
        pre_grad_low, weight, (((1,), (1,)), ((), ())), preferred_element_type=jnp.float32
    )
    input_grad = (
        input_base + jnp.dot(lowrank_gradient, down_projection.T, precision=highest_precision)
    ).astype(jnp.bfloat16)
    down_grad = lax.dot_general(
        tokens_float, lowrank_gradient, (((0,), (0,)), ((), ())), precision=highest_precision
    )
    up_factor_gradient = adapter_scale * lax.dot_general(
        lowrank_output, prenorm_gradient, (((0,), (0,)), ((), ())), precision=highest_precision
    )
    selector_float = selector.astype(jnp.float32)
    down_terms = selector_float[:, None, None] * down_grad[None]
    up_terms = selector_float[:, None, None] * up_factor_gradient[None]
    down_sum, up_sum = (
        lax.psum_scatter(down_terms, "dp", scatter_dimension=1, tiled=True),
        lax.psum_scatter(up_terms, "dp", scatter_dimension=2, tiled=True),
    )
    return (keys, input_grad, down_sum, up_sum)


def solution(mesh):
    placed = (
        P(("dp", "fsdp"), None),
        P("fsdp", None),
        P("fsdp", "dp", None),
        P("fsdp", None, "dp"),
        P(),
        P("dp", "fsdp"),
        P("dp", "fsdp"),
        P(("dp", "fsdp"), None),
    )
    return jax.shard_map(
        on_device,
        mesh=mesh,
        in_specs=placed,
        out_specs=(
            P(("dp", "fsdp"), None),
            P(("dp", "fsdp"), None),
            P("fsdp", "dp", None),
            P("fsdp", None, "dp"),
        ),
        check_vma=False,
    )
```

profile of v0, /device:TPU:0, one launch (start us, length us, event | category | flops | bytes accessed | tf_op | source)
XLA Modules:
  0.0 200.1 jit_solution(571422882816724202)
XLA Ops:
  7.2 0.0 copy-start
  7.2 0.0 copy-start.2
  7.2 0.0 copy-start.3
  7.2 0.0 all-gather.5.cloned.1.call-start
  7.2 0.7 all-gather.5.cloned.1.call-update
  7.9 0.0 all-gather.3.cloned.1.call-start
  8.0 0.7 all-gather.3.cloned.1.call-update
  8.7 0.0 reduce-scatter.5.cloned.1.call-start
  10.0 8.9 %psum.7 = s32[3]{0:T(128)S(1)} all-reduce(s32[3]{0:T(128)S(1)} %fusion.16), channel_id=1, replica_groups=mesh['dp'=4,'fsdp'=8] {'dp'}, use_global_device_ids=true, to_apply=%region_1.2 | all-reduce | flops 3 | bytes 24 | tf_op jit(solution)/shard_map/psum | solution.py:31
  18.9 0.6 select_reduce_fusion
  20.2 1.0 multiply_multiply_fusion
  21.2 0.1 reshape.48
  21.4 0.0 copy-done.2
  21.4 9.2 %all_gather.11 = f32[3,16,512]{2,1,0:T(8,128)S(1)} all-gather(f32[3,16,128]{2,1,0:T(8,128)S(1)} %copy-done.2), channel_id=1, replica_groups=mesh['dp'=4,'fsdp'=8] {'dp'}, dimensions={2}, use_global_device_ids=true | all-gather | bytes 122880 | tf_op jit(solution)/shard_map/all_gather | solution.py:35
  30.6 0.0 copy-done.3
  30.6 13.6 %all-gather.5.cloned.1.call-done = f32[3,8192,16]{1,2,0:T(8,128)} async-done(((f32[3,2048,16]{1,2,0:T(8,128)}), f32[3,8192,16]{1,2,0:T(8,128)}) %all-gather.5.cloned.1.call-update) | async-done | bytes 1572880 | tf_op jit(solution)/shard_map/all_gather | solution.py:34
  44.1 0.0 copy-done
  44.1 2.8 %fusion.3 = f32[16,128]{1,0:T(8,128)S(1)} fusion(bf16[128,8192]{1,0:T(8,128)(2,1)S(1)} %copy-done, f32[3,8192,16]{1,2,0:T(8,128)} %all-gather.5.cloned.1.call-done, s32[]{:T(128)S(6)} %select_n.14), kind=kOutput, calls=%fused_computation.9 | convolution fusion | flops 201326592 | bytes 2629636 | tf_op jit(solution)/shard_map/dot_general | solution.py:42
  46.9 80.9 %all-gather.3.cloned.1.call-done = bf16[8192,512]{1,0:T(8,128)(2,1)} async-done(((bf16[1024,512]{1,0:T(8,128)(2,1)}), bf16[8192,512]{1,0:T(8,128)(2,1)}) %all-gather.3.cloned.1.call-update) | async-done | bytes 8388624 | tf_op jit(solution)/shard_map/all_gather | solution.py:39
  127.8 4.6 %fusion.21 = f32[128,512]{1,0:T(8,128)S(1)} fusion(bf16[128,8192]{1,0:T(8,128)(2,1)S(1)} %copy-done, bf16[8192,512]{1,0:T(8,128)(2,1)} %all-gather.3.cloned.1.call-done), kind=kOutput, calls=%fused_computation.40 | convolution fusion | flops 1073741824 | bytes 10747904 | tf_op jit(solution)/shard_map/dot_general | solution.py:40
  132.5 0.0 copy-start.1
  132.5 0.4 fusion.1
  132.9 0.1 reshape.47
  133.0 0.2 multiply_reduce_fusion.1
  133.3 0.4 multiply_reduce_fusion
  133.6 0.2 mul.139
  133.8 0.2 mul.123
  134.0 0.0 copy-done.1
  134.1 0.7 fusion.8
  134.8 0.3 convolution_multiply_fusion.2
  135.0 0.3 convolution_multiply_fusion.1
  135.3 0.9 convolution_bitcast_fusion
  136.3 0.7 broadcast_multiply_fusion.1
  137.0 0.0 reduce-scatter.5.cloned.1.call-update
  137.0 0.0 reduce-scatter.3.cloned.1.call-start
  137.0 1.3 broadcast_multiply_fusion
  138.4 0.0 reduce-scatter.3.cloned.1.call-update
  138.4 6.2 %fusion.9 = f32[128,8192]{1,0:T(8,128)S(1)} fusion(bf16[8192,512]{1,0:T(8,128)(2,1)} %all-gather.3.cloned.1.call-done, f32[128,512]{1,0:T(8,128)S(1)} %get-tuple-element.4), kind=kOutput, calls=%fused_computation.21 | convolution fusion | flops 1073807360 | bytes 12845056 | tf_op jit(solution)/shard_map/dot_general | solution.py:62
  144.6 5.9 %fusion = bf16[128,8192]{1,0:T(8,128)(2,1)} fusion(f32[128,8192]{1,0:T(8,128)S(1)} %fusion.9, f32[128,16]{0,1:T(8,128)S(1)} %convolution_multiply_fusion.2, f32[3,8192,16]{1,2,0:T(8,128)} %all-gather.5.cloned.1.call-done, s32[]{:T(128)S(6)} %select_n.14), kind=kOutput, calls=%fused_computation.1 | convolution fusion | flops 203423744 | bytes 6823940 | tf_op jit(solution)/shard_map/dot_general | solution.py:66
  150.5 8.4 %reduce-scatter.5.cloned.1.call-done = f32[3,16,128]{2,1,0:T(8,128)} async-done(((f32[3,16,512]{2,1,0:T(8,128)}), f32[3,16,128]{2,1,0:T(8,128)}) %reduce-scatter.5.cloned.1.call-update) | async-done | bytes 24592 | tf_op jit(solution)/shard_map/reduce_scatter | solution.py:79
  158.9 34.6 %reduce-scatter.3.cloned.1.call-done = f32[3,2048,16]{1,2,0:T(8,128)} async-done(((f32[3,8192,16]{1,2,0:T(8,128)}), f32[3,2048,16]{1,2,0:T(8,128)}) %reduce-scatter.3.cloned.1.call-update) | async-done | bytes 393232 | tf_op jit(solution)/shard_map/reduce_scatter | solution.py:78
  (6 shorter events, 0.0 us)
Async XLA Ops:
  7.2 37.0 %copy-start = (bf16[128,8192]{1,0:T(8,128)(2,1)S(1)}, bf16[128,8192]{1,0:T(8,128)(2,1)}, u32[]{:S(2)}) copy-start(bf16[128,8192]{1,0:T(8,128)(2,1)} %param.8) | copy-start | bytes 6291460
  7.2 14.2 %copy-start.2 = (f32[3,16,128]{2,1,0:T(8,128)S(1)}, f32[3,16,128]{2,1,0:T(8,128)}, u32[]{:S(2)}) copy-start(f32[3,16,128]{2,1,0:T(8,128)} %param.11) | copy-start | bytes 73732
  7.2 23.4 %copy-start.3 = (f32[128]{0:T(128)S(1)}, f32[128]{0:T(128)}, u32[]{:S(2)}) copy-start(f32[128]{0:T(128)} %param.12) | copy-start | bytes 1540
  7.2 36.9 %all-gather.5.cloned.1.call-start = ((), (), s32[]{:S(2)}) async-start(), calls=%async_computation.3 | async-start | bytes 1966080 | tf_op jit(solution)/shard_map/all_gather | solution.py:34
  7.9 119.9 %all-gather.3.cloned.1.call-start = ((), (), s32[]{:S(2)}) async-start(), calls=%async_computation.2 | async-start | bytes 9437184 | tf_op jit(solution)/shard_map/all_gather | solution.py:39
  8.7 150.2 %reduce-scatter.5.cloned.1.call-start = ((), (), s32[]{:S(2)}) async-start(), calls=%async_computation.5 | async-start | bytes 122880 | tf_op jit(solution)/shard_map/reduce_scatter | solution.py:79
  132.5 1.6 copy-start.1
  137.0 56.6 %reduce-scatter.3.cloned.1.call-start = ((), (), s32[]{:S(2)}) async-start(), calls=%async_computation.4 | async-start | bytes 1966080 | tf_op jit(solution)/shard_map/reduce_scatter | solution.py:78
Sparse Core Ops, SparseCore 0:
  9.9 34.2 all-gather.4
  45.7 82.0 all-gather.2
  137.1 21.7 reduce-scatter.4
  162.6 30.9 reduce-scatter.2
where the time goes:
time: 200 us
  waiting for transfers between devices  139 us (70%)
  matrix products  21.4 us (11%)
  blocking collectives  18 us (9%)
  between operations  15.9 us (8%)
  other arithmetic  4.98 us (2%)
    all_gather x1, waiting for transfers between devices, on_device(): weight = lax.all_gather(frozen_key_matrix, 'fsdp', axis=0, tiled=True)  80.9 us
    reduce_scatter x1, waiting for transfers between devices, on_device(): lax.psum_scatter(down_terms, 'dp', scatter_dimension=1, tiled=True)  34.6 us
    all_gather x1, waiting for transfers between devices, on_device(): lax.all_gather(adapter_down_factor, 'dp', axis=1, tiled=True)  13.6 us
    all_gather x1, blocking collectives, on_device(): lax.all_gather(adapter_up_factor, 'dp', axis=2, tiled=True)  9.19 us
    psum x1, blocking collectives, on_device(): summed_rows = lax.psum(counted, 'dp')  8.85 us
    reduce_scatter x1, waiting for transfers between devices, on_device(): lax.psum_scatter(up_terms, 'dp', scatter_dimension=2, tiled=True)  8.44 us
    dot_general x1, matrix products, on_device(): lax.dot_general(pre_grad_low, weight, (((1,), (1,)), ((), ())), preferred...  6.19 us
    dot_general x1, matrix products, on_device(): jnp.dot(lowrank_gradient, down_projection.T, precision=highest_precision)  5.9 us
  transfers between devices with their start and end apart: 4, of which 4 were waited for; matrix products, arithmetic and copies ran while one was open for 9% of the time, Pallas kernels for 0%

commit v1 on v0

v1 whole, which is shorter than its diff:
```python
import functools

import jax
import jax.numpy as jnp
from jax import lax
from jax.experimental import pallas as pl
from jax.experimental.pallas import tpu as pltpu
from jax.sharding import PartitionSpec as P

HD = 128
CORES = 2

adapter_scale = 2.0
norm_eps = 1e-06

F32 = jnp.float32
BF16 = jnp.bfloat16
HIGHEST = lax.Precision.HIGHEST
VMEM_LIMIT = 48 * 2**20

vmem = pl.BlockSpec(memory_space=pltpu.VMEM)
smem = pl.BlockSpec(memory_space=pltpu.SMEM)


def split_two(value):
    high = value.astype(BF16)
    low = (value - high.astype(F32)).astype(BF16)
    return high, low


def call(kernel, outs, ins, name, flops=0, moved=0):
    return pl.pallas_call(
        kernel,
        out_shape=[jax.ShapeDtypeStruct(shape, dtype) for shape, dtype in outs],
        in_specs=[spec for spec, _ in ins],
        out_specs=[vmem] * len(outs),
        compiler_params=pltpu.CompilerParams(vmem_limit_bytes=VMEM_LIMIT),
        cost_estimate=pl.CostEstimate(flops=flops, bytes_accessed=moved, transcendentals=0),
        name=name,
    )(*[value for _, value in ins])


def messages_kernel(slots, down, up, *outs):
    width = down.shape[2]
    for partner, out in enumerate(outs):
        slot = slots[partner]
        out[:, :width] = down[slot]
        out[:, width:] = up[slot]


def low_rank_kernel(place, tokens, *refs):
    parts = len(refs) - 4
    messages, (split, up, low_rank, added) = refs[:parts], refs[parts:]
    rank = messages[0].shape[0]
    up_width = up.shape[1] // parts
    down_width = tokens.shape[1] // parts
    for partner, message in enumerate(messages):
        part = place[0] ^ partner
        columns = pl.ds(pl.multiple_of(part * down_width, 128), down_width)
        high, low = split_two(message[:, :down_width])
        split[:rank, columns] = high
        split[rank:, columns] = low
        columns = pl.ds(pl.multiple_of(part * up_width, 128), up_width)
        up[:, columns] = message[:, down_width:]
    both = lax.dot_general(tokens[...], split[...], (((1,), (1,)), ((), ())), preferred_element_type=F32)
    low_rank[...] = both[:, :rank] + both[:, rank:]
    added[...] = adapter_scale * jnp.dot(low_rank[...], up[...], precision=HIGHEST, preferred_element_type=F32)


def column_of(place, piece, part_rows):
    shard = (place[1] ^ piece["z"]) * CORES + (place[2] ^ piece["core"])
    part = 0 if piece["dp"] is None else place[0] ^ piece["dp"]
    column = (shard * piece["parts"] + part) * part_rows + piece["offset"]
    return pl.multiple_of(column, 128)


def base_sum(place, tokens, total, buffers, pieces, part_rows):
    for piece in pieces:
        columns = pl.ds(column_of(place, piece, part_rows), piece["rows"])
        rows = pl.ds(piece["first"], piece["rows"])
        total = total + jnp.dot(tokens[:, columns], buffers[piece["buffer"]][rows, :], preferred_element_type=F32)
    return total


def base_kernel(pieces, part_rows, place, tokens, before, *refs):
    refs[-1][...] = base_sum(place, tokens, before[...], refs[:-1], pieces, part_rows)


def middle_kernel(pieces, part_rows, parts, place, scale, tokens, before, cotangent, gain, low_rank, up, *refs):
    count = len(refs) - 3 - parts
    buffers, (keys, pre_low, low_grad), grads = refs[:count], refs[count : count + 3], refs[count + 3 :]
    projected = base_sum(place, tokens, before[...], buffers, pieces, part_rows)
    rows, width = projected.shape
    gains = gain[...]
    live = lax.broadcasted_iota(jnp.int32, (rows, 1), 0) < place[3]
    weight = jnp.where(live, scale[0], 0.0)
    heads = []
    for head in range(width // HD):
        columns = slice(head * HD, (head + 1) * HD)
        values = projected[:, columns]
        inverse = lax.rsqrt(jnp.mean(values * values, axis=-1, keepdims=True) + norm_eps)
        normed = values * inverse
        keys[:, columns] = (normed * gains).astype(BF16)
        scaled = cotangent[:, columns].astype(F32) * weight * gains
        along = jnp.mean(scaled * normed, axis=-1, keepdims=True)
        heads.append(inverse * (scaled - normed * along))
    pre = jnp.concatenate(heads, axis=-1)
    pre_low[...] = pre.astype(BF16)
    grad = adapter_scale * lax.dot_general(
        pre, up[...], (((1,), (1,)), ((), ())), precision=HIGHEST, preferred_element_type=F32
    )
    low_grad[...] = grad
    up_grad = adapter_scale * lax.dot_general(
        low_rank[...], pre, (((0,), (0,)), ((), ())), precision=HIGHEST, preferred_element_type=F32
    )
    rank = grad.shape[1]
    split = jnp.concatenate(split_two(grad), axis=-1)
    down_width, up_width = tokens.shape[1] // parts, width // parts
    for partner, out in enumerate(grads):
        part = place[0] ^ partner
        columns = pl.ds(pl.multiple_of(part * down_width, 128), down_width)
        both = lax.dot_general(split, tokens[:, columns], (((0,), (0,)), ((), ())), preferred_element_type=F32)
        out[:, :down_width] = (both[:rank] + both[rank:]).astype(out.dtype)
        for other in range(parts):

            @pl.when(part == other)
            def _():
                out[:, down_width:] = up_grad[:, other * up_width : (other + 1) * up_width].astype(out.dtype)


def input_grad_kernel(pieces, part_rows, place, pre_low, low_grad, split, *refs):
    buffers, out = refs[:-1], refs[-1]
    rank = low_grad.shape[1]
    high, low = split_two(low_grad[...])
    left = jnp.concatenate([high, high, low], axis=-1)
    for piece in pieces:
        columns = pl.ds(column_of(place, piece, part_rows), piece["rows"])
        rows = pl.ds(piece["first"], piece["rows"])
        value = lax.dot_general(
            pre_low[...], buffers[piece["buffer"]][rows, :], (((1,), (1,)), ((), ())), preferred_element_type=F32
        )
        right = jnp.concatenate([split[:, columns], split[:rank, columns]], axis=0)
        value = value + jnp.dot(left, right, preferred_element_type=F32)
        out[:, columns] = value.astype(BF16)


def sum_kernel(slots, *refs):
    grads, (down, up) = refs[:-2], refs[-2:]
    width = down.shape[2]
    for stored in range(down.shape[0]):
        total = jnp.zeros(grads[0].shape, F32)
        for partner, grad in enumerate(grads):
            total = total + jnp.where(slots[partner] == stored, grad[...].astype(F32), 0.0)
        down[stored] = total[:, :width]
        up[stored] = total[:, width:]


def flip(value, axis, size, bits):
    return lax.ppermute(value, axis, [(i, i ^ bits) for i in range(size)])


def on_device_lines(
    sizes,
    tokens,
    frozen_key_matrix,
    adapter_down_factor,
    adapter_up_factor,
    key_norm_gain,
    adapter_offset,
    loss_row_count,
    cotangent,
):
    parts, shards = sizes
    rows, model_width = tokens.shape
    key_width = frozen_key_matrix.shape[1]
    stored, down_width, rank = adapter_down_factor.shape
    up_width = adapter_up_factor.shape[2]
    shard_rows = frozen_key_matrix.shape[0]
    part_rows = shard_rows // parts
    half = part_rows // 2
    dp, fsdp = lax.axis_index("dp"), lax.axis_index("fsdp")
    over_dp = lambda value, bits: flip(value, "dp", parts, bits)
    over_z = lambda value, bits: flip(value, "fsdp", shards, bits * CORES)
    over_core = lambda value: flip(value, "fsdp", shards, 1)

    info = jnp.concatenate([adapter_offset[0], loss_row_count[0]])
    infos = [info] + [over_dp(info, bits) for bits in range(1, parts)]
    slots = jnp.stack([value[0] for value in infos])
    live = jnp.stack([value[1] for value in infos])
    adapter_total = jnp.sum(jnp.where(slots == slots[0], live, 0)).astype(F32)
    scale = (rows / adapter_total).reshape(1)
    place = jnp.stack([dp, fsdp // CORES, fsdp % CORES, info[1]]).astype(jnp.int32)

    message = ((rank, down_width + up_width), F32)
    messages = call(
        messages_kernel,
        [message] * parts,
        [(smem, slots), (vmem, jnp.swapaxes(adapter_down_factor, 1, 2)), (vmem, adapter_up_factor)],
        "adapter_messages",
    )
    adapters = [messages[0]] + [over_dp(messages[bits], bits) for bits in range(1, parts)]

    own = lax.dynamic_slice_in_dim(frozen_key_matrix, dp * part_rows, part_rows, 0)
    across = lax.dynamic_slice_in_dim(frozen_key_matrix, (dp ^ 3) * part_rows, part_rows, 0)
    z1 = over_z(own, 1)
    z2 = over_z(own, 2)
    z3 = over_z(z2, 1)
    d3 = over_z(across, 3)
    x1, y1 = over_dp(z1, 1), over_dp(z1, 2)
    x2 = over_dp(jnp.concatenate([z2, y1[half:]]), 1)
    y2 = over_dp(jnp.concatenate([z2, x1[:half]]), 2)
    x3 = over_dp(jnp.concatenate([z3, y2[half:part_rows]]), 1)
    y3 = over_dp(jnp.concatenate([z3, x2[:half]]), 2)

    def piece(z, dp_bits, count, first=0, offset=0):
        return dict(z=z, dp=dp_bits, rows=count, first=first, offset=offset, parts=parts)

    batches = [
        [(frozen_key_matrix, [piece(0, None, shard_rows)])],
        [
            (z1, [piece(1, 0, part_rows)]),
            (x1, [piece(1, 1, part_rows)]),
            (y1, [piece(1, 2, part_rows)]),
        ],
        [
            (z2, [piece(2, 0, part_rows)]),
            (x2, [piece(2, 1, part_rows), piece(1, 3, half, part_rows, half)]),
            (y2, [piece(2, 2, part_rows), piece(1, 3, half, part_rows, 0)]),
        ],
        [
            (z3, [piece(3, 0, part_rows)]),
            (d3, [piece(3, 3, part_rows)]),
            (x3, [piece(3, 1, part_rows), piece(2, 3, half, part_rows, half)]),
            (y3, [piece(3, 2, part_rows), piece(2, 3, half, part_rows, 0)]),
        ],
    ]
    batches = [
        [
            (value if core == 0 else over_core(value), [dict(item, core=core) for item in items])
            for value, items in batch
            for core in range(CORES)
        ]
        for batch in batches
    ]

    def flat(batch):
        buffers = [value for value, _ in batch]
        pieces = [dict(item, buffer=index) for index, (_, items) in enumerate(batch) for item in items]
        return buffers, pieces

    split, up, low_rank, total = call(
        low_rank_kernel,
        [((2 * rank, model_width), BF16), ((rank, key_width), F32), ((rows, rank), F32), ((rows, key_width), F32)],
        [(smem, place), (vmem, tokens)] + [(vmem, value) for value in adapters],
        "low_rank",
        flops=2 * rows * model_width * 256,
        moved=rows * model_width * 2,
    )
    for batch in batches[:-1]:
        buffers, pieces = flat(batch)
        (total,) = call(
            functools.partial(base_kernel, pieces, part_rows),
            [((rows, key_width), F32)],
            [(smem, place), (vmem, tokens), (vmem, total)] + [(vmem, value) for value in buffers],
            "base",
            flops=4 * rows * key_width * sum(item["rows"] for item in pieces),
            moved=sum(value.size for value in buffers) * 2,
        )
    buffers, pieces = flat(batches[-1])
    keys, pre_low, low_grad, *grads = call(
        functools.partial(middle_kernel, pieces, part_rows, parts),
        [((rows, key_width), BF16), ((rows, key_width), BF16), ((rows, rank), F32)] + [message] * parts,
        [
            (smem, place),
            (smem, scale),
            (vmem, tokens),
            (vmem, total),
            (vmem, cotangent),
            (vmem, key_norm_gain.reshape(1, HD)),
            (vmem, low_rank),
            (vmem, up),
        ]
        + [(vmem, value) for value in buffers],
        "key_norm",
        flops=4 * rows * key_width * model_width // 4,
        moved=sum(value.size for value in buffers) * 2,
    )
    received = [grads[0]] + [over_dp(grads[bits], bits) for bits in range(1, parts)]
    buffers, pieces = flat([entry for batch in batches for entry in batch])
    (input_grad,) = call(
        functools.partial(input_grad_kernel, pieces, part_rows),
        [((rows, model_width), BF16)],
        [(smem, place), (vmem, pre_low), (vmem, low_grad), (vmem, split)] + [(vmem, value) for value in buffers],
        "input_grad",
        flops=4 * rows * key_width * model_width,
        moved=2 * model_width * key_width,
    )
    down_sum, up_sum = call(
        sum_kernel,
        [((stored, rank, down_width), F32), ((stored, rank, up_width), F32)],
        [(smem, slots)] + [(vmem, value) for value in received],
        "grad_sum",
    )
    return keys, input_grad, jnp.swapaxes(down_sum, 1, 2), up_sum


def on_device_any(
    tokens,
    frozen_key_matrix,
    adapter_down_factor,
    adapter_up_factor,
    key_norm_gain,
    adapter_offset,
    loss_row_count,
    cotangent,
):
    row_count = tokens.shape[0]
    key_width = frozen_key_matrix.shape[1]
    stored_values = adapter_down_factor.shape[0]
    slot_value = adapter_offset[0, 0]
    live_count = loss_row_count[0, 0]
    selector = jnp.arange(stored_values, dtype=jnp.int32) == slot_value
    counted = jnp.where(selector, live_count, 0)
    summed_rows = lax.psum(counted, "dp")
    adapter_total = jnp.sum(jnp.where(selector, summed_rows, 0)).astype(F32)
    down_whole = lax.all_gather(adapter_down_factor, "dp", axis=1, tiled=True)
    up_whole = lax.all_gather(adapter_up_factor, "dp", axis=2, tiled=True)
    down_projection = lax.dynamic_index_in_dim(down_whole, slot_value, 0, keepdims=False)
    up_projection = lax.dynamic_index_in_dim(up_whole, slot_value, 0, keepdims=False)
    weight = lax.all_gather(frozen_key_matrix, "fsdp", axis=0, tiled=True)
    frozen_output = jnp.dot(tokens, weight, preferred_element_type=F32)
    tokens_float = tokens.astype(F32)
    lowrank_output = jnp.dot(tokens_float, down_projection, precision=HIGHEST)
    projected_keys = frozen_output + adapter_scale * jnp.dot(lowrank_output, up_projection, precision=HIGHEST)
    shaped = projected_keys.reshape(row_count, -1, HD)
    mean_square = jnp.mean(shaped * shaped, axis=-1, keepdims=True)
    inverse_rms = lax.rsqrt(mean_square + norm_eps)
    normed = shaped * inverse_rms
    keys = (normed * key_norm_gain).reshape(row_count, key_width).astype(BF16)
    row_mask = (jnp.arange(row_count, dtype=jnp.int32) < live_count).astype(F32)
    row_grad = cotangent.astype(F32) * row_mask[:, None] * (row_count / adapter_total)
    scaled_grad = row_grad.reshape(normed.shape) * key_norm_gain
    along_norm = jnp.mean(scaled_grad * normed, axis=-1, keepdims=True)
    prenorm_gradient = (inverse_rms * (scaled_grad - normed * along_norm)).reshape(row_count, key_width)
    pre_grad_low = prenorm_gradient.astype(BF16)
    lowrank_gradient = adapter_scale * jnp.dot(prenorm_gradient, up_projection.T, precision=HIGHEST)
    input_base = lax.dot_general(pre_grad_low, weight, (((1,), (1,)), ((), ())), preferred_element_type=F32)
    input_grad = (input_base + jnp.dot(lowrank_gradient, down_projection.T, precision=HIGHEST)).astype(BF16)
    down_grad = lax.dot_general(tokens_float, lowrank_gradient, (((0,), (0,)), ((), ())), precision=HIGHEST)
    up_factor_gradient = adapter_scale * lax.dot_general(
        lowrank_output, prenorm_gradient, (((0,), (0,)), ((), ())), precision=HIGHEST
    )
    selector_float = selector.astype(F32)
    down_terms = selector_float[:, None, None] * down_grad[None]
    up_terms = selector_float[:, None, None] * up_factor_gradient[None]
    down_sum = lax.psum_scatter(down_terms, "dp", scatter_dimension=1, tiled=True)
    up_sum = lax.psum_scatter(up_terms, "dp", scatter_dimension=2, tiled=True)
    return keys, input_grad, down_sum, up_sum


def solution(mesh):
    placed = (
        P(("dp", "fsdp"), None),
        P("fsdp", None),
        P("fsdp", "dp", None),
        P("fsdp", None, "dp"),
        P(),
        P("dp", "fsdp"),
        P("dp", "fsdp"),
        P(("dp", "fsdp"), None),
    )
    sizes = mesh.shape["dp"], mesh.shape["fsdp"]
    lines = sizes == (4, 4 * CORES)
    return jax.shard_map(
        functools.partial(on_device_lines, sizes) if lines else on_device_any,
        mesh=mesh,
        in_specs=placed,
        out_specs=(
            P(("dp", "fsdp"), None),
            P(("dp", "fsdp"), None),
            P("fsdp", "dp", None),
            P("fsdp", None, "dp"),
        ),
        check_vma=False,
    )
```

time: 200 us -> 95.9 us (0.48)
  waiting for transfers between devices: 139 us -> 25 us
  starting transfers between devices: 0.16 us -> 27.7 us
  matrix products: 21.4 us -> 0 us
  Pallas kernels: 0 us -> 20.7 us
  blocking collectives: 18 us -> 0 us
  local copies, waits for them, and re-layouts: 0.6 us -> 14.3 us
  between operations: 15.9 us -> 2.95 us
    all_gather x2 -> x0, waiting for transfers between devices: 94.5 us -> none  [the longest x1 80.9 us: on_device(): weight = lax.all_gather(frozen_key_matrix, 'fsdp', axis=0, tiled=True)]
    reduce_scatter x2 -> x0, waiting for transfers between devices: 43.1 us -> none  [the longest x1 34.6 us: on_device(): lax.psum_scatter(down_terms, 'dp', scatter_dimension=1, tiled=True)]
    ppermute x0 -> x30, starting transfers between devices: none -> 27.7 us  [flip(): return lax.ppermute(value, axis, [(i, i ^ bits) for i in range(size)])]
    ppermute x0 -> x30, waiting for transfers between devices: none -> 25 us  [flip(): return lax.ppermute(value, axis, [(i, i ^ bits) for i in range(size)])]
    dot_general x8 -> x0, matrix products: 21.4 us -> none  [the longest x1 6.19 us: on_device(): lax.dot_general(pre_grad_low, weight, (((1,), (1,)), ((), ())), preferred...]
    pallas_call x0 -> x8, Pallas kernels: none -> 20.7 us  [call(): pl.pallas_call(kernel, out_shape=[jax.ShapeDtypeStruct(shape, dtype) for...]
    unnamed x8 -> x62, local copies, waits for them, and re-layouts: 0.02 us -> 9.4 us
    all_gather x1 -> x0, blocking collectives: 9.19 us -> none  [on_device(): lax.all_gather(adapter_up_factor, 'dp', axis=2, tiled=True)]
  transfers between devices with their start and end apart: 4 -> 30, of which waited for: 4 -> 9; matrix products, arithmetic and copies ran while one was open for 9% -> 9% of each run, Pallas kernels for 0% -> 16%
where the time goes in v1:
time: 95.9 us; the launch traced here: 95.4 us
  starting transfers between devices  27.7 us (29%)
  waiting for transfers between devices  25 us (26%)
  Pallas kernels  20.7 us (22%)
  local copies, waits for them, and re-layouts  14.3 us (15%)
  other arithmetic  4.7 us (5%)
  between operations  2.95 us (3%)
    ppermute x30, starting transfers between devices, flip(): return lax.ppermute(value, axis, [(i, i ^ bits) for i in range(size)])  27.7 us
    ppermute x30, waiting for transfers between devices, flip(): return lax.ppermute(value, axis, [(i, i ^ bits) for i in range(size)])  25 us
    pallas_call x8, Pallas kernels, call(): pl.pallas_call(kernel, out_shape=[jax.ShapeDtypeStruct(shape, dtype) for...  20.7 us
    unnamed x62, local copies, waits for them, and re-layouts  9.4 us
    reduce_sum x1, other arithmetic, on_device_lines(): adapter_total = jnp.sum(jnp.where(slots == slots[0], live, 0)).astype(F32)  4.44 us
  transfers between devices with their start and end apart: 30, of which 9 were waited for; matrix products, arithmetic and copies ran while one was open for 9% of the time, Pallas kernels for 16%

profile of v1, /device:TPU:0, one launch (start us, length us, event | category | flops | bytes accessed | tf_op | source)
XLA Modules:
  0.0 95.4 jit_solution(1410287237315777329)
XLA Ops:
  0.7 1.2 %constant_dynamic-slice_fusion = (bf16[256,512]{1,0:T(8,128)(2,1)S(1)}, bf16[256,512]{1,0:T(8,128)(2,1)S(1)}) fusion(bf16[1024,512]{1,0:T(8,128)(2,1)} %refs_0_.3, s32[]{:T(128)S(6)} %select_n.25, s32[]{:T(128)S(6)} %select_n.24), kind=kLoop, calls=%fused_computation.9 | loop fusion | bytes 1048584 | tf_op jit(solution)/shard_map/dynamic_slice | solution.py:204
  1.8 3.1 %collective-permute-start.7 = (bf16[256,512]{1,0:T(8,128)(2,1)S(1)}, bf16[256,512]{1,0:T(8,128)(2,1)S(1)}, u32[]{:S(2)}, u32[]{:S(2)}) collective-permute-start(bf16[256,512]{1,0:T(8,128)(2,1)S(1)} %get-tuple-element.41), channel_id=1, source_target_pairs={{0,2},{1,3},{2,0},{3,1},{4,6},{5,7},{6,4},{7,5},{8,10},{9,11},{10,... | collective-permute-start | bytes 786440 | tf_op jit(solution)/shard_map/ppermute | solution.py:159
  4.9 2.6 %collective-permute-start.13 = (bf16[256,512]{1,0:T(8,128)(2,1)S(1)}, bf16[256,512]{1,0:T(8,128)(2,1)S(1)}, u32[]{:S(2)}, u32[]{:S(2)}) collective-permute-start(bf16[256,512]{1,0:T(8,128)(2,1)S(1)} %get-tuple-element.41), channel_id=1, source_target_pairs={{0,4},{1,5},{2,6},{3,7},{4,0},{5,1},{6,2},{7,3},{8,12},{9,13},{10,... | collective-permute-start | bytes 786440 | tf_op jit(solution)/shard_map/ppermute | solution.py:159
  8.8 0.1 pad_add_fusion.1
  8.9 1.5 %collective-permute-start = (s32[2]{0:T(128)S(1)}, s32[2]{0:T(128)S(1)}, u32[]{:S(2)}, u32[]{:S(2)}) collective-permute-start(s32[2]{0:T(128)S(1)} %pad_add_fusion.1), channel_id=1, source_target_pairs={{0,8},{8,0},{16,24},{24,16},{1,9},{9,1},{17,25},{25,17},{2,10},{10... | collective-permute-start | bytes 32 | tf_op jit(solution)/shard_map/ppermute | solution.py:159
  10.4 1.5 %collective-permute-start.1 = (s32[2]{0:T(128)S(1)}, s32[2]{0:T(128)S(1)}, u32[]{:S(2)}, u32[]{:S(2)}) collective-permute-start(s32[2]{0:T(128)S(1)} %pad_add_fusion.1), channel_id=1, source_target_pairs={{0,16},{8,24},{16,0},{24,8},{1,17},{9,25},{17,1},{25,9},{2,18},{10... | collective-permute-start | bytes 32 | tf_op jit(solution)/shard_map/ppermute | solution.py:159
  11.9 0.5 collective-permute-start.2
  12.4 0.1 collective-permute-done
  12.4 0.6 fusion.1
  13.0 3.7 %collective-permute-done.7.refs_0_.refs_2_ = bf16[256,512]{1,0:T(8,128)(2,1)S(1)} collective-permute-done((bf16[256,512]{1,0:T(8,128)(2,1)S(1)}, bf16[256,512]{1,0:T(8,128)(2,1)S(1)}, u32[]{:S(2)}, u32[]{:S(2)}) %collective-permute-start.7) | collective-permute-done | bytes 262176 | tf_op jit(solution)/shard_map/ppermute | solution.py:159
  16.7 1.7 %collective-permute-start.11 = (bf16[256,512]{1,0:T(8,128)(2,1)S(1)}, bf16[256,512]{1,0:T(8,128)(2,1)S(1)}, u32[]{:S(2)}, u32[]{:S(2)}) collective-permute-start(bf16[256,512]{1,0:T(8,128)(2,1)S(1)} %collective-permute-done.7.refs_0_.refs_2_), channel_id=1, source_target_pairs={{0,16},{8,24},{16,0},{24,8},{1,17},{9,25},{17,1},{25,9},{2,18},{10... | collective-permute-start | bytes 786440 | tf_op jit(solution)/shard_map/ppermute | solution.py:159
  18.4 1.5 %collective-permute-start.9 = (bf16[256,512]{1,0:T(8,128)(2,1)S(1)}, bf16[256,512]{1,0:T(8,128)(2,1)S(1)}, u32[]{:S(2)}, u32[]{:S(2)}) collective-permute-start(bf16[256,512]{1,0:T(8,128)(2,1)S(1)} %collective-permute-done.7.refs_0_.refs_2_), channel_id=1, source_target_pairs={{0,8},{8,0},{16,24},{24,16},{1,9},{9,1},{17,25},{25,17},{2,10},{10... | collective-permute-start | bytes 786440 | tf_op jit(solution)/shard_map/ppermute | solution.py:159
  19.9 0.6 fusion.2
  20.5 0.6 fusion.3
  21.2 4.4 %fusion = (s32[]{:T(128)}, s32[4]{0:T(128)S(1)}) fusion(s32[1]{0:T(128)} %get-tuple-element.51, s32[1]{0:T(128)} %get-tuple-element.49, s32[1]{0:T(128)} %get-tuple-element.47, s32[1]{0:T(128)} %bitcast.15, s32[]{:T(128)} %bitcast.12, s32[1]{0:T(128)} %get-tuple-element.50, s32[1]{0:T(128)} %get-tuple-element.48, s32[1]{0:T(128)} %get-tuple-element.46, ...), kind=kLoop, calls=%fused_computation.5 | loop fusion | flops 35 | bytes 56 | tf_op jit(solution)/shard_map/reduce_sum | solution.py:190
  25.6 1.0 %copy-done.21 = f32[3,2048,16]{1,2,0:T(8,128)S(1)} copy-done((f32[3,2048,16]{1,2,0:T(8,128)S(1)}, f32[3,2048,16]{1,2,0:T(8,128)}, u32[]{:S(2)}) %copy-start.21) | copy-done | bytes 393240
  26.6 0.7 copy-done.29
  27.4 0.6 adapter_messages.1
  27.9 0.6 collective-permute-start.3
  28.6 0.1 pad_maximum_fusion
  28.7 0.4 collective-permute-start.17
  29.1 1.7 %collective-permute-start.15 = (bf16[384,512]{1,0:T(8,128)(2,1)S(1)}, bf16[384,512]{1,0:T(8,128)(2,1)}, u32[]{:S(2)}, u32[]{:S(2)}) collective-permute-start(bf16[384,512]{1,0:T(8,128)(2,1)S(1)} %get-tuple-element.45), channel_id=1, source_target_pairs={{0,8},{8,0},{16,24},{24,16},{1,9},{9,1},{17,25},{25,17},{2,10},{10... | collective-permute-start | bytes 1179656 | tf_op jit(solution)/shard_map/ppermute | solution.py:159
  30.7 1.5 %collective-permute-start.4 = (f32[16,2176]{1,0:T(8,128)S(1)}, f32[16,2176]{1,0:T(8,128)S(1)}, u32[]{:S(2)}, u32[]{:S(2)}) collective-permute-start(f32[16,2176]{1,0:T(8,128)S(1)} %get-tuple-element.23), channel_id=1, source_target_pairs={{0,16},{8,24},{16,0},{24,8},{1,17},{9,25},{17,1},{25,9},{2,18},{10... | collective-permute-start | bytes 417800 | tf_op jit(solution)/shard_map/ppermute | solution.py:159
  32.3 2.4 %collective-permute-done.3.refs_1_ = f32[16,2176]{1,0:T(8,128)S(1)} collective-permute-done((f32[16,2176]{1,0:T(8,128)S(1)}, f32[16,2176]{1,0:T(8,128)S(1)}, u32[]{:S(2)}, u32[]{:S(2)}) %collective-permute-start.3) | collective-permute-done | bytes 139296 | tf_op jit(solution)/shard_map/ppermute | solution.py:159
  34.6 6.2 %collective-permute-done.4.refs_2_ = f32[16,2176]{1,0:T(8,128)S(1)} collective-permute-done((f32[16,2176]{1,0:T(8,128)S(1)}, f32[16,2176]{1,0:T(8,128)S(1)}, u32[]{:S(2)}, u32[]{:S(2)}) %collective-permute-start.4) | collective-permute-done | bytes 139296 | tf_op jit(solution)/shard_map/ppermute | solution.py:159
  40.9 0.6 copy-done.24
  41.5 1.4 %collective-permute-start.5 = (f32[16,2176]{1,0:T(8,128)S(1)}, f32[16,2176]{1,0:T(8,128)S(1)}, u32[]{:S(2)}, u32[]{:S(2)}) collective-permute-start(f32[16,2176]{1,0:T(8,128)S(1)} %get-tuple-element.24), channel_id=1, source_target_pairs={{0,24},{8,16},{16,8},{24,0},{1,25},{9,17},{17,9},{25,1},{2,26},{10... | collective-permute-start | bytes 417800 | tf_op jit(solution)/shard_map/ppermute | solution.py:159
  42.9 4.5 %collective-permute-done.5.refs_3_ = f32[16,2176]{1,0:T(8,128)S(1)} collective-permute-done((f32[16,2176]{1,0:T(8,128)S(1)}, f32[16,2176]{1,0:T(8,128)S(1)}, u32[]{:S(2)}, u32[]{:S(2)}) %collective-permute-start.5) | collective-permute-done | bytes 139296 | tf_op jit(solution)/shard_map/ppermute | solution.py:159
  47.5 0.7 copy-done.26
  48.1 2.5 %collective-permute-start.21 = (bf16[256,512]{1,0:T(8,128)(2,1)S(1)}, bf16[256,512]{1,0:T(8,128)(2,1)S(1)}, u32[]{:S(2)}, u32[]{:S(2)}) collective-permute-start(bf16[256,512]{1,0:T(8,128)(2,1)S(1)} %get-tuple-element.40), channel_id=1, source_target_pairs={{0,6},{1,7},{2,4},{3,5},{4,2},{5,3},{6,0},{7,1},{8,14},{9,15},{10,... | collective-permute-start | bytes 786440 | tf_op jit(solution)/shard_map/ppermute | solution.py:159
  50.6 0.5 collective-permute-start.14
  51.1 0.1 collective-permute-start.10
  51.2 0.9 slice.42
  52.1 0.9 slice.43
  53.1 0.1 pad_maximum_fusion.2
  53.1 3.3 %collective-permute-done.21.refs_2_.refs_16_ = bf16[256,512]{1,0:T(8,128)(2,1)S(1)} collective-permute-done((bf16[256,512]{1,0:T(8,128)(2,1)S(1)}, bf16[256,512]{1,0:T(8,128)(2,1)S(1)}, u32[]{:S(2)}, u32[]{:S(2)}) %collective-permute-start.21) | collective-permute-done | bytes 262176 | tf_op jit(solution)/shard_map/ppermute | solution.py:159
  56.4 1.5 %collective-permute-start.23 = (bf16[384,512]{1,0:T(8,128)(2,1)S(1)}, bf16[384,512]{1,0:T(8,128)(2,1)}, u32[]{:S(2)}, u32[]{:S(2)}) collective-permute-start(bf16[384,512]{1,0:T(8,128)(2,1)S(1)} %get-tuple-element.43), channel_id=1, source_target_pairs={{0,8},{8,0},{16,24},{24,16},{1,9},{9,1},{17,25},{25,17},{2,10},{10... | collective-permute-start | bytes 1179656 | tf_op jit(solution)/shard_map/ppermute | solution.py:159
  57.9 0.7 copy-done.12
  58.6 0.5 collective-permute-start.25
  59.1 0.7 copy-done.14
  59.8 0.7 copy-done.16
  60.5 0.5 collective-permute-start.16
  61.0 0.3 collective-permute-done.12.refs_5_.refs_7_
  61.4 0.7 copy-done.18
  62.1 0.1 collective-permute-start.18
  62.2 2.6 %collective-permute-done.23.refs_4_.refs_18_ = bf16[384,512]{1,0:T(8,128)(2,1)} collective-permute-done((bf16[384,512]{1,0:T(8,128)(2,1)S(1)}, bf16[384,512]{1,0:T(8,128)(2,1)}, u32[]{:S(2)}, u32[]{:S(2)}) %collective-permute-start.23) | collective-permute-done | bytes 393248 | tf_op jit(solution)/shard_map/ppermute | solution.py:159
  64.8 1.9 %collective-permute-done.25.refs_6_.refs_20_ = bf16[384,512]{1,0:T(8,128)(2,1)} collective-permute-done((bf16[384,512]{1,0:T(8,128)(2,1)S(1)}, bf16[384,512]{1,0:T(8,128)(2,1)}, u32[]{:S(2)}, u32[]{:S(2)}) %collective-permute-start.25) | collective-permute-done | bytes 393248 | tf_op jit(solution)/shard_map/ppermute | solution.py:159
  66.7 0.5 collective-permute-start.22
  67.2 0.1 collective-permute-start.20
  67.3 0.1 pad_add_fusion.place
  68.0 0.9 copy-done.23
  68.9 0.9 copy-done.25
  69.8 0.9 copy-done.27
  70.7 2.1 %low_rank.1 = (bf16[32,8192]{1,0:T(8,128)(2,1)S(1)}, f32[16,512]{1,0:T(8,128)S(1)}, f32[128,16]{1,0:T(8,128)S(1)}, f32[128,512]{1,0:T(8,128)S(1)}) custom-call(s32[4]{0:T(128)S(1)} %pad_add_fusion.place, bf16[128,8192]{1,0:T(8,128)(2,1)S(1)} %copy-done, f32[16,2176]{1,0:T(8,128)S(1)} %get-tuple-element.21.refs_0_, f32[16,2176]{1,0:T(8,128)S(1)} %copy-done.23, ...), custom_call_target="tpu_custom_call" | custom-call | flops 536870912 | bytes 2097152 | tf_op jit(solution)/shard_map/low_rank/pallas_call | solution.py:32
  72.8 0.8 copy-done.20
  73.6 1.8 %base.3.before = f32[128,512]{1,0:T(8,128)S(1)} custom-call(s32[4]{0:T(128)S(1)} %pad_add_fusion.place, bf16[128,8192]{1,0:T(8,128)(2,1)S(1)} %copy-done, f32[128,512]{1,0:T(8,128)S(1)} %get-tuple-element.25.before, bf16[1024,512]{1,0:T(8,128)(2,1)S(1)} %copy-done.1, bf16[1024,512]{1,0:T(8,128)(2,1)} %collective-permute-done.6.refs_1_), custom_call_target="tpu_custom_call" | custom-call | flops 536870912 | bytes 2097152 | tf_op jit(solution)/shard_map/base/pallas_call | solution.py:32
  75.5 0.9 base.4.before
  76.5 1.9 %base.5.before = f32[128,512]{1,0:T(8,128)S(1)} custom-call(s32[4]{0:T(128)S(1)} %pad_add_fusion.place, bf16[128,8192]{1,0:T(8,128)(2,1)S(1)} %copy-done, f32[128,512]{1,0:T(8,128)S(1)} %base.4.before, bf16[256,512]{1,0:T(8,128)(2,1)S(1)} %collective-permute-done.13.refs_0_.refs_8_, bf16[256,512]{1,0:T(8,128)(2,1)S(1)} %copy-done.15, ...), custom_call_target="tpu_custom_call" | custom-call | flops 536870912 | bytes 2097152 | tf_op jit(solution)/shard_map/base/pallas_call | solution.py:32
  78.5 4.5 %key_norm.1 = (bf16[128,512]{1,0:T(8,128)(2,1)}, bf16[128,512]{1,0:T(8,128)(2,1)S(1)}, f32[128,16]{1,0:T(8,128)S(1)}, f32[16,2176]{1,0:T(8,128)S(1)}, f32[16,217...) custom-call(s32[4]{0:T(128)S(1)} %pad_add_fusion.place, f32[1]{0:T(128)} %bitcast.6.scale, ...), custom_call_target="tpu_custom_call" | custom-call | flops 536870912 | bytes 2621440 | tf_op jit(solution)/shard_map/key_norm/pallas_call | solution.py:32
  83.0 0.5 collective-permute-start.27
  83.5 0.5 collective-permute-start.28
  84.0 2.5 %collective-permute-start.29 = (f32[16,2176]{1,0:T(8,128)S(1)}, f32[16,2176]{1,0:T(8,128)S(1)}, u32[]{:S(2)}, u32[]{:S(2)}) collective-permute-start(f32[16,2176]{1,0:T(8,128)S(1)} %get-tuple-element.35), channel_id=1, source_target_pairs={{0,24},{8,16},{16,8},{24,0},{1,25},{9,17},{17,9},{25,1},{2,26},{10... | collective-permute-start | bytes 417800 | tf_op jit(solution)/shard_map/ppermute | solution.py:159
  86.5 7.5 %input_grad.1 = bf16[128,8192]{1,0:T(8,128)(2,1)} custom-call(s32[4]{0:T(128)S(1)} %pad_add_fusion.place, bf16[128,512]{1,0:T(8,128)(2,1)S(1)} %get-tuple-element.29.pre_low, f32[128,16]{1,0:T(8,128)S(1)} %get-tuple-element.30.low_grad, bf16[32,8192]{1,0:T(8,128)(2,1)} %copy-done.20, bf16[1024,512]{1,0:T(8,128)(2,1)} %refs_0_.3, ...), custom_call_target="tpu_custom_call" | custom-call | flops 2147483648 | bytes 8388608 | tf_op jit(solution)/shard_map/input_grad/pallas_call | solution.py:32
  94.0 1.4 %grad_sum.1 = (f32[3,16,2048]{2,1,0:T(8,128)}, f32[3,16,128]{2,1,0:T(8,128)}) custom-call(s32[4]{0:T(128)S(1)} %get-tuple-element.39.slots, f32[16,2176]{1,0:T(8,128)S(1)} %get-tuple-element.32.refs_0_, f32[16,2176]{1,0:T(8,128)S(1)} %collective-permute-done.27.refs_1_, f32[16,2176]{1,0:T(8,128)S(1)} %collective-permute-done.28.refs_2_, ...), custom_call_target="tpu_custom_call" | custom-call | tf_op jit(solution)/shard_map/grad_sum/pallas_call | solution.py:32
  (79 shorter events, 0.2 us)
Async XLA Ops:
  0.6 30.1 %copy-start.1 = (bf16[1024,512]{1,0:T(8,128)(2,1)S(1)}, bf16[1024,512]{1,0:T(8,128)(2,1)}, u32[]{:S(2)}) copy-start(bf16[1024,512]{1,0:T(8,128)(2,1)} %refs_0_.3) | copy-start | bytes 3145732
  1.8 14.9 %collective-permute-start.7 = (bf16[256,512]{1,0:T(8,128)(2,1)S(1)}, bf16[256,512]{1,0:T(8,128)(2,1)S(1)}, u32[]{:S(2)}, u32[]{:S(2)}) collective-permute-start(bf16[256,512]{1,0:T(8,128)(2,1)S(1)} %get-tuple-element.41), channel_id=1, source_target_pairs={{0,2},{1,3},{2,0},{3,1},{4,6},{5,7},{6,4},{7,5},{8,10},{9,11},{10,... | collective-permute-start | bytes 786440 | tf_op jit(solution)/shard_map/ppermute | solution.py:159
  4.9 23.7 %collective-permute-start.13 = (bf16[256,512]{1,0:T(8,128)(2,1)S(1)}, bf16[256,512]{1,0:T(8,128)(2,1)S(1)}, u32[]{:S(2)}, u32[]{:S(2)}) collective-permute-start(bf16[256,512]{1,0:T(8,128)(2,1)S(1)} %get-tuple-element.41), channel_id=1, source_target_pairs={{0,4},{1,5},{2,6},{3,7},{4,0},{5,1},{6,2},{7,3},{8,12},{9,13},{10,... | collective-permute-start | bytes 786440 | tf_op jit(solution)/shard_map/ppermute | solution.py:159
  8.9 3.5 %collective-permute-start = (s32[2]{0:T(128)S(1)}, s32[2]{0:T(128)S(1)}, u32[]{:S(2)}, u32[]{:S(2)}) collective-permute-start(s32[2]{0:T(128)S(1)} %pad_add_fusion.1), channel_id=1, source_target_pairs={{0,8},{8,0},{16,24},{24,16},{1,9},{9,1},{17,25},{25,17},{2,10},{10... | collective-permute-start | bytes 32 | tf_op jit(solution)/shard_map/ppermute | solution.py:159
  10.4 9.5 %collective-permute-start.1 = (s32[2]{0:T(128)S(1)}, s32[2]{0:T(128)S(1)}, u32[]{:S(2)}, u32[]{:S(2)}) collective-permute-start(s32[2]{0:T(128)S(1)} %pad_add_fusion.1), channel_id=1, source_target_pairs={{0,16},{8,24},{16,0},{24,8},{1,17},{9,25},{17,1},{25,9},{2,18},{10... | collective-permute-start | bytes 32 | tf_op jit(solution)/shard_map/ppermute | solution.py:159
  11.9 8.7 %collective-permute-start.2 = (s32[2]{0:T(128)S(1)}, s32[2]{0:T(128)S(1)}, u32[]{:S(2)}, u32[]{:S(2)}) collective-permute-start(s32[2]{0:T(128)S(1)} %pad_add_fusion.1), channel_id=1, source_target_pairs={{0,24},{8,16},{16,8},{24,0},{1,25},{9,17},{17,9},{25,1},{2,26},{10... | collective-permute-start | bytes 32 | tf_op jit(solution)/shard_map/ppermute | solution.py:159
  13.0 54.9 %copy-start = (bf16[128,8192]{1,0:T(8,128)(2,1)S(1)}, bf16[128,8192]{1,0:T(8,128)(2,1)}, u32[]{:S(2)}) copy-start(bf16[128,8192]{1,0:T(8,128)(2,1)} %tokens.9) | copy-start | bytes 6291460
  16.7 45.5 %copy-start.8 = (bf16[256,512]{1,0:T(8,128)(2,1)}, bf16[256,512]{1,0:T(8,128)(2,1)S(1)}, u32[]{:S(2)}) copy-start(bf16[256,512]{1,0:T(8,128)(2,1)S(1)} %collective-permute-done.7.refs_0_.refs_2_) | copy-start | bytes 786436
  16.7 11.8 %collective-permute-start.11 = (bf16[256,512]{1,0:T(8,128)(2,1)S(1)}, bf16[256,512]{1,0:T(8,128)(2,1)S(1)}, u32[]{:S(2)}, u32[]{:S(2)}) collective-permute-start(bf16[256,512]{1,0:T(8,128)(2,1)S(1)} %collective-permute-done.7.refs_0_.refs_2_), channel_id=1, source_target_pairs={{0,16},{8,24},{16,0},{24,8},{1,17},{9,25},{17,1},{25,9},{2,18},{10... | collective-permute-start | bytes 786440 | tf_op jit(solution)/shard_map/ppermute | solution.py:159
  18.4 10.2 %collective-permute-start.9 = (bf16[256,512]{1,0:T(8,128)(2,1)S(1)}, bf16[256,512]{1,0:T(8,128)(2,1)S(1)}, u32[]{:S(2)}, u32[]{:S(2)}) collective-permute-start(bf16[256,512]{1,0:T(8,128)(2,1)S(1)} %collective-permute-done.7.refs_0_.refs_2_), channel_id=1, source_target_pairs={{0,8},{8,0},{16,24},{24,16},{1,9},{9,1},{17,25},{25,17},{2,10},{10... | collective-permute-start | bytes 786440 | tf_op jit(solution)/shard_map/ppermute | solution.py:159
  25.6 1.0 %copy-start.21 = (f32[3,2048,16]{1,2,0:T(8,128)S(1)}, f32[3,2048,16]{1,2,0:T(8,128)}, u32[]{:S(2)}) copy-start(f32[3,2048,16]{1,2,0:T(8,128)} %param.10) | copy-start | bytes 1179652
  26.6 0.7 copy-start.29
  27.9 6.7 %collective-permute-start.3 = (f32[16,2176]{1,0:T(8,128)S(1)}, f32[16,2176]{1,0:T(8,128)S(1)}, u32[]{:S(2)}, u32[]{:S(2)}) collective-permute-start(f32[16,2176]{1,0:T(8,128)S(1)} %get-tuple-element.22), channel_id=1, source_target_pairs={{0,8},{8,0},{16,24},{24,16},{1,9},{9,1},{17,25},{25,17},{2,10},{10... | collective-permute-start | bytes 417800 | tf_op jit(solution)/shard_map/ppermute | solution.py:159
  28.5 31.3 %copy-start.4 = (bf16[256,512]{1,0:T(8,128)(2,1)}, bf16[256,512]{1,0:T(8,128)(2,1)S(1)}, u32[]{:S(2)}) copy-start(bf16[256,512]{1,0:T(8,128)(2,1)S(1)} %collective-permute-done.11.refs_4_.refs_6_) | copy-start | bytes 786436
  28.6 32.8 %copy-start.6 = (bf16[256,512]{1,0:T(8,128)(2,1)}, bf16[256,512]{1,0:T(8,128)(2,1)S(1)}, u32[]{:S(2)}) copy-start(bf16[256,512]{1,0:T(8,128)(2,1)S(1)} %collective-permute-done.9.refs_2_.refs_4_) | copy-start | bytes 786436
  28.7 22.0 %collective-permute-start.17 = (bf16[384,512]{1,0:T(8,128)(2,1)S(1)}, bf16[384,512]{1,0:T(8,128)(2,1)}, u32[]{:S(2)}, u32[]{:S(2)}) collective-permute-start(bf16[384,512]{1,0:T(8,128)(2,1)S(1)} %get-tuple-element.44), channel_id=1, source_target_pairs={{0,16},{8,24},{16,0},{24,8},{1,17},{9,25},{17,1},{25,9},{2,18},{10... | collective-permute-start | bytes 1179656 | tf_op jit(solution)/shard_map/ppermute | solution.py:159
  29.1 22.1 %collective-permute-start.15 = (bf16[384,512]{1,0:T(8,128)(2,1)S(1)}, bf16[384,512]{1,0:T(8,128)(2,1)}, u32[]{:S(2)}, u32[]{:S(2)}) collective-permute-start(bf16[384,512]{1,0:T(8,128)(2,1)S(1)} %get-tuple-element.45), channel_id=1, source_target_pairs={{0,8},{8,0},{16,24},{24,16},{1,9},{9,1},{17,25},{25,17},{2,10},{10... | collective-permute-start | bytes 1179656 | tf_op jit(solution)/shard_map/ppermute | solution.py:159
  30.7 35.9 %collective-permute-start.6 = (bf16[1024,512]{1,0:T(8,128)(2,1)S(1)}, bf16[1024,512]{1,0:T(8,128)(2,1)}, u32[]{:S(2)}, u32[]{:S(2)}) collective-permute-start(bf16[1024,512]{1,0:T(8,128)(2,1)S(1)} %copy-done.1), channel_id=1, source_target_pairs={{0,1},{1,0},{2,3},{3,2},{4,5},{5,4},{6,7},{7,6},{8,9},{9,8},{10,11... | collective-permute-start | bytes 3145736 | tf_op jit(solution)/shard_map/ppermute | solution.py:159
  30.7 10.1 %collective-permute-start.4 = (f32[16,2176]{1,0:T(8,128)S(1)}, f32[16,2176]{1,0:T(8,128)S(1)}, u32[]{:S(2)}, u32[]{:S(2)}) collective-permute-start(f32[16,2176]{1,0:T(8,128)S(1)} %get-tuple-element.23), channel_id=1, source_target_pairs={{0,16},{8,24},{16,0},{24,8},{1,17},{9,25},{17,1},{25,9},{2,18},{10... | collective-permute-start | bytes 417800 | tf_op jit(solution)/shard_map/ppermute | solution.py:159
  34.6 30.1 %copy-start.22 = (f32[16,2176]{1,0:T(8,128)}, f32[16,2176]{1,0:T(8,128)S(1)}, u32[]{:S(2)}) copy-start(f32[16,2176]{1,0:T(8,128)S(1)} %collective-permute-done.3.refs_1_) | copy-start | bytes 417796
  34.6 16.0 %collective-permute-start.19 = (bf16[256,512]{1,0:T(8,128)(2,1)S(1)}, bf16[256,512]{1,0:T(8,128)(2,1)S(1)}, u32[]{:S(2)}, u32[]{:S(2)}) collective-permute-start(bf16[256,512]{1,0:T(8,128)(2,1)S(1)} %collective-permute-done.13.refs_0_.refs_8_), channel_id=1, source_target_pairs={{0,2},{1,3},{2,0},{3,1},{4,6},{5,7},{6,4},{7,5},{8,10},{9,11},{10,... | collective-permute-start | bytes 786440 | tf_op jit(solution)/shard_map/ppermute | solution.py:159
  40.9 0.6 copy-start.24
  41.5 6.0 %collective-permute-start.5 = (f32[16,2176]{1,0:T(8,128)S(1)}, f32[16,2176]{1,0:T(8,128)S(1)}, u32[]{:S(2)}, u32[]{:S(2)}) collective-permute-start(f32[16,2176]{1,0:T(8,128)S(1)} %get-tuple-element.24), channel_id=1, source_target_pairs={{0,24},{8,16},{16,8},{24,0},{1,25},{9,17},{17,9},{25,1},{2,26},{10... | collective-permute-start | bytes 417800 | tf_op jit(solution)/shard_map/ppermute | solution.py:159
  47.5 0.7 copy-start.26
  48.1 8.3 %collective-permute-start.21 = (bf16[256,512]{1,0:T(8,128)(2,1)S(1)}, bf16[256,512]{1,0:T(8,128)(2,1)S(1)}, u32[]{:S(2)}, u32[]{:S(2)}) collective-permute-start(bf16[256,512]{1,0:T(8,128)(2,1)S(1)} %get-tuple-element.40), channel_id=1, source_target_pairs={{0,6},{1,7},{2,4},{3,5},{4,2},{5,3},{6,0},{7,1},{8,14},{9,15},{10,... | collective-permute-start | bytes 786440 | tf_op jit(solution)/shard_map/ppermute | solution.py:159
  50.6 8.5 %copy-start.2 = (bf16[256,512]{1,0:T(8,128)(2,1)}, bf16[256,512]{1,0:T(8,128)(2,1)S(1)}, u32[]{:S(2)}) copy-start(bf16[256,512]{1,0:T(8,128)(2,1)S(1)} %collective-permute-done.19.refs_0_.refs_14_) | copy-start | bytes 786436
  50.6 7.3 %collective-permute-start.8 = (bf16[256,512]{1,0:T(8,128)(2,1)S(1)}, bf16[256,512]{1,0:T(8,128)(2,1)S(1)}, u32[]{:S(2)}, u32[]{:S(2)}) collective-permute-start(bf16[256,512]{1,0:T(8,128)(2,1)S(1)} %collective-permute-done.7.refs_0_.refs_2_), channel_id=1, source_target_pairs={{0,1},{1,0},{2,3},{3,2},{4,5},{5,4},{6,7},{7,6},{8,9},{9,8},{10,11... | collective-permute-start | bytes 786440 | tf_op jit(solution)/shard_map/ppermute | solution.py:159
  50.6 8.5 %collective-permute-start.14 = (bf16[256,512]{1,0:T(8,128)(2,1)S(1)}, bf16[256,512]{1,0:T(8,128)(2,1)S(1)}, u32[]{:S(2)}, u32[]{:S(2)}) collective-permute-start(bf16[256,512]{1,0:T(8,128)(2,1)S(1)} %collective-permute-done.13.refs_0_.refs_8_), channel_id=1, source_target_pairs={{0,1},{1,0},{2,3},{3,2},{4,5},{5,4},{6,7},{7,6},{8,9},{9,8},{10,11... | collective-permute-start | bytes 786440 | tf_op jit(solution)/shard_map/ppermute | solution.py:159
  51.1 8.7 %collective-permute-start.10 = (bf16[256,512]{1,0:T(8,128)(2,1)S(1)}, bf16[256,512]{1,0:T(8,128)(2,1)S(1)}, u32[]{:S(2)}, u32[]{:S(2)}) collective-permute-start(bf16[256,512]{1,0:T(8,128)(2,1)S(1)} %collective-permute-done.9.refs_2_.refs_4_), channel_id=1, source_target_pairs={{0,1},{1,0},{2,3},{3,2},{4,5},{5,4},{6,7},{7,6},{8,9},{9,8},{10,11... | collective-permute-start | bytes 786440 | tf_op jit(solution)/shard_map/ppermute | solution.py:159
  56.4 8.4 %copy-start.10 = (bf16[256,512]{1,0:T(8,128)(2,1)}, bf16[256,512]{1,0:T(8,128)(2,1)S(1)}, u32[]{:S(2)}) copy-start(bf16[256,512]{1,0:T(8,128)(2,1)S(1)} %collective-permute-done.21.refs_2_.refs_16_) | copy-start | bytes 786436
  56.4 8.3 %collective-permute-start.23 = (bf16[384,512]{1,0:T(8,128)(2,1)S(1)}, bf16[384,512]{1,0:T(8,128)(2,1)}, u32[]{:S(2)}, u32[]{:S(2)}) collective-permute-start(bf16[384,512]{1,0:T(8,128)(2,1)S(1)} %get-tuple-element.43), channel_id=1, source_target_pairs={{0,8},{8,0},{16,24},{24,16},{1,9},{9,1},{17,25},{25,17},{2,10},{10... | collective-permute-start | bytes 1179656 | tf_op jit(solution)/shard_map/ppermute | solution.py:159
  57.9 0.7 copy-start.12
  58.6 8.1 %collective-permute-start.25 = (bf16[384,512]{1,0:T(8,128)(2,1)S(1)}, bf16[384,512]{1,0:T(8,128)(2,1)}, u32[]{:S(2)}, u32[]{:S(2)}) collective-permute-start(bf16[384,512]{1,0:T(8,128)(2,1)S(1)} %get-tuple-element.42), channel_id=1, source_target_pairs={{0,16},{8,24},{16,0},{24,8},{1,17},{9,25},{17,1},{25,9},{2,18},{10... | collective-permute-start | bytes 1179656 | tf_op jit(solution)/shard_map/ppermute | solution.py:159
  59.1 0.7 copy-start.14
  59.8 1.5 %collective-permute-start.12 = (bf16[256,512]{1,0:T(8,128)(2,1)S(1)}, bf16[256,512]{1,0:T(8,128)(2,1)S(1)}, u32[]{:S(2)}, u32[]{:S(2)}) collective-permute-start(bf16[256,512]{1,0:T(8,128)(2,1)S(1)} %collective-permute-done.11.refs_4_.refs_6_), channel_id=1, source_target_pairs={{0,1},{1,0},{2,3},{3,2},{4,5},{5,4},{6,7},{7,6},{8,9},{9,8},{10,11... | collective-permute-start | bytes 786440 | tf_op jit(solution)/shard_map/ppermute | solution.py:159
  59.8 0.7 copy-start.16
  60.5 6.7 %collective-permute-start.16 = (bf16[384,512]{1,0:T(8,128)(2,1)}, bf16[384,512]{1,0:T(8,128)(2,1)}, u32[]{:S(2)}, u32[]{:S(2)}) collective-permute-start(bf16[384,512]{1,0:T(8,128)(2,1)} %collective-permute-done.15.refs_2_.refs_10_), channel_id=1, source_target_pairs={{0,1},{1,0},{2,3},{3,2},{4,5},{5,4},{6,7},{7,6},{8,9},{9,8},{10,11... | collective-permute-start | bytes 1179656 | tf_op jit(solution)/shard_map/ppermute | solution.py:159
  61.4 0.7 copy-start.18
  62.1 14.4 %collective-permute-start.18 = (bf16[384,512]{1,0:T(8,128)(2,1)}, bf16[384,512]{1,0:T(8,128)(2,1)}, u32[]{:S(2)}, u32[]{:S(2)}) collective-permute-start(bf16[384,512]{1,0:T(8,128)(2,1)} %collective-permute-done.17.refs_4_.refs_12_), channel_id=1, source_target_pairs={{0,1},{1,0},{2,3},{3,2},{4,5},{5,4},{6,7},{7,6},{8,9},{9,8},{10,11... | collective-permute-start | bytes 1179656 | tf_op jit(solution)/shard_map/ppermute | solution.py:159
  64.8 13.7 %collective-permute-start.24 = (bf16[384,512]{1,0:T(8,128)(2,1)}, bf16[384,512]{1,0:T(8,128)(2,1)}, u32[]{:S(2)}, u32[]{:S(2)}) collective-permute-start(bf16[384,512]{1,0:T(8,128)(2,1)} %collective-permute-done.23.refs_4_.refs_18_), channel_id=1, source_target_pairs={{0,1},{1,0},{2,3},{3,2},{4,5},{5,4},{6,7},{7,6},{8,9},{9,8},{10,11... | collective-permute-start | bytes 1179656 | tf_op jit(solution)/shard_map/ppermute | solution.py:159
  66.7 11.8 %collective-permute-start.26 = (bf16[384,512]{1,0:T(8,128)(2,1)}, bf16[384,512]{1,0:T(8,128)(2,1)}, u32[]{:S(2)}, u32[]{:S(2)}) collective-permute-start(bf16[384,512]{1,0:T(8,128)(2,1)} %collective-permute-done.25.refs_6_.refs_20_), channel_id=1, source_target_pairs={{0,1},{1,0},{2,3},{3,2},{4,5},{5,4},{6,7},{7,6},{8,9},{9,8},{10,11... | collective-permute-start | bytes 1179656 | tf_op jit(solution)/shard_map/ppermute | solution.py:159
  66.7 11.7 %collective-permute-start.22 = (bf16[256,512]{1,0:T(8,128)(2,1)}, bf16[256,512]{1,0:T(8,128)(2,1)}, u32[]{:S(2)}, u32[]{:S(2)}) collective-permute-start(bf16[256,512]{1,0:T(8,128)(2,1)} %copy-done.10), channel_id=1, source_target_pairs={{0,1},{1,0},{2,3},{3,2},{4,5},{5,4},{6,7},{7,6},{8,9},{9,8},{10,11... | collective-permute-start | bytes 786440 | tf_op jit(solution)/shard_map/ppermute | solution.py:159
  67.2 11.2 %collective-permute-start.20 = (bf16[256,512]{1,0:T(8,128)(2,1)}, bf16[256,512]{1,0:T(8,128)(2,1)}, u32[]{:S(2)}, u32[]{:S(2)}) collective-permute-start(bf16[256,512]{1,0:T(8,128)(2,1)} %copy-done.2), channel_id=1, source_target_pairs={{0,1},{1,0},{2,3},{3,2},{4,5},{5,4},{6,7},{7,6},{8,9},{9,8},{10,11... | collective-permute-start | bytes 786440 | tf_op jit(solution)/shard_map/ppermute | solution.py:159
  68.0 0.9 copy-start.23
  68.9 0.9 copy-start.25
  69.8 0.9 copy-start.27
  72.8 0.8 copy-start.20
  73.6 1.8 %copy-start.5 = (bf16[256,512]{1,0:T(8,128)(2,1)S(1)}, bf16[256,512]{1,0:T(8,128)(2,1)}, u32[]{:S(2)}) copy-start(bf16[256,512]{1,0:T(8,128)(2,1)} %copy-done.4) | copy-start | bytes 786436
  73.6 1.8 %copy-start.7 = (bf16[256,512]{1,0:T(8,128)(2,1)S(1)}, bf16[256,512]{1,0:T(8,128)(2,1)}, u32[]{:S(2)}) copy-start(bf16[256,512]{1,0:T(8,128)(2,1)} %copy-done.6) | copy-start | bytes 786436
  73.6 1.8 %copy-start.9 = (bf16[256,512]{1,0:T(8,128)(2,1)S(1)}, bf16[256,512]{1,0:T(8,128)(2,1)}, u32[]{:S(2)}) copy-start(bf16[256,512]{1,0:T(8,128)(2,1)} %copy-done.8) | copy-start | bytes 786436
  73.6 1.9 %copy-start.13 = (bf16[256,512]{1,0:T(8,128)(2,1)S(1)}, bf16[256,512]{1,0:T(8,128)(2,1)}, u32[]{:S(2)}) copy-start(bf16[256,512]{1,0:T(8,128)(2,1)} %copy-done.12) | copy-start | bytes 786436
  73.6 1.9 %copy-start.17 = (bf16[256,512]{1,0:T(8,128)(2,1)S(1)}, bf16[256,512]{1,0:T(8,128)(2,1)}, u32[]{:S(2)}) copy-start(bf16[256,512]{1,0:T(8,128)(2,1)} %copy-done.16) | copy-start | bytes 786436
  73.6 1.9 %copy-start.19 = (bf16[256,512]{1,0:T(8,128)(2,1)S(1)}, bf16[256,512]{1,0:T(8,128)(2,1)}, u32[]{:S(2)}) copy-start(bf16[256,512]{1,0:T(8,128)(2,1)} %copy-done.18) | copy-start | bytes 786436
  75.4 1.0 %copy-start.15 = (bf16[256,512]{1,0:T(8,128)(2,1)S(1)}, bf16[256,512]{1,0:T(8,128)(2,1)}, u32[]{:S(2)}) copy-start(bf16[256,512]{1,0:T(8,128)(2,1)} %copy-done.14) | copy-start | bytes 786436
  76.4 2.1 %copy-start.3 = (bf16[256,512]{1,0:T(8,128)(2,1)S(1)}, bf16[256,512]{1,0:T(8,128)(2,1)}, u32[]{:S(2)}) copy-start(bf16[256,512]{1,0:T(8,128)(2,1)} %copy-done.2) | copy-start | bytes 786436
  76.4 2.1 %copy-start.11 = (bf16[256,512]{1,0:T(8,128)(2,1)S(1)}, bf16[256,512]{1,0:T(8,128)(2,1)}, u32[]{:S(2)}) copy-start(bf16[256,512]{1,0:T(8,128)(2,1)} %copy-done.10) | copy-start | bytes 786436
  76.4 2.1 %copy-start.28 = (bf16[128,512]{1,0:T(8,128)(2,1)S(1)}, bf16[128,512]{1,0:T(8,128)(2,1)}, u32[]{:S(2)}) copy-start(bf16[128,512]{1,0:T(8,128)(2,1)} %cotangent.1) | copy-start | bytes 393220
  76.4 2.1 %copy-start.30 = (f32[128]{0:T(128)S(1)}, f32[128]{0:T(128)}, u32[]{:S(2)}) copy-start(f32[128]{0:T(128)} %param.12) | copy-start | bytes 1540
  83.0 11.0 %collective-permute-start.27 = (f32[16,2176]{1,0:T(8,128)S(1)}, f32[16,2176]{1,0:T(8,128)S(1)}, u32[]{:S(2)}, u32[]{:S(2)}) collective-permute-start(f32[16,2176]{1,0:T(8,128)S(1)} %get-tuple-element.33), channel_id=1, source_target_pairs={{0,8},{8,0},{16,24},{24,16},{1,9},{9,1},{17,25},{25,17},{2,10},{10... | collective-permute-start | bytes 417800 | tf_op jit(solution)/shard_map/ppermute | solution.py:159
  83.5 10.5 %collective-permute-start.28 = (f32[16,2176]{1,0:T(8,128)S(1)}, f32[16,2176]{1,0:T(8,128)S(1)}, u32[]{:S(2)}, u32[]{:S(2)}) collective-permute-start(f32[16,2176]{1,0:T(8,128)S(1)} %get-tuple-element.34), channel_id=1, source_target_pairs={{0,16},{8,24},{16,0},{24,8},{1,17},{9,25},{17,1},{25,9},{2,18},{10... | collective-permute-start | bytes 417800 | tf_op jit(solution)/shard_map/ppermute | solution.py:159
  84.0 10.0 %collective-permute-start.29 = (f32[16,2176]{1,0:T(8,128)S(1)}, f32[16,2176]{1,0:T(8,128)S(1)}, u32[]{:S(2)}, u32[]{:S(2)}) collective-permute-start(f32[16,2176]{1,0:T(8,128)S(1)} %get-tuple-element.35), channel_id=1, source_target_pairs={{0,24},{8,16},{16,8},{24,0},{1,25},{9,17},{17,9},{25,1},{2,26},{10... | collective-permute-start | bytes 417800 | tf_op jit(solution)/shard_map/ppermute | solution.py:159

commit v2 on v1

v2 whole, which is shorter than its diff:
```python
import functools

import jax
import jax.numpy as jnp
from jax import lax
from jax.experimental import pallas as pl
from jax.experimental.pallas import tpu as pltpu
from jax.sharding import PartitionSpec as P

HD = 128
CORES = 2

adapter_scale = 2.0
norm_eps = 1e-06

F32 = jnp.float32
BF16 = jnp.bfloat16
HIGHEST = lax.Precision.HIGHEST
VMEM_LIMIT = 8 * 2**20

vmem = pl.BlockSpec(memory_space=pltpu.VMEM)
smem = pl.BlockSpec(memory_space=pltpu.SMEM)
hbm = pl.BlockSpec(memory_space=pltpu.HBM)


def split_two(value):
    high = value.astype(BF16)
    low = (value - high.astype(F32)).astype(BF16)
    return high, low


def call(kernel, outs, ins, name, scratch=(), limit=VMEM_LIMIT):
    return pl.pallas_call(
        kernel,
        out_shape=[jax.ShapeDtypeStruct(shape, dtype) for shape, dtype in outs],
        in_specs=[spec for spec, _ in ins],
        out_specs=[vmem] * len(outs),
        scratch_shapes=scratch,
        compiler_params=pltpu.CompilerParams(vmem_limit_bytes=limit),
        cost_estimate=pl.CostEstimate(flops=0, bytes_accessed=0, transcendentals=0),
        name=name,
    )(*[value for _, value in ins])


def position():
    fsdp = lax.axis_index("fsdp")
    return lax.axis_index("dp"), lax.div(fsdp, CORES), lax.rem(fsdp, CORES)


def start_kernel(matrix, near, far):
    rows = near.shape[0]
    parts = matrix.shape[0] // rows
    for out, bits in ((near, 0), (far, parts - 1)):
        part = lax.axis_index("dp") ^ bits
        out[...] = matrix[pl.ds(pl.multiple_of(part * rows, rows), rows), :]


def info_kernel(offset, info):
    info[...] = jnp.broadcast_to(offset[...].astype(F32), info.shape)


def hold_kernel(count, down, up, count_held, down_held, up_held):
    count_held[...] = jnp.broadcast_to(count[...].astype(F32), count_held.shape)
    down_held[...] = down[...]
    up_held[...] = up[...]


def chosen(stored, slot):
    return sum(jnp.where(slot == index, stored[index], 0.0) for index in range(stored.shape[0]))


def messages_kernel(*refs):
    parts = len(refs) - 7
    offsets, (count, down, up), (slots, own, sooner, later) = refs[:parts], refs[parts : parts + 3], refs[parts + 3 :]
    rank, width = down.shape[1], down.shape[2]
    wide = width + up.shape[2]
    first_core = position()[2] == 0
    for partner, offset in enumerate(offsets):
        slots[partner : partner + 1, :] = offset[...]
    near, side, beside, far = (offset[:, :1] for offset in offsets)
    wanted = jnp.where(first_core, side, beside), jnp.where(first_core, beside, side)
    for slot, out, first in ((near, own, 0), (wanted[0], sooner, 0), (wanted[1], later, 0), (far, sooner, rank)):
        rows = pl.ds(first, rank)
        out[rows, :width] = chosen(down, slot)
        out[rows, width:wide] = chosen(up, slot)
        out[rows, wide:] = jnp.broadcast_to(count[...], (rank, HD))


def pass_on_kernel(later, received, out):
    rank = later.shape[0]
    out[:rank] = later[...]
    out[rank:] = received[rank:]


def take_kernel(each, wanted, value, out):
    for index, place in enumerate(wanted):
        out[index * each : (index + 1) * each] = value[place * each : (place + 1) * each]


def join_kernel(each, *refs):
    out = refs[-1]
    for index, ref in enumerate(refs[:-1]):
        out[index * each : (index + 1) * each] = ref[:each]


def low_rank_kernel(tokens, slots, own, sooner, later, split, up, low_rank, total, told):
    rank = low_rank.shape[1]
    messages = own, sooner.at[:rank], later.at[:rank], later.at[rank:]
    parts = len(messages)
    down_width = tokens.shape[1] // parts
    up_width = up.shape[1] // parts
    dp, _, core = position()
    lane = lax.broadcasted_iota(jnp.int32, (1, HD), 1)
    counts = [message[:1, down_width + up_width :] for message in messages]
    counts[1:3] = jnp.where(core == 0, counts[1], counts[2]), jnp.where(core == 0, counts[2], counts[1])
    for partner, count in enumerate(counts):
        told[partner : partner + 1, :] = jnp.where(lane == 0, slots[partner : partner + 1, :], count)
    partners = 0, jnp.where(core == 0, 1, 2), jnp.where(core == 0, 2, 1), 3
    for partner, message in zip(partners, messages):
        part = dp ^ partner
        columns = pl.ds(pl.multiple_of(part * down_width, 128), down_width)
        high, low = split_two(message[:, :down_width])
        split[:rank, columns] = high
        split[rank:, columns] = low
        columns = pl.ds(pl.multiple_of(part * up_width, 128), up_width)
        up[:, columns] = message[:, down_width : down_width + up_width]
    both = lax.dot_general(tokens[...], split[...], (((1,), (1,)), ((), ())), preferred_element_type=F32)
    low_rank[...] = both[:, :rank] + both[:, rank:]
    total[...] = adapter_scale * jnp.dot(low_rank[...], up[...], precision=HIGHEST, preferred_element_type=F32)


def by_core(place, value):
    first, second = value
    return first if first == second else jnp.where(place[2] == 0, first, second)


def column_of(place, piece, part_rows, parts):
    shard = (place[1] ^ by_core(place, piece["z"])) * CORES + (place[2] ^ piece["core"])
    part = 0 if piece["dp"] is None else place[0] ^ by_core(place, piece["dp"])
    return pl.multiple_of((shard * parts + part) * part_rows, 128)


def base_sum(place, tokens, total, buffers, pieces, sizes):
    for piece in pieces:
        columns = pl.ds(column_of(place, piece, *sizes), piece["rows"])
        rows = pl.ds(piece["first"], piece["rows"])
        value = jnp.dot(tokens[:, columns], buffers[piece["buffer"]][rows, :], preferred_element_type=F32)
        total = value if total is None else total + value
    return total


def base_kernel(pieces, sizes, tokens, before, *refs):
    refs[-1][...] = base_sum(position(), tokens, before[...], refs[:-1], pieces, sizes)


def middle_kernel(pieces, sizes, told, *refs):
    parts = sizes[1]
    place = position()
    (tokens, before, cotangent, gain, low_rank, up), refs = refs[:6], refs[6:]
    count = len(refs) - 3 - parts
    buffers, (keys, pre_low, low_grad), grads = refs[:count], refs[count : count + 3], refs[count + 3 :]
    projected = base_sum(place, tokens, before[...], buffers, pieces, sizes)
    rows, width = projected.shape
    gains = gain[...]
    slots, counts = told[:, :1], told[:, 1:2]
    adapter_total = jnp.sum(jnp.where(slots == slots[:1], counts, 0.0), axis=0, keepdims=True)
    live = lax.broadcasted_iota(jnp.int32, (rows, 1), 0).astype(F32) < counts[:1]
    weight = rows / jnp.broadcast_to(adapter_total, (rows, 1))
    weight = jnp.where(live, weight, 0.0)
    heads = []
    for head in range(width // HD):
        columns = slice(head * HD, (head + 1) * HD)
        values = projected[:, columns]
        inverse = lax.rsqrt(jnp.mean(values * values, axis=-1, keepdims=True) + norm_eps)
        normed = values * inverse
        keys[:, columns] = (normed * gains).astype(BF16)
        scaled = cotangent[:, columns].astype(F32) * weight * gains
        along = jnp.mean(scaled * normed, axis=-1, keepdims=True)
        heads.append(inverse * (scaled - normed * along))
    pre = jnp.concatenate(heads, axis=-1)
    pre_low[...] = pre.astype(BF16)
    grad = adapter_scale * lax.dot_general(
        pre, up[...], (((1,), (1,)), ((), ())), precision=HIGHEST, preferred_element_type=F32
    )
    low_grad[...] = grad
    up_grad = adapter_scale * lax.dot_general(
        low_rank[...], pre, (((0,), (0,)), ((), ())), precision=HIGHEST, preferred_element_type=F32
    )
    rank = grad.shape[1]
    split = jnp.concatenate(split_two(grad), axis=-1)
    down_width, up_width = tokens.shape[1] // parts, width // parts
    for partner, out in enumerate(grads):
        part = place[0] ^ partner
        columns = pl.ds(pl.multiple_of(part * down_width, 128), down_width)
        both = lax.dot_general(split, tokens[:, columns], (((0,), (0,)), ((), ())), preferred_element_type=F32)
        out[:, :down_width] = (both[:rank] + both[rank:]).astype(out.dtype)
        for other in range(parts):

            @pl.when(part == other)
            def _():
                out[:, down_width:] = up_grad[:, other * up_width : (other + 1) * up_width].astype(out.dtype)


def input_grad_kernel(pieces, sizes, pre_low, low_grad, split, *refs):
    place = position()
    buffers, out = refs[:-1], refs[-1]
    rank = low_grad.shape[1]
    high, low = split_two(low_grad[...])
    left = jnp.concatenate([high, high, low], axis=-1)
    for piece in pieces:
        columns = pl.ds(column_of(place, piece, *sizes), piece["rows"])
        rows = pl.ds(piece["first"], piece["rows"])
        value = lax.dot_general(
            pre_low[...], buffers[piece["buffer"]][rows, :], (((1,), (1,)), ((), ())), preferred_element_type=F32
        )
        right = jnp.concatenate([split[:, columns], split[:rank, columns]], axis=0)
        value = value + jnp.dot(left, right, preferred_element_type=F32)
        out[:, columns] = value.astype(BF16)


def sum_kernel(told, *refs):
    grads, (down, up) = refs[:-2], refs[-2:]
    width = down.shape[2]
    for stored in range(down.shape[0]):
        total = jnp.zeros(grads[0].shape, F32)
        for partner, grad in enumerate(grads):
            slot = told[partner : partner + 1, :1]
            total = total + jnp.where(slot == stored, grad[...].astype(F32), 0.0)
        down[stored] = total[:, :width]
        up[stored] = total[:, width:]


def ordered(value, *earlier):
    return lax.optimization_barrier((value, *earlier))[0]


def flip(value, axis, size, bits):
    return lax.ppermute(value, axis, [(i, i ^ bits) for i in range(size)])


def on_device_lines(
    sizes,
    tokens,
    frozen_key_matrix,
    adapter_down_factor,
    adapter_up_factor,
    key_norm_gain,
    adapter_offset,
    loss_row_count,
    cotangent,
):
    parts, shards = sizes
    rows, model_width = tokens.shape
    key_width = frozen_key_matrix.shape[1]
    stored, down_width, rank = adapter_down_factor.shape
    up_width = adapter_up_factor.shape[2]
    shard_rows = frozen_key_matrix.shape[0]
    part_rows = shard_rows // parts
    over_dp = lambda value, bits: flip(value, "dp", parts, bits)
    over_z = lambda value, bits: flip(value, "fsdp", shards, bits * CORES)
    over_core = lambda value: flip(value, "fsdp", shards, 1)

    def over_split(value, dp_bits, z_bits):
        pairs = []
        for i in range(parts):
            for j in range(shards):
                core = j % CORES
                pairs.append((i * shards + j, (i ^ dp_bits[core]) * shards + (j ^ (z_bits[core] * CORES))))
        return lax.ppermute(value, ("dp", "fsdp"), pairs)

    near_both = (CORES * part_rows, key_width)

    def joined(*values):
        rows = len(values) * part_rows
        outs = [((rows, key_width), BF16)]
        return call(functools.partial(join_kernel, part_rows), outs, [(vmem, value) for value in values], "join")[0]

    matrix = frozen_key_matrix
    part = ((part_rows, key_width), BF16)
    near, far = call(start_kernel, [part, part], [(vmem, matrix)], "start")
    z1, z2 = over_z(near, 1), over_z(near, 2)
    (info,) = call(info_kernel, [((1, HD), F32)], [(vmem, adapter_offset)], "info")
    offsets = [info] + [over_dp(info, bits) for bits in range(1, parts)]
    held = call(
        hold_kernel,
        [((1, HD), F32), ((stored, rank, down_width), F32), (adapter_up_factor.shape, F32)],
        [(vmem, loss_row_count), (vmem, jnp.swapaxes(adapter_down_factor, 1, 2)), (vmem, adapter_up_factor)],
        "hold",
    )
    offsets, held = lax.optimization_barrier((offsets, held))
    wide = down_width + up_width + HD
    slots, own, sooner, later = call(
        messages_kernel,
        [((parts, HD), F32), ((rank, wide), F32), ((2 * rank, wide), F32), ((rank, wide), F32)],
        [(vmem, value) for value in (*offsets, *held)],
        "adapter_messages",
    )
    z1, z2 = ordered((z1, z2), sooner)
    sooner = over_split(sooner, (1, 2), (0, 0))
    z3 = over_z(z2, 1)
    z1_pair, z2_pair, sooner = lax.optimization_barrier((over_core(z1), over_core(z2), sooner))
    m12 = joined(z1, z1_pair, z2, z2_pair)
    xy12 = over_split(m12, (1, 2), (0, 0))
    d1 = over_z(ordered(far, m12), 1)
    (onward,) = call(pass_on_kernel, [((2 * rank, wide), F32)], [(vmem, later), (vmem, sooner)], "pass_on")
    later = over_split(onward, (2, 1), (0, 0))
    d3 = over_z(ordered(far, d1), 3)
    z3, matrix_pair = lax.optimization_barrier((z3, over_core(ordered(matrix, m12))))
    m3 = joined(z3, over_core(z3))
    xy3 = over_split(m3, (1, 2), (0, 0))
    xy12 = ordered(xy12, m3)
    (m4,) = call(functools.partial(take_kernel, part_rows, (2,)), [part], [(vmem, xy12)], "take")
    xy4 = over_split(m4, (2, 1), (0, 0))
    def piece(z, dp_bits, core, count=part_rows, first=0):
        pair = lambda value: value if isinstance(value, tuple) else (value, value)
        dp_bits = None if dp_bits is None else pair(dp_bits)
        return dict(z=pair(z), dp=dp_bits, core=core, rows=count, first=first)

    def two(z, dp_bits, core=0, first=0):
        return [piece(z, dp_bits, core, first=first), piece(z, dp_bits, 1 - core, first=first + part_rows)]

    def flat(batch):
        buffers = [value for value, _ in batch]
        pieces = [dict(item, buffer=index) for index, (_, items) in enumerate(batch) for item in items]
        return buffers, pieces

    def base(before, batch):
        buffers, pieces = flat(batch)
        (total,) = call(
            functools.partial(base_kernel, pieces, (part_rows, parts)),
            [((rows, key_width), F32)],
            [(vmem, tokens), (vmem, before)] + [(vmem, value) for value in buffers],
            "base",
        )
        return total

    split, up, low_rank, total, told = call(
        low_rank_kernel,
        [
            ((2 * rank, model_width), BF16),
            ((rank, key_width), F32),
            ((rows, rank), F32),
            ((rows, key_width), F32),
            ((parts, HD), F32),
        ],
        [(vmem, value) for value in (tokens, slots, own, sooner, later)],
        "low_rank",
    )
    batch0 = [
        (matrix, [piece(0, None, 0, shard_rows)]),
        (matrix_pair, [piece(0, None, 1, shard_rows)]),
        (m12, two(1, 0) + two(2, 0, 0, CORES * part_rows)),
        (xy12, two(1, (1, 2)) + two(2, (1, 2), 0, CORES * part_rows)),
        (m3, two(3, 0)),
    ]
    total = base(total, batch0)
    xy12, xy3, xy4, d1, d3, total = lax.optimization_barrier((xy12, xy3, xy4, d1, d3, total))
    batch1 = [
        (d1, [piece(1, 3, 0)]),
        (d3, [piece(3, 3, 0)]),
        (xy3, two(3, (1, 2))),
        (xy4, [piece(2, 3, 0)]),
    ]
    total = base(total, batch1)
    batch2 = [
        (over_core(xy12), two(1, (2, 1), 1) + two(2, (2, 1), 1, CORES * part_rows)),
        (over_core(d1), [piece(1, 3, 1)]),
        (over_core(d3), [piece(3, 3, 1)]),
        (over_core(xy3), two(3, (2, 1), 1)),
        (over_core(xy4), [piece(2, 3, 1)]),
    ]
    buffers, pieces = flat(batch2)
    keys, pre_low, low_grad, *grads = call(
        functools.partial(middle_kernel, pieces, (part_rows, parts)),
        [((rows, key_width), BF16), ((rows, key_width), BF16), ((rows, rank), F32)] + [((rank, down_width + up_width), F32)] * parts,
        [(vmem, value) for value in (told, tokens, total, cotangent, key_norm_gain.reshape(1, HD), low_rank, up)]
        + [(vmem, value) for value in buffers],
        "key_norm",
    )
    received = [grads[0]] + [over_dp(grads[bits], bits) for bits in range(1, parts)]
    buffers, pieces = flat(batch0 + batch1 + batch2)
    (input_grad,) = call(
        functools.partial(input_grad_kernel, pieces, (part_rows, parts)),
        [((rows, model_width), BF16)],
        [(vmem, pre_low), (vmem, low_grad), (vmem, split)] + [(vmem, value) for value in buffers],
        "input_grad",
    )
    down_sum, up_sum = call(
        sum_kernel,
        [((stored, rank, down_width), F32), ((stored, rank, up_width), F32)],
        [(vmem, told)] + [(vmem, value) for value in received],
        "grad_sum",
    )
    return keys, input_grad, jnp.swapaxes(down_sum, 1, 2), up_sum


def on_device_any(
    tokens,
    frozen_key_matrix,
    adapter_down_factor,
    adapter_up_factor,
    key_norm_gain,
    adapter_offset,
    loss_row_count,
    cotangent,
):
    row_count = tokens.shape[0]
    key_width = frozen_key_matrix.shape[1]
    stored_values = adapter_down_factor.shape[0]
    slot_value = adapter_offset[0, 0]
    live_count = loss_row_count[0, 0]
    selector = jnp.arange(stored_values, dtype=jnp.int32) == slot_value
    counted = jnp.where(selector, live_count, 0)
    summed_rows = lax.psum(counted, "dp")
    adapter_total = jnp.sum(jnp.where(selector, summed_rows, 0)).astype(F32)
    down_whole = lax.all_gather(adapter_down_factor, "dp", axis=1, tiled=True)
    up_whole = lax.all_gather(adapter_up_factor, "dp", axis=2, tiled=True)
    down_projection = lax.dynamic_index_in_dim(down_whole, slot_value, 0, keepdims=False)
    up_projection = lax.dynamic_index_in_dim(up_whole, slot_value, 0, keepdims=False)
    weight = lax.all_gather(frozen_key_matrix, "fsdp", axis=0, tiled=True)
    frozen_output = jnp.dot(tokens, weight, preferred_element_type=F32)
    tokens_float = tokens.astype(F32)
    lowrank_output = jnp.dot(tokens_float, down_projection, precision=HIGHEST)
    projected_keys = frozen_output + adapter_scale * jnp.dot(lowrank_output, up_projection, precision=HIGHEST)
    shaped = projected_keys.reshape(row_count, -1, HD)
    mean_square = jnp.mean(shaped * shaped, axis=-1, keepdims=True)
    inverse_rms = lax.rsqrt(mean_square + norm_eps)
    normed = shaped * inverse_rms
    keys = (normed * key_norm_gain).reshape(row_count, key_width).astype(BF16)
    row_mask = (jnp.arange(row_count, dtype=jnp.int32) < live_count).astype(F32)
    row_grad = cotangent.astype(F32) * row_mask[:, None] * (row_count / adapter_total)
    scaled_grad = row_grad.reshape(normed.shape) * key_norm_gain
    along_norm = jnp.mean(scaled_grad * normed, axis=-1, keepdims=True)
    prenorm_gradient = (inverse_rms * (scaled_grad - normed * along_norm)).reshape(row_count, key_width)
    pre_grad_low = prenorm_gradient.astype(BF16)
    lowrank_gradient = adapter_scale * jnp.dot(prenorm_gradient, up_projection.T, precision=HIGHEST)
    input_base = lax.dot_general(pre_grad_low, weight, (((1,), (1,)), ((), ())), preferred_element_type=F32)
    input_grad = (input_base + jnp.dot(lowrank_gradient, down_projection.T, precision=HIGHEST)).astype(BF16)
    down_grad = lax.dot_general(tokens_float, lowrank_gradient, (((0,), (0,)), ((), ())), precision=HIGHEST)
    up_factor_gradient = adapter_scale * lax.dot_general(
        lowrank_output, prenorm_gradient, (((0,), (0,)), ((), ())), precision=HIGHEST
    )
    selector_float = selector.astype(F32)
    down_terms = selector_float[:, None, None] * down_grad[None]
    up_terms = selector_float[:, None, None] * up_factor_gradient[None]
    down_sum = lax.psum_scatter(down_terms, "dp", scatter_dimension=1, tiled=True)
    up_sum = lax.psum_scatter(up_terms, "dp", scatter_dimension=2, tiled=True)
    return keys, input_grad, down_sum, up_sum


def solution(mesh):
    placed = (
        P(("dp", "fsdp"), None),
        P("fsdp", None),
        P("fsdp", "dp", None),
        P("fsdp", None, "dp"),
        P(),
        P("dp", "fsdp"),
        P("dp", "fsdp"),
        P(("dp", "fsdp"), None),
    )
    sizes = mesh.shape["dp"], mesh.shape["fsdp"]
    lines = sizes == (4, 4 * CORES)
    return jax.shard_map(
        functools.partial(on_device_lines, sizes) if lines else on_device_any,
        mesh=mesh,
        in_specs=placed,
        out_specs=(
            P(("dp", "fsdp"), None),
            P(("dp", "fsdp"), None),
            P("fsdp", "dp", None),
            P("fsdp", None, "dp"),
        ),
        check_vma=False,
    )
```

time: 95.9 us -> 69.8 us (0.73)
  the two profiles are of different devices: /device:TPU:0 before, /device:TPU:8 now
where the time goes in v2:
time: 69.8 us; the launch traced here: 69.6 us
  waiting for transfers between devices  32.4 us (46%)
  starting transfers between devices  20.3 us (29%)
  Pallas kernels  11.7 us (17%)
  local copies, waits for them, and re-layouts  2.97 us (4%)
  between operations  2.1 us (3%)
    ppermute x20, waiting for transfers between devices, flip(): return lax.ppermute(value, axis, [(i, i ^ bits) for i in range(size)])  27.5 us
    ppermute x20, starting transfers between devices, flip(): return lax.ppermute(value, axis, [(i, i ^ bits) for i in range(size)])  15.8 us
    pallas_call x14, Pallas kernels, call(): pl.pallas_call(kernel, out_shape=[jax.ShapeDtypeStruct(shape, dtype) for...  11.7 us
    ppermute x5, waiting for transfers between devices, over_split(): return lax.ppermute(value, ('dp', 'fsdp'), pairs)  4.93 us
    ppermute x5, starting transfers between devices, over_split(): return lax.ppermute(value, ('dp', 'fsdp'), pairs)  4.56 us
    unnamed x14, local copies, waits for them, and re-layouts  2.97 us
  transfers between devices with their start and end apart: 25, of which 11 were waited for; matrix products, arithmetic and copies ran while one was open for 0% of the time, Pallas kernels for 11%

profile of v2, /device:TPU:8, one launch (start us, length us, event | category | flops | bytes accessed | tf_op | source)
XLA Modules:
  0.0 69.6 jit_solution(1103451664147590827)
XLA Ops:
  0.6 1.2 %copy-done.1 = bf16[1024,512]{1,0:T(8,128)(2,1)S(1)} copy-done((bf16[1024,512]{1,0:T(8,128)(2,1)S(1)}, bf16[1024,512]{1,0:T(8,128)(2,1)}, u32[]{:S(2)}) %copy-start.1) | copy-done | bytes 1048600
  1.9 0.1 collective-permute-start.3
  2.0 3.0 %collective-permute-start.4 = (bf16[256,512]{1,0:T(8,128)(2,1)S(1)}, bf16[256,512]{1,0:T(8,128)(2,1)S(1)}, u32[]{:S(2)}, u32[]{:S(2)}) collective-permute-start(bf16[256,512]{1,0:T(8,128)(2,1)S(1)} %get-tuple-element.63), channel_id=1, source_target_pairs={{0,4},{1,5},{2,6},{3,7},{4,0},{5,1},{6,2},{7,3},{8,12},{9,13},{10,... | collective-permute-start | bytes 786440 | tf_op jit(solution)/shard_map/ppermute | solution.py:238
  5.7 0.1 info.1.refs_0_
  5.7 1.5 %collective-permute-start = (f32[1,128]{1,0:T(1,128)S(1)}, f32[1,128]{1,0:T(1,128)S(1)}, u32[]{:S(2)}, u32[]{:S(2)}) collective-permute-start(f32[1,128]{1,0:T(1,128)S(1)} %info.1.refs_0_), channel_id=1, source_target_pairs={{0,8},{8,0},{16,24},{24,16},{1,9},{9,1},{17,25},{25,17},{2,10},{10... | collective-permute-start | bytes 1544 | tf_op jit(solution)/shard_map/ppermute | solution.py:238
  7.2 1.5 %collective-permute-start.1 = (f32[1,128]{1,0:T(1,128)S(1)}, f32[1,128]{1,0:T(1,128)S(1)}, u32[]{:S(2)}, u32[]{:S(2)}) collective-permute-start(f32[1,128]{1,0:T(1,128)S(1)} %info.1.refs_0_), channel_id=1, source_target_pairs={{0,16},{8,24},{16,0},{24,8},{1,17},{9,25},{17,1},{25,9},{2,18},{10... | collective-permute-start | bytes 1544 | tf_op jit(solution)/shard_map/ppermute | solution.py:238
  8.7 0.5 collective-permute-start.2
  9.9 0.0 copy-start.3
  9.9 1.0 %copy-done.3 = f32[3,2048,16]{1,2,0:T(8,128)S(1)} copy-done((f32[3,2048,16]{1,2,0:T(8,128)S(1)}, f32[3,2048,16]{1,2,0:T(8,128)}, u32[]{:S(2)}) %copy-start.3) | copy-done | bytes 393240
  10.9 0.7 %copy-done.5 = f32[3,16,128]{2,1,0:T(8,128)S(1)} copy-done((f32[3,16,128]{2,1,0:T(8,128)S(1)}, f32[3,16,128]{2,1,0:T(8,128)}, u32[]{:S(2)}) %copy-start.5) | copy-done | bytes 24600
  11.6 0.1 hold.1
  11.7 0.0 collective-permute-done.refs_1_
  11.7 0.0 collective-permute-done.1.refs_2_
  11.7 1.5 %collective-permute-done.2.refs_3_ = f32[1,128]{1,0:T(1,128)S(1)} collective-permute-done((f32[1,128]{1,0:T(1,128)S(1)}, f32[1,128]{1,0:T(1,128)S(1)}, u32[]{:S(2)}, u32[]{:S(2)}) %collective-permute-start.2) | collective-permute-done | bytes 544 | tf_op jit(solution)/shard_map/ppermute | solution.py:238
  13.2 0.2 adapter_messages.1
  13.4 0.0 copy-start
  13.4 0.6 collective-permute-start.7
  14.0 0.0 collective-permute-done.3.refs_0_
  14.0 2.7 %collective-permute-done.4.refs_2_ = bf16[256,512]{1,0:T(8,128)(2,1)S(1)} collective-permute-done((bf16[256,512]{1,0:T(8,128)(2,1)S(1)}, bf16[256,512]{1,0:T(8,128)(2,1)S(1)}, u32[]{:S(2)}, u32[]{:S(2)}) %collective-permute-start.4) | collective-permute-done | bytes 262176 | tf_op jit(solution)/shard_map/ppermute | solution.py:238
  16.7 0.0 collective-permute-start.5
  16.7 0.5 collective-permute-start.6
  17.3 3.0 %collective-permute-done.7.received.sooner = f32[32,2304]{1,0:T(8,128)S(1)} collective-permute-done((f32[32,2304]{1,0:T(8,128)S(1)}, f32[32,2304]{1,0:T(8,128)S(1)}, u32[]{:S(2)}, u32[]{:S(2)}) %collective-permute-start.7) | collective-permute-done | bytes 294944 | tf_op jit(solution)/shard_map/ppermute | solution.py:269
  20.2 0.0 collective-permute-done.5.refs_1_
  20.2 0.0 collective-permute-done.6.refs_3_
  20.2 0.1 join.2.refs_2_
  20.3 0.1 collective-permute-start.11
  20.4 0.6 collective-permute-start.9
  21.0 1.6 %collective-permute-start.10 = (bf16[256,512]{1,0:T(8,128)(2,1)S(1)}, bf16[256,512]{1,0:T(8,128)(2,1)S(1)}, u32[]{:S(2)}, u32[]{:S(2)}) collective-permute-start(bf16[256,512]{1,0:T(8,128)(2,1)S(1)} %collective-permute-done.4.refs_2_), channel_id=1, source_target_pairs={{0,2},{1,3},{2,0},{3,1},{4,6},{5,7},{6,4},{7,5},{8,10},{9,11},{10,... | collective-permute-start | bytes 786440 | tf_op jit(solution)/shard_map/ppermute | solution.py:238
  22.6 6.8 %collective-permute-done.10.refs_0_ = bf16[256,512]{1,0:T(8,128)(2,1)S(1)} collective-permute-done((bf16[256,512]{1,0:T(8,128)(2,1)S(1)}, bf16[256,512]{1,0:T(8,128)(2,1)S(1)}, u32[]{:S(2)}, u32[]{:S(2)}) %collective-permute-start.10) | collective-permute-done | bytes 262176 | tf_op jit(solution)/shard_map/ppermute | solution.py:238
  29.3 0.0 collective-permute-done.11.refs_1_
  29.3 0.0 collective-permute-start.12
  29.3 1.6 %collective-permute-start.15 = (bf16[256,512]{1,0:T(8,128)(2,1)S(1)}, bf16[256,512]{1,0:T(8,128)(2,1)S(1)}, u32[]{:S(2)}, u32[]{:S(2)}) collective-permute-start(bf16[256,512]{1,0:T(8,128)(2,1)S(1)} %get-tuple-element.77), channel_id=1, source_target_pairs={{0,2},{1,3},{2,0},{3,1},{4,6},{5,7},{6,4},{7,5},{8,10},{9,11},{10,... | collective-permute-start | bytes 786440 | tf_op jit(solution)/shard_map/ppermute | solution.py:238
  30.9 0.0 collective-permute-done.12.refs_1_
  30.9 1.1 %collective-permute-start.13 = (bf16[512,512]{1,0:T(8,128)(2,1)S(1)}, bf16[512,512]{1,0:T(8,128)(2,1)S(1)}, u32[]{:S(2)}, u32[]{:S(2)}) collective-permute-start(bf16[512,512]{1,0:T(8,128)(2,1)S(1)} %join.3.refs_4_), channel_id=1, source_target_pairs={{0,8},{1,17},{2,10},{3,19},{4,12},{5,21},{6,14},{7,23},{8,0},{9,25... | collective-permute-start | bytes 1572872 | tf_op jit(solution)/shard_map/ppermute | solution.py:269
  32.1 1.1 %collective-permute-start.8 = (f32[32,2304]{1,0:T(8,128)S(1)}, f32[32,2304]{1,0:T(8,128)S(1)}, u32[]{:S(2)}, u32[]{:S(2)}) collective-permute-start(f32[32,2304]{1,0:T(8,128)S(1)} %pass_on.1), channel_id=1, source_target_pairs={{0,16},{1,9},{2,18},{3,11},{4,20},{5,13},{6,22},{7,15},{8,24},{9,1... | collective-permute-start | bytes 884744 | tf_op jit(solution)/shard_map/ppermute | solution.py:269
  33.1 4.9 %collective-permute-done.15.refs_0_.refs_5_ = bf16[256,512]{1,0:T(8,128)(2,1)S(1)} collective-permute-done((bf16[256,512]{1,0:T(8,128)(2,1)S(1)}, bf16[256,512]{1,0:T(8,128)(2,1)S(1)}, u32[]{:S(2)}, u32[]{:S(2)}) %collective-permute-start.15) | collective-permute-done | bytes 262176 | tf_op jit(solution)/shard_map/ppermute | solution.py:238
  38.0 0.9 %collective-permute-start.16 = (bf16[256,512]{1,0:T(8,128)(2,1)S(1)}, bf16[256,512]{1,0:T(8,128)(2,1)S(1)}, u32[]{:S(2)}, u32[]{:S(2)}) collective-permute-start(bf16[256,512]{1,0:T(8,128)(2,1)S(1)} %get-tuple-element.77), channel_id=1, source_target_pairs={{0,6},{1,7},{2,4},{3,5},{4,2},{5,3},{6,0},{7,1},{8,14},{9,15},{10,... | collective-permute-start | bytes 786440 | tf_op jit(solution)/shard_map/ppermute | solution.py:238
  38.9 0.0 collective-permute-done.9.value.refs_3_
  38.9 1.2 %collective-permute-start.14 = (bf16[256,512]{1,0:T(8,128)(2,1)S(1)}, bf16[256,512]{1,0:T(8,128)(2,1)S(1)}, u32[]{:S(2)}, u32[]{:S(2)}) collective-permute-start(bf16[256,512]{1,0:T(8,128)(2,1)S(1)} %take.1), channel_id=1, source_target_pairs={{0,16},{1,9},{2,18},{3,11},{4,20},{5,13},{6,22},{7,15},{8,24},{9,1... | collective-permute-start | bytes 786440 | tf_op jit(solution)/shard_map/ppermute | solution.py:269
  40.1 2.0 %collective-permute-done.8.later = f32[32,2304]{1,0:T(8,128)S(1)} collective-permute-done((f32[32,2304]{1,0:T(8,128)S(1)}, f32[32,2304]{1,0:T(8,128)S(1)}, u32[]{:S(2)}, u32[]{:S(2)}) %collective-permute-start.8) | collective-permute-done | bytes 294944 | tf_op jit(solution)/shard_map/ppermute | solution.py:269
  42.1 1.5 %low_rank.1 = (bf16[32,8192]{1,0:T(8,128)(2,1)S(1)}, f32[16,512]{1,0:T(8,128)S(1)}, f32[128,16]{1,0:T(8,128)S(1)}, f32[128,512]{1,0:T(8,128)S(1)}, f32[4,128]{1,0:T(4,128)S(1)}) custom-call(bf16[128,8192]{1,0:T(8,128)(2,1)S(1)} %copy-done, f32[4,128]{1,0:T(4,128)S(1)} %get-tuple-element.61.slots, f32[16,2304]{1,0:T(8,128)S(1)} %get-tuple-element.62.own, ...), custom_call_target="tpu_custom_call" | custom-call | tf_op jit(solution)/shard_map/low_rank/pallas_call | solution.py:33
  43.6 0.8 %base.2.before = f32[128,512]{1,0:T(8,128)S(1)} custom-call(bf16[128,8192]{1,0:T(8,128)(2,1)S(1)} %copy-done, f32[128,512]{1,0:T(8,128)S(1)} %get-tuple-element.78.before, bf16[1024,512]{1,0:T(8,128)(2,1)S(1)} %copy-done.2, bf16[1024,512]{1,0:T(8,128)(2,1)S(1)} %collective-permute-done.11.refs_1_, bf16[1024,512]{1,0:T(8,128)(2,1)S(1)} %join.2.refs_2_, ...), custom_call_target="tpu_custom_call" | custom-call | tf_op jit(solution)/shard_map/base/pallas_call | solution.py:33
  44.4 0.0 copy-start.4
  44.4 0.0 copy-start.6
  44.5 7.1 %collective-permute-done.16.refs_1_.refs_6_ = bf16[256,512]{1,0:T(8,128)(2,1)S(1)} collective-permute-done((bf16[256,512]{1,0:T(8,128)(2,1)S(1)}, bf16[256,512]{1,0:T(8,128)(2,1)S(1)}, u32[]{:S(2)}, u32[]{:S(2)}) %collective-permute-start.16) | collective-permute-done | bytes 262176 | tf_op jit(solution)/shard_map/ppermute | solution.py:238
  51.6 0.0 collective-permute-done.14.refs_3_.refs_8_
  51.6 0.5 collective-permute-start.20
  52.1 0.1 collective-permute-start.18
  52.2 0.4 collective-permute-start.19
  52.6 0.1 collective-permute-start.21
  52.7 0.4 base.3.refs_1_
  53.1 2.3 %collective-permute-done.18.refs_7_.refs_10_ = bf16[256,512]{1,0:T(8,128)(2,1)S(1)} collective-permute-done((bf16[256,512]{1,0:T(8,128)(2,1)S(1)}, bf16[256,512]{1,0:T(8,128)(2,1)S(1)}, u32[]{:S(2)}, u32[]{:S(2)}) %collective-permute-start.18) | collective-permute-done | bytes 262176 | tf_op jit(solution)/shard_map/ppermute | solution.py:238
  55.4 0.4 collective-permute-done.19.refs_8_.refs_11_
  55.8 0.4 collective-permute-done.21.refs_10_.refs_13_
  56.1 0.0 collective-permute-done.20.refs_9_.refs_12_
  56.1 0.0 collective-permute-done.17.refs_6_.refs_9_
  56.2 2.8 %key_norm.1 = (bf16[128,512]{1,0:T(8,128)(2,1)}, bf16[128,512]{1,0:T(8,128)(2,1)S(1)}, f32[128,16]{1,0:T(8,128)S(1)}, f32[16,2176]{1,0:T(8,128)S(1)}, f32[16,217...) custom-call(f32[4,128]{1,0:T(4,128)S(1)} %get-tuple-element.69.told, bf16[128,8192]{1,0:T(8,128)(2,1)S(1)} %copy-done, ...), custom_call_target="tpu_custom_call" | custom-call | tf_op jit(solution)/shard_map/key_norm/pallas_call | solution.py:33
  59.0 1.0 %collective-permute-start.22 = (f32[16,2176]{1,0:T(8,128)S(1)}, f32[16,2176]{1,0:T(8,128)S(1)}, u32[]{:S(2)}, u32[]{:S(2)}) collective-permute-start(f32[16,2176]{1,0:T(8,128)S(1)} %get-tuple-element.93), channel_id=1, source_target_pairs={{0,8},{8,0},{16,24},{24,16},{1,9},{9,1},{17,25},{25,17},{2,10},{10... | collective-permute-start | bytes 417800 | tf_op jit(solution)/shard_map/ppermute | solution.py:238
  60.0 1.0 %collective-permute-start.23 = (f32[16,2176]{1,0:T(8,128)S(1)}, f32[16,2176]{1,0:T(8,128)S(1)}, u32[]{:S(2)}, u32[]{:S(2)}) collective-permute-start(f32[16,2176]{1,0:T(8,128)S(1)} %get-tuple-element.94), channel_id=1, source_target_pairs={{0,16},{8,24},{16,0},{24,8},{1,17},{9,25},{17,1},{25,9},{2,18},{10... | collective-permute-start | bytes 417800 | tf_op jit(solution)/shard_map/ppermute | solution.py:238
  61.1 1.4 %collective-permute-start.24 = (f32[16,2176]{1,0:T(8,128)S(1)}, f32[16,2176]{1,0:T(8,128)S(1)}, u32[]{:S(2)}, u32[]{:S(2)}) collective-permute-start(f32[16,2176]{1,0:T(8,128)S(1)} %get-tuple-element.95), channel_id=1, source_target_pairs={{0,24},{8,16},{16,8},{24,0},{1,25},{9,17},{17,9},{25,1},{2,26},{10... | collective-permute-start | bytes 417800 | tf_op jit(solution)/shard_map/ppermute | solution.py:238
  62.5 4.7 %input_grad.1 = bf16[128,8192]{1,0:T(8,128)(2,1)} custom-call(bf16[128,512]{1,0:T(8,128)(2,1)S(1)} %get-tuple-element.89.pre_low, f32[128,16]{1,0:T(8,128)S(1)} %get-tuple-element.90.low_grad, bf16[32,8192]{1,0:T(8,128)(2,1)S(1)} %get-tuple-element.91.split, bf16[1024,512]{1,0:T(8,128)(2,1)S(1)} %copy-done.2, ...), custom_call_target="tpu_custom_call" | custom-call | tf_op jit(solution)/shard_map/input_grad/pallas_call | solution.py:33
  67.2 0.0 collective-permute-done.23.refs_2_
  67.2 1.4 %collective-permute-done.24.refs_3_ = f32[16,2176]{1,0:T(8,128)S(1)} collective-permute-done((f32[16,2176]{1,0:T(8,128)S(1)}, f32[16,2176]{1,0:T(8,128)S(1)}, u32[]{:S(2)}, u32[]{:S(2)}) %collective-permute-start.24) | collective-permute-done | bytes 139296 | tf_op jit(solution)/shard_map/ppermute | solution.py:238
  68.7 0.9 %grad_sum.1 = (f32[3,16,2048]{2,1,0:T(8,128)}, f32[3,16,128]{2,1,0:T(8,128)}) custom-call(f32[4,128]{1,0:T(4,128)S(1)} %get-tuple-element.69.told, f32[16,2176]{1,0:T(8,128)S(1)} %get-tuple-element.92.refs_0_, f32[16,2176]{1,0:T(8,128)S(1)} %collective-permute-done.22.refs_1_, f32[16,2176]{1,0:T(8,128)S(1)} %collective-permute-done.23.refs_2_, ...), custom_call_target="tpu_custom_call" | custom-call | tf_op jit(solution)/shard_map/grad_sum/pallas_call | solution.py:33
  (14 shorter events, 0.1 us)
Async XLA Ops:
  0.6 1.2 %copy-start.1 = (bf16[1024,512]{1,0:T(8,128)(2,1)S(1)}, bf16[1024,512]{1,0:T(8,128)(2,1)}, u32[]{:S(2)}) copy-start(bf16[1024,512]{1,0:T(8,128)(2,1)} %refs_0_.5) | copy-start | bytes 3145732
  1.9 18.4 %copy-start.2 = (bf16[1024,512]{1,0:T(8,128)(2,1)S(1)}, bf16[1024,512]{1,0:T(8,128)(2,1)}, u32[]{:S(2)}) copy-start(bf16[1024,512]{1,0:T(8,128)(2,1)} %refs_0_.5) | copy-start | bytes 3145732
  1.9 12.1 %collective-permute-start.3 = (bf16[256,512]{1,0:T(8,128)(2,1)S(1)}, bf16[256,512]{1,0:T(8,128)(2,1)S(1)}, u32[]{:S(2)}, u32[]{:S(2)}) collective-permute-start(bf16[256,512]{1,0:T(8,128)(2,1)S(1)} %get-tuple-element.63), channel_id=1, source_target_pairs={{0,2},{1,3},{2,0},{3,1},{4,6},{5,7},{6,4},{7,5},{8,10},{9,11},{10,... | collective-permute-start | bytes 786440 | tf_op jit(solution)/shard_map/ppermute | solution.py:238
  2.0 14.8 %collective-permute-start.4 = (bf16[256,512]{1,0:T(8,128)(2,1)S(1)}, bf16[256,512]{1,0:T(8,128)(2,1)S(1)}, u32[]{:S(2)}, u32[]{:S(2)}) collective-permute-start(bf16[256,512]{1,0:T(8,128)(2,1)S(1)} %get-tuple-element.63), channel_id=1, source_target_pairs={{0,4},{1,5},{2,6},{3,7},{4,0},{5,1},{6,2},{7,3},{8,12},{9,13},{10,... | collective-permute-start | bytes 786440 | tf_op jit(solution)/shard_map/ppermute | solution.py:238
  5.7 6.0 %collective-permute-start = (f32[1,128]{1,0:T(1,128)S(1)}, f32[1,128]{1,0:T(1,128)S(1)}, u32[]{:S(2)}, u32[]{:S(2)}) collective-permute-start(f32[1,128]{1,0:T(1,128)S(1)} %info.1.refs_0_), channel_id=1, source_target_pairs={{0,8},{8,0},{16,24},{24,16},{1,9},{9,1},{17,25},{25,17},{2,10},{10... | collective-permute-start | bytes 1544 | tf_op jit(solution)/shard_map/ppermute | solution.py:238
  7.2 4.5 %collective-permute-start.1 = (f32[1,128]{1,0:T(1,128)S(1)}, f32[1,128]{1,0:T(1,128)S(1)}, u32[]{:S(2)}, u32[]{:S(2)}) collective-permute-start(f32[1,128]{1,0:T(1,128)S(1)} %info.1.refs_0_), channel_id=1, source_target_pairs={{0,16},{8,24},{16,0},{24,8},{1,17},{9,25},{17,1},{25,9},{2,18},{10... | collective-permute-start | bytes 1544 | tf_op jit(solution)/shard_map/ppermute | solution.py:238
  8.7 4.4 %collective-permute-start.2 = (f32[1,128]{1,0:T(1,128)S(1)}, f32[1,128]{1,0:T(1,128)S(1)}, u32[]{:S(2)}, u32[]{:S(2)}) collective-permute-start(f32[1,128]{1,0:T(1,128)S(1)} %info.1.refs_0_), channel_id=1, source_target_pairs={{0,24},{8,16},{16,8},{24,0},{1,25},{9,17},{17,9},{25,1},{2,26},{10... | collective-permute-start | bytes 1544 | tf_op jit(solution)/shard_map/ppermute | solution.py:238
  9.9 1.0 %copy-start.3 = (f32[3,2048,16]{1,2,0:T(8,128)S(1)}, f32[3,2048,16]{1,2,0:T(8,128)}, u32[]{:S(2)}) copy-start(f32[3,2048,16]{1,2,0:T(8,128)} %param.10) | copy-start | bytes 1179652
  10.9 0.7 %copy-start.5 = (f32[3,16,128]{2,1,0:T(8,128)S(1)}, f32[3,16,128]{2,1,0:T(8,128)}, u32[]{:S(2)}) copy-start(f32[3,16,128]{2,1,0:T(8,128)} %up.1) | copy-start | bytes 73732
  13.4 28.7 %copy-start = (bf16[128,8192]{1,0:T(8,128)(2,1)S(1)}, bf16[128,8192]{1,0:T(8,128)(2,1)}, u32[]{:S(2)}) copy-start(bf16[128,8192]{1,0:T(8,128)(2,1)} %refs_0_.4) | copy-start | bytes 6291460
  13.4 6.8 %collective-permute-start.7 = (f32[32,2304]{1,0:T(8,128)S(1)}, f32[32,2304]{1,0:T(8,128)S(1)}, u32[]{:S(2)}, u32[]{:S(2)}) collective-permute-start(f32[32,2304]{1,0:T(8,128)S(1)} %get-tuple-element.64), channel_id=1, source_target_pairs={{0,8},{1,17},{2,10},{3,19},{4,12},{5,21},{6,14},{7,23},{8,0},{9,25... | collective-permute-start | bytes 884744 | tf_op jit(solution)/shard_map/ppermute | solution.py:269
  16.7 3.5 %collective-permute-start.5 = (bf16[256,512]{1,0:T(8,128)(2,1)S(1)}, bf16[256,512]{1,0:T(8,128)(2,1)S(1)}, u32[]{:S(2)}, u32[]{:S(2)}) collective-permute-start(bf16[256,512]{1,0:T(8,128)(2,1)S(1)} %collective-permute-done.3.refs_0_), channel_id=1, source_target_pairs={{0,1},{1,0},{2,3},{3,2},{4,5},{5,4},{6,7},{7,6},{8,9},{9,8},{10,11... | collective-permute-start | bytes 786440 | tf_op jit(solution)/shard_map/ppermute | solution.py:238
  16.7 3.5 %collective-permute-start.6 = (bf16[256,512]{1,0:T(8,128)(2,1)S(1)}, bf16[256,512]{1,0:T(8,128)(2,1)S(1)}, u32[]{:S(2)}, u32[]{:S(2)}) collective-permute-start(bf16[256,512]{1,0:T(8,128)(2,1)S(1)} %collective-permute-done.4.refs_2_), channel_id=1, source_target_pairs={{0,1},{1,0},{2,3},{3,2},{4,5},{5,4},{6,7},{7,6},{8,9},{9,8},{10,11... | collective-permute-start | bytes 786440 | tf_op jit(solution)/shard_map/ppermute | solution.py:238
  20.3 9.0 %collective-permute-start.11 = (bf16[1024,512]{1,0:T(8,128)(2,1)S(1)}, bf16[1024,512]{1,0:T(8,128)(2,1)S(1)}, u32[]{:S(2)}, u32[]{:S(2)}) collective-permute-start(bf16[1024,512]{1,0:T(8,128)(2,1)S(1)} %copy-done.2), channel_id=1, source_target_pairs={{0,1},{1,0},{2,3},{3,2},{4,5},{5,4},{6,7},{7,6},{8,9},{9,8},{10,11... | collective-permute-start | bytes 3145736 | tf_op jit(solution)/shard_map/ppermute | solution.py:238
  20.4 18.5 %collective-permute-start.9 = (bf16[1024,512]{1,0:T(8,128)(2,1)S(1)}, bf16[1024,512]{1,0:T(8,128)(2,1)S(1)}, u32[]{:S(2)}, u32[]{:S(2)}) collective-permute-start(bf16[1024,512]{1,0:T(8,128)(2,1)S(1)} %join.2.refs_2_), channel_id=1, source_target_pairs={{0,8},{1,17},{2,10},{3,19},{4,12},{5,21},{6,14},{7,23},{8,0},{9,25... | collective-permute-start | bytes 3145736 | tf_op jit(solution)/shard_map/ppermute | solution.py:269
  21.0 8.3 %collective-permute-start.10 = (bf16[256,512]{1,0:T(8,128)(2,1)S(1)}, bf16[256,512]{1,0:T(8,128)(2,1)S(1)}, u32[]{:S(2)}, u32[]{:S(2)}) collective-permute-start(bf16[256,512]{1,0:T(8,128)(2,1)S(1)} %collective-permute-done.4.refs_2_), channel_id=1, source_target_pairs={{0,2},{1,3},{2,0},{3,1},{4,6},{5,7},{6,4},{7,5},{8,10},{9,11},{10,... | collective-permute-start | bytes 786440 | tf_op jit(solution)/shard_map/ppermute | solution.py:238
  29.3 1.6 %collective-permute-start.12 = (bf16[256,512]{1,0:T(8,128)(2,1)S(1)}, bf16[256,512]{1,0:T(8,128)(2,1)S(1)}, u32[]{:S(2)}, u32[]{:S(2)}) collective-permute-start(bf16[256,512]{1,0:T(8,128)(2,1)S(1)} %collective-permute-done.10.refs_0_), channel_id=1, source_target_pairs={{0,1},{1,0},{2,3},{3,2},{4,5},{5,4},{6,7},{7,6},{8,9},{9,8},{10,11... | collective-permute-start | bytes 786440 | tf_op jit(solution)/shard_map/ppermute | solution.py:238
  29.3 8.7 %collective-permute-start.15 = (bf16[256,512]{1,0:T(8,128)(2,1)S(1)}, bf16[256,512]{1,0:T(8,128)(2,1)S(1)}, u32[]{:S(2)}, u32[]{:S(2)}) collective-permute-start(bf16[256,512]{1,0:T(8,128)(2,1)S(1)} %get-tuple-element.77), channel_id=1, source_target_pairs={{0,2},{1,3},{2,0},{3,1},{4,6},{5,7},{6,4},{7,5},{8,10},{9,11},{10,... | collective-permute-start | bytes 786440 | tf_op jit(solution)/shard_map/ppermute | solution.py:238
  30.9 20.7 %collective-permute-start.13 = (bf16[512,512]{1,0:T(8,128)(2,1)S(1)}, bf16[512,512]{1,0:T(8,128)(2,1)S(1)}, u32[]{:S(2)}, u32[]{:S(2)}) collective-permute-start(bf16[512,512]{1,0:T(8,128)(2,1)S(1)} %join.3.refs_4_), channel_id=1, source_target_pairs={{0,8},{1,17},{2,10},{3,19},{4,12},{5,21},{6,14},{7,23},{8,0},{9,25... | collective-permute-start | bytes 1572872 | tf_op jit(solution)/shard_map/ppermute | solution.py:269
  32.1 10.0 %collective-permute-start.8 = (f32[32,2304]{1,0:T(8,128)S(1)}, f32[32,2304]{1,0:T(8,128)S(1)}, u32[]{:S(2)}, u32[]{:S(2)}) collective-permute-start(f32[32,2304]{1,0:T(8,128)S(1)} %pass_on.1), channel_id=1, source_target_pairs={{0,16},{1,9},{2,18},{3,11},{4,20},{5,13},{6,22},{7,15},{8,24},{9,1... | collective-permute-start | bytes 884744 | tf_op jit(solution)/shard_map/ppermute | solution.py:269
  38.0 13.6 %collective-permute-start.16 = (bf16[256,512]{1,0:T(8,128)(2,1)S(1)}, bf16[256,512]{1,0:T(8,128)(2,1)S(1)}, u32[]{:S(2)}, u32[]{:S(2)}) collective-permute-start(bf16[256,512]{1,0:T(8,128)(2,1)S(1)} %get-tuple-element.77), channel_id=1, source_target_pairs={{0,6},{1,7},{2,4},{3,5},{4,2},{5,3},{6,0},{7,1},{8,14},{9,15},{10,... | collective-permute-start | bytes 786440 | tf_op jit(solution)/shard_map/ppermute | solution.py:238
  38.9 12.7 %collective-permute-start.14 = (bf16[256,512]{1,0:T(8,128)(2,1)S(1)}, bf16[256,512]{1,0:T(8,128)(2,1)S(1)}, u32[]{:S(2)}, u32[]{:S(2)}) collective-permute-start(bf16[256,512]{1,0:T(8,128)(2,1)S(1)} %take.1), channel_id=1, source_target_pairs={{0,16},{1,9},{2,18},{3,11},{4,20},{5,13},{6,22},{7,15},{8,24},{9,1... | collective-permute-start | bytes 786440 | tf_op jit(solution)/shard_map/ppermute | solution.py:269
  44.4 11.7 %copy-start.4 = (bf16[128,512]{1,0:T(8,128)(2,1)S(1)}, bf16[128,512]{1,0:T(8,128)(2,1)}, u32[]{:S(2)}) copy-start(bf16[128,512]{1,0:T(8,128)(2,1)} %refs_2_.1) | copy-start | bytes 393220
  44.4 11.7 %copy-start.6 = (f32[128]{0:T(128)S(1)}, f32[128]{0:T(128)}, u32[]{:S(2)}) copy-start(f32[128]{0:T(128)} %param.12) | copy-start | bytes 1540
  51.6 4.5 %collective-permute-start.17 = (bf16[1024,512]{1,0:T(8,128)(2,1)S(1)}, bf16[1024,512]{1,0:T(8,128)(2,1)S(1)}, u32[]{:S(2)}, u32[]{:S(2)}) collective-permute-start(bf16[1024,512]{1,0:T(8,128)(2,1)S(1)} %collective-permute-done.9.value.refs_3_), channel_id=1, source_target_pairs={{0,1},{1,0},{2,3},{3,2},{4,5},{5,4},{6,7},{7,6},{8,9},{9,8},{10,11... | collective-permute-start | bytes 3145736 | tf_op jit(solution)/shard_map/ppermute | solution.py:238
  51.6 4.5 %collective-permute-start.20 = (bf16[512,512]{1,0:T(8,128)(2,1)S(1)}, bf16[512,512]{1,0:T(8,128)(2,1)S(1)}, u32[]{:S(2)}, u32[]{:S(2)}) collective-permute-start(bf16[512,512]{1,0:T(8,128)(2,1)S(1)} %collective-permute-done.13.refs_2_.refs_7_), channel_id=1, source_target_pairs={{0,1},{1,0},{2,3},{3,2},{4,5},{5,4},{6,7},{7,6},{8,9},{9,8},{10,11... | collective-permute-start | bytes 1572872 | tf_op jit(solution)/shard_map/ppermute | solution.py:238
  52.1 3.3 %collective-permute-start.18 = (bf16[256,512]{1,0:T(8,128)(2,1)S(1)}, bf16[256,512]{1,0:T(8,128)(2,1)S(1)}, u32[]{:S(2)}, u32[]{:S(2)}) collective-permute-start(bf16[256,512]{1,0:T(8,128)(2,1)S(1)} %collective-permute-done.15.refs_0_.refs_5_), channel_id=1, source_target_pairs={{0,1},{1,0},{2,3},{3,2},{4,5},{5,4},{6,7},{7,6},{8,9},{9,8},{10,11... | collective-permute-start | bytes 786440 | tf_op jit(solution)/shard_map/ppermute | solution.py:238
  52.2 3.6 %collective-permute-start.19 = (bf16[256,512]{1,0:T(8,128)(2,1)S(1)}, bf16[256,512]{1,0:T(8,128)(2,1)S(1)}, u32[]{:S(2)}, u32[]{:S(2)}) collective-permute-start(bf16[256,512]{1,0:T(8,128)(2,1)S(1)} %collective-permute-done.16.refs_1_.refs_6_), channel_id=1, source_target_pairs={{0,1},{1,0},{2,3},{3,2},{4,5},{5,4},{6,7},{7,6},{8,9},{9,8},{10,11... | collective-permute-start | bytes 786440 | tf_op jit(solution)/shard_map/ppermute | solution.py:238
  52.6 3.5 %collective-permute-start.21 = (bf16[256,512]{1,0:T(8,128)(2,1)S(1)}, bf16[256,512]{1,0:T(8,128)(2,1)S(1)}, u32[]{:S(2)}, u32[]{:S(2)}) collective-permute-start(bf16[256,512]{1,0:T(8,128)(2,1)S(1)} %collective-permute-done.14.refs_3_.refs_8_), channel_id=1, source_target_pairs={{0,1},{1,0},{2,3},{3,2},{4,5},{5,4},{6,7},{7,6},{8,9},{9,8},{10,11... | collective-permute-start | bytes 786440 | tf_op jit(solution)/shard_map/ppermute | solution.py:238
  59.0 8.2 %collective-permute-start.22 = (f32[16,2176]{1,0:T(8,128)S(1)}, f32[16,2176]{1,0:T(8,128)S(1)}, u32[]{:S(2)}, u32[]{:S(2)}) collective-permute-start(f32[16,2176]{1,0:T(8,128)S(1)} %get-tuple-element.93), channel_id=1, source_target_pairs={{0,8},{8,0},{16,24},{24,16},{1,9},{9,1},{17,25},{25,17},{2,10},{10... | collective-permute-start | bytes 417800 | tf_op jit(solution)/shard_map/ppermute | solution.py:238
  60.0 7.2 %collective-permute-start.23 = (f32[16,2176]{1,0:T(8,128)S(1)}, f32[16,2176]{1,0:T(8,128)S(1)}, u32[]{:S(2)}, u32[]{:S(2)}) collective-permute-start(f32[16,2176]{1,0:T(8,128)S(1)} %get-tuple-element.94), channel_id=1, source_target_pairs={{0,16},{8,24},{16,0},{24,8},{1,17},{9,25},{17,1},{25,9},{2,18},{10... | collective-permute-start | bytes 417800 | tf_op jit(solution)/shard_map/ppermute | solution.py:238
  61.1 7.6 %collective-permute-start.24 = (f32[16,2176]{1,0:T(8,128)S(1)}, f32[16,2176]{1,0:T(8,128)S(1)}, u32[]{:S(2)}, u32[]{:S(2)}) collective-permute-start(f32[16,2176]{1,0:T(8,128)S(1)} %get-tuple-element.95), channel_id=1, source_target_pairs={{0,24},{8,16},{16,8},{24,0},{1,25},{9,17},{17,9},{25,1},{2,26},{10... | collective-permute-start | bytes 417800 | tf_op jit(solution)/shard_map/ppermute | solution.py:238

commit v3 on v2

--- a/solution.py
+++ b/solution.py
@@ -29,15 +29,14 @@
     return high, low
 
 
-def call(kernel, outs, ins, name, scratch=(), limit=VMEM_LIMIT):
+def call(kernel, outs, ins, name, moved=0):
     return pl.pallas_call(
         kernel,
         out_shape=[jax.ShapeDtypeStruct(shape, dtype) for shape, dtype in outs],
         in_specs=[spec for spec, _ in ins],
         out_specs=[vmem] * len(outs),
-        scratch_shapes=scratch,
-        compiler_params=pltpu.CompilerParams(vmem_limit_bytes=limit),
-        cost_estimate=pl.CostEstimate(flops=0, bytes_accessed=0, transcendentals=0),
+        compiler_params=pltpu.CompilerParams(vmem_limit_bytes=VMEM_LIMIT),
+        cost_estimate=pl.CostEstimate(flops=0, bytes_accessed=moved, transcendentals=0),
         name=name,
     )(*[value for _, value in ins])
 
@@ -47,12 +46,12 @@
     return lax.axis_index("dp"), lax.div(fsdp, CORES), lax.rem(fsdp, CORES)
 
 
-def start_kernel(matrix, near, far):
-    rows = near.shape[0]
-    parts = matrix.shape[0] // rows
-    for out, bits in ((near, 0), (far, parts - 1)):
-        part = lax.axis_index("dp") ^ bits
-        out[...] = matrix[pl.ds(pl.multiple_of(part * rows, rows), rows), :]
+def part_kernel(bits, *refs):
+    out = refs[-1]
+    rows = out.shape[0] // (len(refs) - 1)
+    part = lax.axis_index("dp") ^ bits
+    for index, matrix in enumerate(refs[:-1]):
+        out[index * rows : (index + 1) * rows] = matrix[pl.ds(pl.multiple_of(part * rows, rows), rows), :]
 
 
 def info_kernel(offset, info):
@@ -98,9 +97,11 @@
 
 
 def join_kernel(each, *refs):
-    out = refs[-1]
-    for index, ref in enumerate(refs[:-1]):
-        out[index * each : (index + 1) * each] = ref[:each]
+    out, first = refs[-1], 0
+    for ref in refs[:-1]:
+        rows = each or ref.shape[0]
+        out[first : first + rows] = ref[:rows]
+        first += rows
 
 
 def low_rank_kernel(tokens, slots, own, sooner, later, split, up, low_rank, total, told):
@@ -140,26 +141,30 @@
     return pl.multiple_of((shard * parts + part) * part_rows, 128)
 
 
-def base_sum(place, tokens, total, buffers, pieces, sizes):
+def base_sum(place, rows, total, buffers, pieces, sizes):
     for piece in pieces:
         columns = pl.ds(column_of(place, piece, *sizes), piece["rows"])
-        rows = pl.ds(piece["first"], piece["rows"])
-        value = jnp.dot(tokens[:, columns], buffers[piece["buffer"]][rows, :], preferred_element_type=F32)
+        part = pl.ds(piece["first"], piece["rows"])
+        left = jnp.concatenate([ref[:, columns] for ref in rows], axis=0) if len(rows) > 1 else rows[0][:, columns]
+        value = jnp.dot(left, buffers[piece["buffer"]][part, :], preferred_element_type=F32)
         total = value if total is None else total + value
     return total
 
 
-def base_kernel(pieces, sizes, tokens, before, *refs):
-    refs[-1][...] = base_sum(position(), tokens, before[...], refs[:-1], pieces, sizes)
-
-
-def middle_kernel(pieces, sizes, told, *refs):
-    parts = sizes[1]
+def base_kernel(pieces, alone, sizes, tokens, tokens_pair, before, before_pair, *refs):
     place = position()
-    (tokens, before, cotangent, gain, low_rank, up), refs = refs[:6], refs[6:]
-    count = len(refs) - 3 - parts
-    buffers, (keys, pre_low, low_grad), grads = refs[:count], refs[count : count + 3], refs[count + 3 :]
-    projected = base_sum(place, tokens, before[...], buffers, pieces, sizes)
+    buffers, (total, total_pair) = refs[:-2], refs[-2:]
+    count = tokens.shape[0]
+    both = base_sum(place, (tokens, tokens_pair), None, buffers, alone, sizes)
+    total[...] = base_sum(place, (tokens,), before[...] + both[:count], buffers, pieces, sizes)
+    total_pair[...] = before_pair[...] + both[count:]
+
+
+def middle_kernel(parts, told, *refs):
+    place = position()
+    (tokens, own, received, cotangent, gain, low_rank, up), refs = refs[:7], refs[7:]
+    (keys, pre_low, low_grad), grads = refs[:3], refs[3:]
+    projected = own[...] + received[...]
     rows, width = projected.shape
     gains = gain[...]
     slots, counts = told[:, :1], told[:, 1:2]
@@ -277,8 +282,8 @@
 
     matrix = frozen_key_matrix
     part = ((part_rows, key_width), BF16)
-    near, far = call(start_kernel, [part, part], [(vmem, matrix)], "start")
-    z1, z2 = over_z(near, 1), over_z(near, 2)
+    (near,) = call(functools.partial(part_kernel, 0), [part], [(vmem, matrix)], "near")
+    z2, z1 = over_z(near, 2), over_z(near, 1)
     (info,) = call(info_kernel, [((1, HD), F32)], [(vmem, adapter_offset)], "info")
     offsets = [info] + [over_dp(info, bits) for bits in range(1, parts)]
     held = call(
@@ -295,22 +300,26 @@
         [(vmem, value) for value in (*offsets, *held)],
         "adapter_messages",
     )
-    z1, z2 = ordered((z1, z2), sooner)
+    z2, z1 = ordered((z2, z1), sooner)
     sooner = over_split(sooner, (1, 2), (0, 0))
     z3 = over_z(z2, 1)
     z1_pair, z2_pair, sooner = lax.optimization_barrier((over_core(z1), over_core(z2), sooner))
     m12 = joined(z1, z1_pair, z2, z2_pair)
     xy12 = over_split(m12, (1, 2), (0, 0))
-    d1 = over_z(ordered(far, m12), 1)
+    matrix_pair, tokens_pair = over_core(ordered(matrix, m12)), over_core(ordered(tokens, m12))
+    z3, matrix_pair, tokens_pair = lax.optimization_barrier((z3, matrix_pair, tokens_pair))
     (onward,) = call(pass_on_kernel, [((2 * rank, wide), F32)], [(vmem, later), (vmem, sooner)], "pass_on")
     later = over_split(onward, (2, 1), (0, 0))
-    d3 = over_z(ordered(far, d1), 3)
-    z3, matrix_pair = lax.optimization_barrier((z3, over_core(ordered(matrix, m12))))
     m3 = joined(z3, over_core(z3))
     xy3 = over_split(m3, (1, 2), (0, 0))
+    (fars,) = call(
+        functools.partial(part_kernel, parts - 1), [(near_both, BF16)], [(vmem, matrix), (vmem, matrix_pair)], "far"
+    )
+    d13 = over_split(ordered(fars, z3), (0, 0), (1, 3))
     xy12 = ordered(xy12, m3)
     (m4,) = call(functools.partial(take_kernel, part_rows, (2,)), [part], [(vmem, xy12)], "take")
     xy4 = over_split(m4, (2, 1), (0, 0))
+
     def piece(z, dp_bits, core, count=part_rows, first=0):
         pair = lambda value: value if isinstance(value, tuple) else (value, value)
         dp_bits = None if dp_bits is None else pair(dp_bits)
@@ -324,15 +333,16 @@
         pieces = [dict(item, buffer=index) for index, (_, items) in enumerate(batch) for item in items]
         return buffers, pieces
 
-    def base(before, batch):
-        buffers, pieces = flat(batch)
-        (total,) = call(
-            functools.partial(base_kernel, pieces, (part_rows, parts)),
-            [((rows, key_width), F32)],
-            [(vmem, tokens), (vmem, before)] + [(vmem, value) for value in buffers],
+    def base(before, shared, alone):
+        buffers, pieces = flat(shared + alone)
+        mine = [item for item in pieces if item["buffer"] < len(shared)]
+        lone = [item for item in pieces if item["buffer"] >= len(shared)]
+        return call(
+            functools.partial(base_kernel, mine, lone, (part_rows, parts)),
+            [((rows, key_width), F32)] * 2,
+            [(vmem, value) for value in (tokens, tokens_pair, *before, *buffers)],
             "base",
         )
-        return total
 
     split, up, low_rank, total, told = call(
         low_rank_kernel,
@@ -345,46 +355,51 @@
         ],
         [(vmem, value) for value in (tokens, slots, own, sooner, later)],
         "low_rank",
-    )
-    batch0 = [
+        moved=12 * 2**20,
+    )
+    last = CORES * part_rows
+    shared = [
         (matrix, [piece(0, None, 0, shard_rows)]),
         (matrix_pair, [piece(0, None, 1, shard_rows)]),
-        (m12, two(1, 0) + two(2, 0, 0, CORES * part_rows)),
-        (xy12, two(1, (1, 2)) + two(2, (1, 2), 0, CORES * part_rows)),
+        (m12, two(1, 0) + two(2, 0, 0, last)),
         (m3, two(3, 0)),
     ]
-    total = base(total, batch0)
-    xy12, xy3, xy4, d1, d3, total = lax.optimization_barrier((xy12, xy3, xy4, d1, d3, total))
-    batch1 = [
-        (d1, [piece(1, 3, 0)]),
-        (d3, [piece(3, 3, 0)]),
-        (xy3, two(3, (1, 2))),
-        (xy4, [piece(2, 3, 0)]),
+    early = [(xy12, two(1, (1, 2)) + two(2, (1, 2), 0, last))]
+    totals = base((total, jnp.zeros_like(total)), shared, early)
+    xy12, xy3, xy4, d13, totals = lax.optimization_barrier((xy12, xy3, xy4, d13, totals))
+    late = [(xy3, two(3, (1, 2))), (d13, two((1, 3), 3)), (xy4, [piece(2, 3, 0)])]
+    total, total_pair = base(totals, [], late)
+    received = over_core(total_pair)
+    lone = call(
+        functools.partial(join_kernel, None),
+        [((5 * part_rows, key_width), BF16)],
+        [(vmem, value) for value in (xy3, d13, xy4)],
+        "join",
+    )[0]
+    xy12_pair, lone_pair = over_core(ordered(xy12, received)), over_core(ordered(lone, received))
+    keys, pre_low, low_grad, *grads = call(
+        functools.partial(middle_kernel, parts),
+        [((rows, key_width), BF16), ((rows, key_width), BF16), ((rows, rank), F32)]
+        + [((rank, down_width + up_width), F32)] * parts,
+        [
+            (vmem, value)
+            for value in (told, tokens, total, received, cotangent, key_norm_gain.reshape(1, HD), low_rank, up)
+        ],
+        "key_norm",
+    )
+    others = [
+        (xy12_pair, two(1, (2, 1), 1) + two(2, (2, 1), 1, last)),
+        (lone_pair, two(3, (2, 1), 1) + two((3, 1), 3, 1, last) + [piece(2, 3, 1, first=2 * last)]),
     ]
-    total = base(total, batch1)
-    batch2 = [
-        (over_core(xy12), two(1, (2, 1), 1) + two(2, (2, 1), 1, CORES * part_rows)),
-        (over_core(d1), [piece(1, 3, 1)]),
-        (over_core(d3), [piece(3, 3, 1)]),
-        (over_core(xy3), two(3, (2, 1), 1)),
-        (over_core(xy4), [piece(2, 3, 1)]),
-    ]
-    buffers, pieces = flat(batch2)
-    keys, pre_low, low_grad, *grads = call(
-        functools.partial(middle_kernel, pieces, (part_rows, parts)),
-        [((rows, key_width), BF16), ((rows, key_width), BF16), ((rows, rank), F32)] + [((rank, down_width + up_width), F32)] * parts,
-        [(vmem, value) for value in (told, tokens, total, cotangent, key_norm_gain.reshape(1, HD), low_rank, up)]
-        + [(vmem, value) for value in buffers],
-        "key_norm",
-    )
     received = [grads[0]] + [over_dp(grads[bits], bits) for bits in range(1, parts)]
-    buffers, pieces = flat(batch0 + batch1 + batch2)
+    buffers, pieces = flat(shared + early + late + others)
     (input_grad,) = call(
         functools.partial(input_grad_kernel, pieces, (part_rows, parts)),
         [((rows, model_width), BF16)],
         [(vmem, pre_low), (vmem, low_grad), (vmem, split)] + [(vmem, value) for value in buffers],
         "input_grad",
     )
+    received, input_grad = lax.optimization_barrier((received, input_grad))
     down_sum, up_sum = call(
         sum_kernel,
         [((stored, rank, down_width), F32), ((stored, rank, up_width), F32)],

time: 69.8 us -> 65 us (0.931)
  the two profiles are of different devices: /device:TPU:8 before, /device:TPU:0 now
where the time goes in v3:
time: 65 us; the launch traced here: 64.7 us
  waiting for transfers between devices  27.1 us (42%)
  starting transfers between devices  20.6 us (32%)
  Pallas kernels  11.8 us (18%)
  local copies, waits for them, and re-layouts  3.13 us (5%)
  between operations  2.1 us (3%)
    ppermute x17, waiting for transfers between devices, flip(): return lax.ppermute(value, axis, [(i, i ^ bits) for i in range(size)])  15.9 us
    ppermute x17, starting transfers between devices, flip(): return lax.ppermute(value, axis, [(i, i ^ bits) for i in range(size)])  14.9 us
    pallas_call x16, Pallas kernels, call(): pl.pallas_call(kernel, out_shape=[jax.ShapeDtypeStruct(shape, dtype) for...  11.8 us
    ppermute x6, waiting for transfers between devices, over_split(): return lax.ppermute(value, ('dp', 'fsdp'), pairs)  11.2 us
    ppermute x6, starting transfers between devices, over_split(): return lax.ppermute(value, ('dp', 'fsdp'), pairs)  5.7 us
    unnamed x14, local copies, waits for them, and re-layouts  3.11 us
  transfers between devices with their start and end apart: 23, of which 11 were waited for; matrix products, arithmetic and copies ran while one was open for 0% of the time, Pallas kernels for 16%

profile of v3, /device:TPU:0, one launch (start us, length us, event | category | flops | bytes accessed | tf_op | source)
XLA Modules:
  0.0 64.7 jit_solution(54638287558328328)
XLA Ops:
  0.7 1.4 %copy-done.1 = bf16[1024,512]{1,0:T(8,128)(2,1)S(1)} copy-done((bf16[1024,512]{1,0:T(8,128)(2,1)S(1)}, bf16[1024,512]{1,0:T(8,128)(2,1)}, u32[]{:S(2)}) %copy-start.1) | copy-done | bytes 1048600
  2.0 3.1 %collective-permute-start.4 = (bf16[256,512]{1,0:T(8,128)(2,1)S(1)}, bf16[256,512]{1,0:T(8,128)(2,1)S(1)}, u32[]{:S(2)}, u32[]{:S(2)}) collective-permute-start(bf16[256,512]{1,0:T(8,128)(2,1)S(1)} %near.1), channel_id=1, source_target_pairs={{0,2},{1,3},{2,0},{3,1},{4,6},{5,7},{6,4},{7,5},{8,10},{9,11},{10,... | collective-permute-start | bytes 786440 | tf_op jit(solution)/shard_map/ppermute | solution.py:243
  5.1 2.6 %collective-permute-start.3 = (bf16[256,512]{1,0:T(8,128)(2,1)S(1)}, bf16[256,512]{1,0:T(8,128)(2,1)S(1)}, u32[]{:S(2)}, u32[]{:S(2)}) collective-permute-start(bf16[256,512]{1,0:T(8,128)(2,1)S(1)} %near.1), channel_id=1, source_target_pairs={{0,4},{1,5},{2,6},{3,7},{4,0},{5,1},{6,2},{7,3},{8,12},{9,13},{10,... | collective-permute-start | bytes 786440 | tf_op jit(solution)/shard_map/ppermute | solution.py:243
  8.4 0.1 info.1.refs_0_
  8.4 2.4 %collective-permute-start.2 = (f32[1,128]{1,0:T(1,128)S(1)}, f32[1,128]{1,0:T(1,128)S(1)}, u32[]{:S(2)}, u32[]{:S(2)}) collective-permute-start(f32[1,128]{1,0:T(1,128)S(1)} %info.1.refs_0_), channel_id=1, source_target_pairs={{0,24},{8,16},{16,8},{24,0},{1,25},{9,17},{17,9},{25,1},{2,26},{10... | collective-permute-start | bytes 1544 | tf_op jit(solution)/shard_map/ppermute | solution.py:243
  10.9 0.5 collective-permute-start.1
  11.4 0.5 collective-permute-start
  12.6 0.0 copy-start.3
  12.6 1.0 %copy-done.3 = f32[3,2048,16]{1,2,0:T(8,128)S(1)} copy-done((f32[3,2048,16]{1,2,0:T(8,128)S(1)}, f32[3,2048,16]{1,2,0:T(8,128)}, u32[]{:S(2)}) %copy-start.3) | copy-done | bytes 393240
  13.6 0.7 %copy-done.5 = f32[3,16,128]{2,1,0:T(8,128)S(1)} copy-done((f32[3,16,128]{2,1,0:T(8,128)S(1)}, f32[3,16,128]{2,1,0:T(8,128)}, u32[]{:S(2)}) %copy-start.5) | copy-done | bytes 24600
  14.3 0.1 hold.1
  14.4 0.0 collective-permute-done.2.refs_3_
  14.4 0.0 collective-permute-done.1.refs_2_
  14.4 0.5 collective-permute-done.refs_1_
  14.9 0.2 adapter_messages.1
  15.2 1.0 %collective-permute-start.7 = (f32[32,2304]{1,0:T(8,128)S(1)}, f32[32,2304]{1,0:T(8,128)S(1)}, u32[]{:S(2)}, u32[]{:S(2)}) collective-permute-start(f32[32,2304]{1,0:T(8,128)S(1)} %get-tuple-element.73), channel_id=1, source_target_pairs={{0,8},{1,17},{2,10},{3,19},{4,12},{5,21},{6,14},{7,23},{8,0},{9,25... | collective-permute-start | bytes 884744 | tf_op jit(solution)/shard_map/ppermute | solution.py:274
  16.2 0.7 %collective-permute-done.4.refs_0_ = bf16[256,512]{1,0:T(8,128)(2,1)S(1)} collective-permute-done((bf16[256,512]{1,0:T(8,128)(2,1)S(1)}, bf16[256,512]{1,0:T(8,128)(2,1)S(1)}, u32[]{:S(2)}, u32[]{:S(2)}) %collective-permute-start.4) | collective-permute-done | bytes 262176 | tf_op jit(solution)/shard_map/ppermute | solution.py:243
  16.9 2.5 %collective-permute-done.3.refs_2_ = bf16[256,512]{1,0:T(8,128)(2,1)S(1)} collective-permute-done((bf16[256,512]{1,0:T(8,128)(2,1)S(1)}, bf16[256,512]{1,0:T(8,128)(2,1)S(1)}, u32[]{:S(2)}, u32[]{:S(2)}) %collective-permute-start.3) | collective-permute-done | bytes 262176 | tf_op jit(solution)/shard_map/ppermute | solution.py:243
  19.5 0.0 collective-permute-start.5
  19.5 0.5 collective-permute-start.6
  20.0 2.0 %collective-permute-done.7.received.sooner = f32[32,2304]{1,0:T(8,128)S(1)} collective-permute-done((f32[32,2304]{1,0:T(8,128)S(1)}, f32[32,2304]{1,0:T(8,128)S(1)}, u32[]{:S(2)}, u32[]{:S(2)}) %collective-permute-start.7) | collective-permute-done | bytes 294944 | tf_op jit(solution)/shard_map/ppermute | solution.py:274
  22.0 0.0 collective-permute-done.5.refs_1_
  22.0 0.0 collective-permute-done.6.refs_3_
  22.0 0.1 join.3.refs_2_
  22.0 0.1 collective-permute-start.11
  22.1 0.5 collective-permute-start.10
  22.6 1.0 %collective-permute-start.12 = (bf16[1024,512]{1,0:T(8,128)(2,1)S(1)}, bf16[1024,512]{1,0:T(8,128)(2,1)S(1)}, u32[]{:S(2)}, u32[]{:S(2)}) collective-permute-start(bf16[1024,512]{1,0:T(8,128)(2,1)S(1)} %join.3.refs_2_), channel_id=1, source_target_pairs={{0,8},{1,17},{2,10},{3,19},{4,12},{5,21},{6,14},{7,23},{8,0},{9,25... | collective-permute-start | bytes 3145736 | tf_op jit(solution)/shard_map/ppermute | solution.py:274
  23.6 0.5 collective-permute-start.9
  24.1 8.1 %collective-permute-done.9.refs_0_ = bf16[256,512]{1,0:T(8,128)(2,1)S(1)} collective-permute-done((bf16[256,512]{1,0:T(8,128)(2,1)S(1)}, bf16[256,512]{1,0:T(8,128)(2,1)S(1)}, u32[]{:S(2)}, u32[]{:S(2)}) %collective-permute-start.9) | collective-permute-done | bytes 262176 | tf_op jit(solution)/shard_map/ppermute | solution.py:243
  32.2 0.0 collective-permute-done.10.refs_1_
  32.2 0.0 collective-permute-done.11.tokens_pair
  32.2 0.0 collective-permute-start.13
  32.2 0.5 collective-permute-start.16
  32.7 1.0 %collective-permute-done.13.refs_1_ = bf16[256,512]{1,0:T(8,128)(2,1)S(1)} collective-permute-done((bf16[256,512]{1,0:T(8,128)(2,1)S(1)}, bf16[256,512]{1,0:T(8,128)(2,1)S(1)}, u32[]{:S(2)}, u32[]{:S(2)}) %collective-permute-start.13) | collective-permute-done | bytes 262176 | tf_op jit(solution)/shard_map/ppermute | solution.py:243
  33.7 1.0 %collective-permute-start.14 = (bf16[512,512]{1,0:T(8,128)(2,1)S(1)}, bf16[512,512]{1,0:T(8,128)(2,1)S(1)}, u32[]{:S(2)}, u32[]{:S(2)}) collective-permute-start(bf16[512,512]{1,0:T(8,128)(2,1)S(1)} %join.4.refs_3_), channel_id=1, source_target_pairs={{0,8},{1,17},{2,10},{3,19},{4,12},{5,21},{6,14},{7,23},{8,0},{9,25... | collective-permute-start | bytes 1572872 | tf_op jit(solution)/shard_map/ppermute | solution.py:274
  34.8 0.6 collective-permute-start.8
  35.4 2.0 %collective-permute-done.12.value.refs_4_ = bf16[1024,512]{1,0:T(8,128)(2,1)S(1)} collective-permute-done((bf16[1024,512]{1,0:T(8,128)(2,1)S(1)}, bf16[1024,512]{1,0:T(8,128)(2,1)S(1)}, u32[]{:S(2)}, u32[]{:S(2)}) %collective-permute-start.12) | collective-permute-done | bytes 1048608 | tf_op jit(solution)/shard_map/ppermute | solution.py:274
  37.4 1.6 %collective-permute-start.15 = (bf16[256,512]{1,0:T(8,128)(2,1)S(1)}, bf16[256,512]{1,0:T(8,128)(2,1)S(1)}, u32[]{:S(2)}, u32[]{:S(2)}) collective-permute-start(bf16[256,512]{1,0:T(8,128)(2,1)S(1)} %take.1), channel_id=1, source_target_pairs={{0,16},{1,9},{2,18},{3,11},{4,20},{5,13},{6,22},{7,15},{8,24},{9,1... | collective-permute-start | bytes 786440 | tf_op jit(solution)/shard_map/ppermute | solution.py:274
  39.0 5.8 %collective-permute-done.8.later = f32[32,2304]{1,0:T(8,128)S(1)} collective-permute-done((f32[32,2304]{1,0:T(8,128)S(1)}, f32[32,2304]{1,0:T(8,128)S(1)}, u32[]{:S(2)}, u32[]{:S(2)}) %collective-permute-start.8) | collective-permute-done | bytes 294944 | tf_op jit(solution)/shard_map/ppermute | solution.py:274
  44.8 1.5 %low_rank.1 = (bf16[32,8192]{1,0:T(8,128)(2,1)S(1)}, f32[16,512]{1,0:T(8,128)S(1)}, f32[128,16]{1,0:T(8,128)S(1)}, f32[128,512]{1,0:T(8,128)S(1)}, f32[4,128]{1,0:T(4,128)S(1)}) custom-call(bf16[128,8192]{1,0:T(8,128)(2,1)S(1)} %copy-done, f32[4,128]{1,0:T(4,128)S(1)} %get-tuple-element.71.slots, f32[16,2304]{1,0:T(8,128)S(1)} %get-tuple-element.72.own, ...), custom_call_target="tpu_custom_call" | custom-call | bytes 12582912 | tf_op jit(solution)/shard_map/low_rank/pallas_call | solution.py:33
  46.4 0.9 %base.2 = (f32[128,512]{1,0:T(8,128)S(1)}, f32[128,512]{1,0:T(8,128)S(1)}) custom-call(bf16[128,8192]{1,0:T(8,128)(2,1)S(1)} %copy-done, bf16[128,8192]{1,0:T(8,128)(2,1)S(1)} %collective-permute-done.11.tokens_pair, f32[128,512]{1,0:T(8,128)S(1)} %get-tuple-element.88.before, f32[128,512]{1,0:T(8,128)S(1)} %broadcast_in_dim.3.before_pair, ...), custom_call_target="tpu_custom_call" | custom-call | tf_op jit(solution)/shard_map/base/pallas_call | solution.py:33
  47.3 1.4 %collective-permute-done.15.refs_2_.refs_7_ = bf16[256,512]{1,0:T(8,128)(2,1)S(1)} collective-permute-done((bf16[256,512]{1,0:T(8,128)(2,1)S(1)}, bf16[256,512]{1,0:T(8,128)(2,1)S(1)}, u32[]{:S(2)}, u32[]{:S(2)}) %collective-permute-start.15) | collective-permute-done | bytes 262176 | tf_op jit(solution)/shard_map/ppermute | solution.py:274
  48.7 0.0 collective-permute-done.16.refs_1_.refs_6_
  48.7 0.0 collective-permute-done.14.refs_0_.refs_5_
  48.7 0.5 base.3
  49.2 0.0 copy-start.4
  49.3 0.0 copy-start.6
  49.3 0.2 collective-permute-start.17
  49.4 0.1 join.5
  49.5 1.3 %collective-permute-done.17.refs_2_ = f32[128,512]{1,0:T(8,128)S(1)} collective-permute-done((f32[128,512]{1,0:T(8,128)S(1)}, f32[128,512]{1,0:T(8,128)S(1)}, u32[]{:S(2)}, u32[]{:S(2)}) %collective-permute-start.17) | collective-permute-done | bytes 262176 | tf_op jit(solution)/shard_map/ppermute | solution.py:243
  50.9 0.1 collective-permute-start.22
  51.0 0.4 collective-permute-start.21
  51.4 0.0 copy-done.4
  51.4 2.5 %key_norm.1 = (bf16[128,512]{1,0:T(8,128)(2,1)}, bf16[128,512]{1,0:T(8,128)(2,1)S(1)}, f32[128,16]{1,0:T(8,128)S(1)}, f32[16,2176]{1,0:T(8,128)S(1)}, f32[16,217...) custom-call(f32[4,128]{1,0:T(4,128)S(1)} %get-tuple-element.78.told, bf16[128,8192]{1,0:T(8,128)(2,1)S(1)} %copy-done, ...), custom_call_target="tpu_custom_call" | custom-call | tf_op jit(solution)/shard_map/key_norm/pallas_call | solution.py:33
  53.9 1.5 %collective-permute-start.18 = (f32[16,2176]{1,0:T(8,128)S(1)}, f32[16,2176]{1,0:T(8,128)S(1)}, u32[]{:S(2)}, u32[]{:S(2)}) collective-permute-start(f32[16,2176]{1,0:T(8,128)S(1)} %get-tuple-element.102), channel_id=1, source_target_pairs={{0,8},{8,0},{16,24},{24,16},{1,9},{9,1},{17,25},{25,17},{2,10},{10... | collective-permute-start | bytes 417800 | tf_op jit(solution)/shard_map/ppermute | solution.py:243
  55.4 0.8 %collective-permute-start.19 = (f32[16,2176]{1,0:T(8,128)S(1)}, f32[16,2176]{1,0:T(8,128)S(1)}, u32[]{:S(2)}, u32[]{:S(2)}) collective-permute-start(f32[16,2176]{1,0:T(8,128)S(1)} %get-tuple-element.103), channel_id=1, source_target_pairs={{0,16},{8,24},{16,0},{24,8},{1,17},{9,25},{17,1},{25,9},{2,18},{10... | collective-permute-start | bytes 417800 | tf_op jit(solution)/shard_map/ppermute | solution.py:243
  56.2 1.3 %collective-permute-start.20 = (f32[16,2176]{1,0:T(8,128)S(1)}, f32[16,2176]{1,0:T(8,128)S(1)}, u32[]{:S(2)}, u32[]{:S(2)}) collective-permute-start(f32[16,2176]{1,0:T(8,128)S(1)} %get-tuple-element.104), channel_id=1, source_target_pairs={{0,24},{8,16},{16,8},{24,0},{1,25},{9,17},{17,9},{25,1},{2,26},{10... | collective-permute-start | bytes 417800 | tf_op jit(solution)/shard_map/ppermute | solution.py:243
  57.4 0.0 collective-permute-done.21.refs_8_
  57.4 0.0 collective-permute-done.22.refs_9_
  57.4 4.8 %input_grad.1 = bf16[128,8192]{1,0:T(8,128)(2,1)} custom-call(bf16[128,512]{1,0:T(8,128)(2,1)S(1)} %get-tuple-element.105.pre_low, f32[128,16]{1,0:T(8,128)S(1)} %get-tuple-element.106.low_grad, bf16[32,8192]{1,0:T(8,128)(2,1)S(1)} %get-tuple-element.107.split, bf16[1024,512]{1,0:T(8,128)(2,1)S(1)} %copy-done.2, ...), custom_call_target="tpu_custom_call" | custom-call | tf_op jit(solution)/shard_map/input_grad/pallas_call | solution.py:33
  62.2 0.0 collective-permute-done.18.refs_1_
  62.2 1.6 %collective-permute-done.19.refs_2_ = f32[16,2176]{1,0:T(8,128)S(1)} collective-permute-done((f32[16,2176]{1,0:T(8,128)S(1)}, f32[16,2176]{1,0:T(8,128)S(1)}, u32[]{:S(2)}, u32[]{:S(2)}) %collective-permute-start.19) | collective-permute-done | bytes 139296 | tf_op jit(solution)/shard_map/ppermute | solution.py:243
  63.8 0.0 collective-permute-done.20.refs_3_
  63.8 0.9 %grad_sum.1 = (f32[3,16,2048]{2,1,0:T(8,128)}, f32[3,16,128]{2,1,0:T(8,128)}) custom-call(f32[4,128]{1,0:T(4,128)S(1)} %get-tuple-element.78.told, f32[16,2176]{1,0:T(8,128)S(1)} %get-tuple-element.112.refs_0_, f32[16,2176]{1,0:T(8,128)S(1)} %collective-permute-done.18.refs_1_, f32[16,2176]{1,0:T(8,128)S(1)} %collective-permute-done.19.refs_2_, ...), custom_call_target="tpu_custom_call" | custom-call | tf_op jit(solution)/shard_map/grad_sum/pallas_call | solution.py:33
  (13 shorter events, 0.2 us)
Async XLA Ops:
  0.6 21.4 %copy-start = (bf16[128,8192]{1,0:T(8,128)(2,1)S(1)}, bf16[128,8192]{1,0:T(8,128)(2,1)}, u32[]{:S(2)}) copy-start(bf16[128,8192]{1,0:T(8,128)(2,1)} %refs_0_.8) | copy-start | bytes 6291460
  0.6 1.4 %copy-start.1 = (bf16[1024,512]{1,0:T(8,128)(2,1)S(1)}, bf16[1024,512]{1,0:T(8,128)(2,1)}, u32[]{:S(2)}) copy-start(bf16[1024,512]{1,0:T(8,128)(2,1)} %refs_0_.9) | copy-start | bytes 3145732
  2.0 20.1 %copy-start.2 = (bf16[1024,512]{1,0:T(8,128)(2,1)S(1)}, bf16[1024,512]{1,0:T(8,128)(2,1)}, u32[]{:S(2)}) copy-start(bf16[1024,512]{1,0:T(8,128)(2,1)} %refs_0_.9) | copy-start | bytes 3145732
  2.0 14.9 %collective-permute-start.4 = (bf16[256,512]{1,0:T(8,128)(2,1)S(1)}, bf16[256,512]{1,0:T(8,128)(2,1)S(1)}, u32[]{:S(2)}, u32[]{:S(2)}) collective-permute-start(bf16[256,512]{1,0:T(8,128)(2,1)S(1)} %near.1), channel_id=1, source_target_pairs={{0,2},{1,3},{2,0},{3,1},{4,6},{5,7},{6,4},{7,5},{8,10},{9,11},{10,... | collective-permute-start | bytes 786440 | tf_op jit(solution)/shard_map/ppermute | solution.py:243
  5.1 14.3 %collective-permute-start.3 = (bf16[256,512]{1,0:T(8,128)(2,1)S(1)}, bf16[256,512]{1,0:T(8,128)(2,1)S(1)}, u32[]{:S(2)}, u32[]{:S(2)}) collective-permute-start(bf16[256,512]{1,0:T(8,128)(2,1)S(1)} %near.1), channel_id=1, source_target_pairs={{0,4},{1,5},{2,6},{3,7},{4,0},{5,1},{6,2},{7,3},{8,12},{9,13},{10,... | collective-permute-start | bytes 786440 | tf_op jit(solution)/shard_map/ppermute | solution.py:243
  8.4 6.0 %collective-permute-start.2 = (f32[1,128]{1,0:T(1,128)S(1)}, f32[1,128]{1,0:T(1,128)S(1)}, u32[]{:S(2)}, u32[]{:S(2)}) collective-permute-start(f32[1,128]{1,0:T(1,128)S(1)} %info.1.refs_0_), channel_id=1, source_target_pairs={{0,24},{8,16},{16,8},{24,0},{1,25},{9,17},{17,9},{25,1},{2,26},{10... | collective-permute-start | bytes 1544 | tf_op jit(solution)/shard_map/ppermute | solution.py:243
  10.9 3.5 %collective-permute-start.1 = (f32[1,128]{1,0:T(1,128)S(1)}, f32[1,128]{1,0:T(1,128)S(1)}, u32[]{:S(2)}, u32[]{:S(2)}) collective-permute-start(f32[1,128]{1,0:T(1,128)S(1)} %info.1.refs_0_), channel_id=1, source_target_pairs={{0,16},{8,24},{16,0},{24,8},{1,17},{9,25},{17,1},{25,9},{2,18},{10... | collective-permute-start | bytes 1544 | tf_op jit(solution)/shard_map/ppermute | solution.py:243
  11.4 3.5 %collective-permute-start = (f32[1,128]{1,0:T(1,128)S(1)}, f32[1,128]{1,0:T(1,128)S(1)}, u32[]{:S(2)}, u32[]{:S(2)}) collective-permute-start(f32[1,128]{1,0:T(1,128)S(1)} %info.1.refs_0_), channel_id=1, source_target_pairs={{0,8},{8,0},{16,24},{24,16},{1,9},{9,1},{17,25},{25,17},{2,10},{10... | collective-permute-start | bytes 1544 | tf_op jit(solution)/shard_map/ppermute | solution.py:243
  12.6 1.0 %copy-start.3 = (f32[3,2048,16]{1,2,0:T(8,128)S(1)}, f32[3,2048,16]{1,2,0:T(8,128)}, u32[]{:S(2)}) copy-start(f32[3,2048,16]{1,2,0:T(8,128)} %param.10) | copy-start | bytes 1179652
  13.6 0.7 %copy-start.5 = (f32[3,16,128]{2,1,0:T(8,128)S(1)}, f32[3,16,128]{2,1,0:T(8,128)}, u32[]{:S(2)}) copy-start(f32[3,16,128]{2,1,0:T(8,128)} %up.1) | copy-start | bytes 73732
  15.2 6.8 %collective-permute-start.7 = (f32[32,2304]{1,0:T(8,128)S(1)}, f32[32,2304]{1,0:T(8,128)S(1)}, u32[]{:S(2)}, u32[]{:S(2)}) collective-permute-start(f32[32,2304]{1,0:T(8,128)S(1)} %get-tuple-element.73), channel_id=1, source_target_pairs={{0,8},{1,17},{2,10},{3,19},{4,12},{5,21},{6,14},{7,23},{8,0},{9,25... | collective-permute-start | bytes 884744 | tf_op jit(solution)/shard_map/ppermute | solution.py:274
  19.5 2.5 %collective-permute-start.5 = (bf16[256,512]{1,0:T(8,128)(2,1)S(1)}, bf16[256,512]{1,0:T(8,128)(2,1)S(1)}, u32[]{:S(2)}, u32[]{:S(2)}) collective-permute-start(bf16[256,512]{1,0:T(8,128)(2,1)S(1)} %collective-permute-done.4.refs_0_), channel_id=1, source_target_pairs={{0,1},{1,0},{2,3},{3,2},{4,5},{5,4},{6,7},{7,6},{8,9},{9,8},{10,11... | collective-permute-start | bytes 786440 | tf_op jit(solution)/shard_map/ppermute | solution.py:243
  19.5 2.5 %collective-permute-start.6 = (bf16[256,512]{1,0:T(8,128)(2,1)S(1)}, bf16[256,512]{1,0:T(8,128)(2,1)S(1)}, u32[]{:S(2)}, u32[]{:S(2)}) collective-permute-start(bf16[256,512]{1,0:T(8,128)(2,1)S(1)} %collective-permute-done.3.refs_2_), channel_id=1, source_target_pairs={{0,1},{1,0},{2,3},{3,2},{4,5},{5,4},{6,7},{7,6},{8,9},{9,8},{10,11... | collective-permute-start | bytes 786440 | tf_op jit(solution)/shard_map/ppermute | solution.py:243
  22.0 10.1 %collective-permute-start.11 = (bf16[128,8192]{1,0:T(8,128)(2,1)S(1)}, bf16[128,8192]{1,0:T(8,128)(2,1)S(1)}, u32[]{:S(2)}, u32[]{:S(2)}) collective-permute-start(bf16[128,8192]{1,0:T(8,128)(2,1)S(1)} %copy-done), channel_id=1, source_target_pairs={{0,1},{1,0},{2,3},{3,2},{4,5},{5,4},{6,7},{7,6},{8,9},{9,8},{10,11... | collective-permute-start | bytes 6291464 | tf_op jit(solution)/shard_map/ppermute | solution.py:243
  22.1 10.0 %collective-permute-start.10 = (bf16[1024,512]{1,0:T(8,128)(2,1)S(1)}, bf16[1024,512]{1,0:T(8,128)(2,1)S(1)}, u32[]{:S(2)}, u32[]{:S(2)}) collective-permute-start(bf16[1024,512]{1,0:T(8,128)(2,1)S(1)} %copy-done.2), channel_id=1, source_target_pairs={{0,1},{1,0},{2,3},{3,2},{4,5},{5,4},{6,7},{7,6},{8,9},{9,8},{10,11... | collective-permute-start | bytes 3145736 | tf_op jit(solution)/shard_map/ppermute | solution.py:243
  22.6 14.8 %collective-permute-start.12 = (bf16[1024,512]{1,0:T(8,128)(2,1)S(1)}, bf16[1024,512]{1,0:T(8,128)(2,1)S(1)}, u32[]{:S(2)}, u32[]{:S(2)}) collective-permute-start(bf16[1024,512]{1,0:T(8,128)(2,1)S(1)} %join.3.refs_2_), channel_id=1, source_target_pairs={{0,8},{1,17},{2,10},{3,19},{4,12},{5,21},{6,14},{7,23},{8,0},{9,25... | collective-permute-start | bytes 3145736 | tf_op jit(solution)/shard_map/ppermute | solution.py:274
  23.6 8.6 %collective-permute-start.9 = (bf16[256,512]{1,0:T(8,128)(2,1)S(1)}, bf16[256,512]{1,0:T(8,128)(2,1)S(1)}, u32[]{:S(2)}, u32[]{:S(2)}) collective-permute-start(bf16[256,512]{1,0:T(8,128)(2,1)S(1)} %collective-permute-done.3.refs_2_), channel_id=1, source_target_pairs={{0,2},{1,3},{2,0},{3,1},{4,6},{5,7},{6,4},{7,5},{8,10},{9,11},{10,... | collective-permute-start | bytes 786440 | tf_op jit(solution)/shard_map/ppermute | solution.py:243
  32.2 1.5 %collective-permute-start.13 = (bf16[256,512]{1,0:T(8,128)(2,1)S(1)}, bf16[256,512]{1,0:T(8,128)(2,1)S(1)}, u32[]{:S(2)}, u32[]{:S(2)}) collective-permute-start(bf16[256,512]{1,0:T(8,128)(2,1)S(1)} %collective-permute-done.9.refs_0_), channel_id=1, source_target_pairs={{0,1},{1,0},{2,3},{3,2},{4,5},{5,4},{6,7},{7,6},{8,9},{9,8},{10,11... | collective-permute-start | bytes 786440 | tf_op jit(solution)/shard_map/ppermute | solution.py:243
  32.2 16.5 %collective-permute-start.16 = (bf16[512,512]{1,0:T(8,128)(2,1)S(1)}, bf16[512,512]{1,0:T(8,128)(2,1)S(1)}, u32[]{:S(2)}, u32[]{:S(2)}) collective-permute-start(bf16[512,512]{1,0:T(8,128)(2,1)S(1)} %far.1), channel_id=1, source_target_pairs={{0,2},{1,7},{2,0},{3,5},{4,6},{5,3},{6,4},{7,1},{8,10},{9,15},{10,... | collective-permute-start | bytes 1572872 | tf_op jit(solution)/shard_map/ppermute | solution.py:274
  33.7 15.0 %collective-permute-start.14 = (bf16[512,512]{1,0:T(8,128)(2,1)S(1)}, bf16[512,512]{1,0:T(8,128)(2,1)S(1)}, u32[]{:S(2)}, u32[]{:S(2)}) collective-permute-start(bf16[512,512]{1,0:T(8,128)(2,1)S(1)} %join.4.refs_3_), channel_id=1, source_target_pairs={{0,8},{1,17},{2,10},{3,19},{4,12},{5,21},{6,14},{7,23},{8,0},{9,25... | collective-permute-start | bytes 1572872 | tf_op jit(solution)/shard_map/ppermute | solution.py:274
  34.8 10.0 %collective-permute-start.8 = (f32[32,2304]{1,0:T(8,128)S(1)}, f32[32,2304]{1,0:T(8,128)S(1)}, u32[]{:S(2)}, u32[]{:S(2)}) collective-permute-start(f32[32,2304]{1,0:T(8,128)S(1)} %pass_on.1), channel_id=1, source_target_pairs={{0,16},{1,9},{2,18},{3,11},{4,20},{5,13},{6,22},{7,15},{8,24},{9,1... | collective-permute-start | bytes 884744 | tf_op jit(solution)/shard_map/ppermute | solution.py:274
  37.4 11.3 %collective-permute-start.15 = (bf16[256,512]{1,0:T(8,128)(2,1)S(1)}, bf16[256,512]{1,0:T(8,128)(2,1)S(1)}, u32[]{:S(2)}, u32[]{:S(2)}) collective-permute-start(bf16[256,512]{1,0:T(8,128)(2,1)S(1)} %take.1), channel_id=1, source_target_pairs={{0,16},{1,9},{2,18},{3,11},{4,20},{5,13},{6,22},{7,15},{8,24},{9,1... | collective-permute-start | bytes 786440 | tf_op jit(solution)/shard_map/ppermute | solution.py:274
  49.2 2.1 %copy-start.4 = (bf16[128,512]{1,0:T(8,128)(2,1)S(1)}, bf16[128,512]{1,0:T(8,128)(2,1)}, u32[]{:S(2)}) copy-start(bf16[128,512]{1,0:T(8,128)(2,1)} %refs_3_.1) | copy-start | bytes 393220
  49.3 2.1 %copy-start.6 = (f32[128]{0:T(128)S(1)}, f32[128]{0:T(128)}, u32[]{:S(2)}) copy-start(f32[128]{0:T(128)} %param.12) | copy-start | bytes 1540
  49.3 1.6 %collective-permute-start.17 = (f32[128,512]{1,0:T(8,128)S(1)}, f32[128,512]{1,0:T(8,128)S(1)}, u32[]{:S(2)}, u32[]{:S(2)}) collective-permute-start(f32[128,512]{1,0:T(8,128)S(1)} %get-tuple-element.97), channel_id=1, source_target_pairs={{0,1},{1,0},{2,3},{3,2},{4,5},{5,4},{6,7},{7,6},{8,9},{9,8},{10,11... | collective-permute-start | bytes 786440 | tf_op jit(solution)/shard_map/ppermute | solution.py:243
  50.9 6.6 %collective-permute-start.22 = (bf16[1280,512]{1,0:T(8,128)(2,1)S(1)}, bf16[1280,512]{1,0:T(8,128)(2,1)S(1)}, u32[]{:S(2)}, u32[]{:S(2)}) collective-permute-start(bf16[1280,512]{1,0:T(8,128)(2,1)S(1)} %join.5), channel_id=1, source_target_pairs={{0,1},{1,0},{2,3},{3,2},{4,5},{5,4},{6,7},{7,6},{8,9},{9,8},{10,11... | collective-permute-start | bytes 3932168 | tf_op jit(solution)/shard_map/ppermute | solution.py:243
  51.0 6.4 %collective-permute-start.21 = (bf16[1024,512]{1,0:T(8,128)(2,1)S(1)}, bf16[1024,512]{1,0:T(8,128)(2,1)S(1)}, u32[]{:S(2)}, u32[]{:S(2)}) collective-permute-start(bf16[1024,512]{1,0:T(8,128)(2,1)S(1)} %collective-permute-done.12.value.refs_4_), channel_id=1, source_target_pairs={{0,1},{1,0},{2,3},{3,2},{4,5},{5,4},{6,7},{7,6},{8,9},{9,8},{10,11... | collective-permute-start | bytes 3145736 | tf_op jit(solution)/shard_map/ppermute | solution.py:243
  53.9 8.3 %collective-permute-start.18 = (f32[16,2176]{1,0:T(8,128)S(1)}, f32[16,2176]{1,0:T(8,128)S(1)}, u32[]{:S(2)}, u32[]{:S(2)}) collective-permute-start(f32[16,2176]{1,0:T(8,128)S(1)} %get-tuple-element.102), channel_id=1, source_target_pairs={{0,8},{8,0},{16,24},{24,16},{1,9},{9,1},{17,25},{25,17},{2,10},{10... | collective-permute-start | bytes 417800 | tf_op jit(solution)/shard_map/ppermute | solution.py:243
  55.4 8.4 %collective-permute-start.19 = (f32[16,2176]{1,0:T(8,128)S(1)}, f32[16,2176]{1,0:T(8,128)S(1)}, u32[]{:S(2)}, u32[]{:S(2)}) collective-permute-start(f32[16,2176]{1,0:T(8,128)S(1)} %get-tuple-element.103), channel_id=1, source_target_pairs={{0,16},{8,24},{16,0},{24,8},{1,17},{9,25},{17,1},{25,9},{2,18},{10... | collective-permute-start | bytes 417800 | tf_op jit(solution)/shard_map/ppermute | solution.py:243
  56.2 7.7 %collective-permute-start.20 = (f32[16,2176]{1,0:T(8,128)S(1)}, f32[16,2176]{1,0:T(8,128)S(1)}, u32[]{:S(2)}, u32[]{:S(2)}) collective-permute-start(f32[16,2176]{1,0:T(8,128)S(1)} %get-tuple-element.104), channel_id=1, source_target_pairs={{0,24},{8,16},{16,8},{24,0},{1,25},{9,17},{17,9},{25,1},{2,26},{10... | collective-permute-start | bytes 417800 | tf_op jit(solution)/shard_map/ppermute | solution.py:243

commit v4 on v3

--- a/solution.py
+++ b/solution.py
@@ -29,12 +29,13 @@
     return high, low
 
 
-def call(kernel, outs, ins, name, moved=0):
+def call(kernel, outs, ins, name, moved=0, out=vmem, scratch=()):
     return pl.pallas_call(
         kernel,
         out_shape=[jax.ShapeDtypeStruct(shape, dtype) for shape, dtype in outs],
         in_specs=[spec for spec, _ in ins],
-        out_specs=[vmem] * len(outs),
+        out_specs=[out] * len(outs),
+        scratch_shapes=scratch,
         compiler_params=pltpu.CompilerParams(vmem_limit_bytes=VMEM_LIMIT),
         cost_estimate=pl.CostEstimate(flops=0, bytes_accessed=moved, transcendentals=0),
         name=name,
@@ -184,14 +185,22 @@
         heads.append(inverse * (scaled - normed * along))
     pre = jnp.concatenate(heads, axis=-1)
     pre_low[...] = pre.astype(BF16)
-    grad = adapter_scale * lax.dot_general(
-        pre, up[...], (((1,), (1,)), ((), ())), precision=HIGHEST, preferred_element_type=F32
-    )
+    (pre_high, pre_rest), (up_high, up_rest), (low_high, low_rest) = map(split_two, (pre, up[...], low_rank[...]))
+    rank = up.shape[0]
+    both = lax.dot_general(
+        jnp.concatenate([pre_high, pre_rest], axis=0),
+        jnp.concatenate([up_high, up_rest], axis=0),
+        (((1,), (1,)), ((), ())),
+        preferred_element_type=F32,
+    )
+    grad = adapter_scale * (both[:rows, :rank] + both[:rows, rank:] + both[rows:, :rank])
     low_grad[...] = grad
-    up_grad = adapter_scale * lax.dot_general(
-        low_rank[...], pre, (((0,), (0,)), ((), ())), precision=HIGHEST, preferred_element_type=F32
-    )
-    rank = grad.shape[1]
+    across = (((0,), (0,)), ((), ()))
+    both = lax.dot_general(
+        jnp.concatenate([low_high, low_rest], axis=-1), pre_high, across, preferred_element_type=F32
+    )
+    rest = lax.dot_general(low_high, pre_rest, across, preferred_element_type=F32)
+    up_grad = adapter_scale * (both[:rank] + both[rank:] + rest)
     split = jnp.concatenate(split_two(grad), axis=-1)
     down_width, up_width = tokens.shape[1] // parts, width // parts
     for partner, out in enumerate(grads):
@@ -208,19 +217,23 @@
 
 def input_grad_kernel(pieces, sizes, pre_low, low_grad, split, *refs):
     place = position()
-    buffers, out = refs[:-1], refs[-1]
+    buffers, (out, held, copied) = refs[:-3], refs[-3:]
     rank = low_grad.shape[1]
     high, low = split_two(low_grad[...])
     left = jnp.concatenate([high, high, low], axis=-1)
-    for piece in pieces:
+    turned = pre_low[...].T
+    copies = []
+    for index, piece in enumerate(pieces):
         columns = pl.ds(column_of(place, piece, *sizes), piece["rows"])
         rows = pl.ds(piece["first"], piece["rows"])
-        value = lax.dot_general(
-            pre_low[...], buffers[piece["buffer"]][rows, :], (((1,), (1,)), ((), ())), preferred_element_type=F32
-        )
+        value = jnp.dot(buffers[piece["buffer"]][rows, :], turned, preferred_element_type=F32).T
         right = jnp.concatenate([split[:, columns], split[:rank, columns]], axis=0)
         value = value + jnp.dot(left, right, preferred_element_type=F32)
-        out[:, columns] = value.astype(BF16)
+        held[:, columns] = value.astype(BF16)
+        copies.append(pltpu.make_async_copy(held.at[:, columns], out.at[:, columns], copied.at[index]))
+        copies[-1].start()
+    for copy in copies:
+        copy.wait()
 
 
 def sum_kernel(told, *refs):
@@ -380,7 +393,8 @@
     keys, pre_low, low_grad, *grads = call(
         functools.partial(middle_kernel, parts),
         [((rows, key_width), BF16), ((rows, key_width), BF16), ((rows, rank), F32)]
-        + [((rank, down_width + up_width), F32)] * parts,
+        + [((rank, down_width + up_width), F32)]
+        + [((rank, down_width + up_width), BF16)] * (parts - 1),
         [
             (vmem, value)
             for value in (told, tokens, total, received, cotangent, key_norm_gain.reshape(1, HD), low_rank, up)
@@ -398,6 +412,8 @@
         [((rows, model_width), BF16)],
         [(vmem, pre_low), (vmem, low_grad), (vmem, split)] + [(vmem, value) for value in buffers],
         "input_grad",
+        out=hbm,
+        scratch=[pltpu.VMEM((rows, model_width), BF16), pltpu.SemaphoreType.DMA((len(pieces),))],
     )
     received, input_grad = lax.optimization_barrier((received, input_grad))
     down_sum, up_sum = call(

time: 65 us -> 62.3 us (0.958)
  waiting for transfers between devices: 27.1 us -> 25.5 us
  Pallas kernels: 11.8 us -> 10.7 us
    ppermute x17, waiting for transfers between devices: 15.9 us -> 14.2 us  [flip(): return lax.ppermute(value, axis, [(i, i ^ bits) for i in range(size)])]
    pallas_call x16, Pallas kernels: 11.8 us -> 10.7 us  [call(): pl.pallas_call(kernel, out_shape=[jax.ShapeDtypeStruct(shape, dtype) for...]
  transfers between devices with their start and end apart: 23 -> 23, of which waited for: 11 -> 10; matrix products, arithmetic and copies ran while one was open for 0% -> 0% of each run, Pallas kernels for 16% -> 15%
where the time goes in v4:
time: 62.3 us; the launch traced here: 62 us
  waiting for transfers between devices  25.5 us (41%)
  starting transfers between devices  20.6 us (33%)
  Pallas kernels  10.7 us (17%)
  local copies, waits for them, and re-layouts  3.13 us (5%)
  between operations  2.12 us (3%)
    ppermute x17, starting transfers between devices, flip(): return lax.ppermute(value, axis, [(i, i ^ bits) for i in range(size)])  14.9 us
    ppermute x17, waiting for transfers between devices, flip(): return lax.ppermute(value, axis, [(i, i ^ bits) for i in range(size)])  14.2 us
    ppermute x6, waiting for transfers between devices, over_split(): return lax.ppermute(value, ('dp', 'fsdp'), pairs)  11.2 us
    pallas_call x16, Pallas kernels, call(): pl.pallas_call(kernel, out_shape=[jax.ShapeDtypeStruct(shape, dtype) for...  10.7 us
    ppermute x6, starting transfers between devices, over_split(): return lax.ppermute(value, ('dp', 'fsdp'), pairs)  5.7 us
    unnamed x14, local copies, waits for them, and re-layouts  3.11 us
  transfers between devices with their start and end apart: 23, of which 10 were waited for; matrix products, arithmetic and copies ran while one was open for 0% of the time, Pallas kernels for 15%

profile of v4, /device:TPU:0, one launch (start us, length us, event | category | flops | bytes accessed | tf_op | source)
XLA Modules:
  0.0 62.0 jit_solution(184050792894938855)
XLA Ops:
  0.7 1.4 %copy-done.1 = bf16[1024,512]{1,0:T(8,128)(2,1)S(1)} copy-done((bf16[1024,512]{1,0:T(8,128)(2,1)S(1)}, bf16[1024,512]{1,0:T(8,128)(2,1)}, u32[]{:S(2)}) %copy-start.1) | copy-done | bytes 1048600
  2.0 3.1 %collective-permute-start.4 = (bf16[256,512]{1,0:T(8,128)(2,1)S(1)}, bf16[256,512]{1,0:T(8,128)(2,1)S(1)}, u32[]{:S(2)}, u32[]{:S(2)}) collective-permute-start(bf16[256,512]{1,0:T(8,128)(2,1)S(1)} %near.1), channel_id=1, source_target_pairs={{0,2},{1,3},{2,0},{3,1},{4,6},{5,7},{6,4},{7,5},{8,10},{9,11},{10,... | collective-permute-start | bytes 786440 | tf_op jit(solution)/shard_map/ppermute | solution.py:256
  5.1 2.6 %collective-permute-start.3 = (bf16[256,512]{1,0:T(8,128)(2,1)S(1)}, bf16[256,512]{1,0:T(8,128)(2,1)S(1)}, u32[]{:S(2)}, u32[]{:S(2)}) collective-permute-start(bf16[256,512]{1,0:T(8,128)(2,1)S(1)} %near.1), channel_id=1, source_target_pairs={{0,4},{1,5},{2,6},{3,7},{4,0},{5,1},{6,2},{7,3},{8,12},{9,13},{10,... | collective-permute-start | bytes 786440 | tf_op jit(solution)/shard_map/ppermute | solution.py:256
  8.4 0.1 info.1.refs_0_
  8.4 2.4 %collective-permute-start.2 = (f32[1,128]{1,0:T(1,128)S(1)}, f32[1,128]{1,0:T(1,128)S(1)}, u32[]{:S(2)}, u32[]{:S(2)}) collective-permute-start(f32[1,128]{1,0:T(1,128)S(1)} %info.1.refs_0_), channel_id=1, source_target_pairs={{0,24},{8,16},{16,8},{24,0},{1,25},{9,17},{17,9},{25,1},{2,26},{10... | collective-permute-start | bytes 1544 | tf_op jit(solution)/shard_map/ppermute | solution.py:256
  10.9 0.5 collective-permute-start.1
  11.4 0.5 collective-permute-start
  12.6 0.0 copy-start.3
  12.6 1.0 %copy-done.3 = f32[3,2048,16]{1,2,0:T(8,128)S(1)} copy-done((f32[3,2048,16]{1,2,0:T(8,128)S(1)}, f32[3,2048,16]{1,2,0:T(8,128)}, u32[]{:S(2)}) %copy-start.3) | copy-done | bytes 393240
  13.6 0.7 %copy-done.5 = f32[3,16,128]{2,1,0:T(8,128)S(1)} copy-done((f32[3,16,128]{2,1,0:T(8,128)S(1)}, f32[3,16,128]{2,1,0:T(8,128)}, u32[]{:S(2)}) %copy-start.5) | copy-done | bytes 24600
  14.3 0.1 hold.1
  14.4 0.0 collective-permute-done.2.refs_3_
  14.4 0.0 collective-permute-done.1.refs_2_
  14.4 0.5 collective-permute-done.refs_1_
  14.9 0.2 adapter_messages.1
  15.2 1.0 %collective-permute-start.7 = (f32[32,2304]{1,0:T(8,128)S(1)}, f32[32,2304]{1,0:T(8,128)S(1)}, u32[]{:S(2)}, u32[]{:S(2)}) collective-permute-start(f32[32,2304]{1,0:T(8,128)S(1)} %get-tuple-element.73), channel_id=1, source_target_pairs={{0,8},{1,17},{2,10},{3,19},{4,12},{5,21},{6,14},{7,23},{8,0},{9,25... | collective-permute-start | bytes 884744 | tf_op jit(solution)/shard_map/ppermute | solution.py:287
  16.2 0.7 %collective-permute-done.4.refs_0_ = bf16[256,512]{1,0:T(8,128)(2,1)S(1)} collective-permute-done((bf16[256,512]{1,0:T(8,128)(2,1)S(1)}, bf16[256,512]{1,0:T(8,128)(2,1)S(1)}, u32[]{:S(2)}, u32[]{:S(2)}) %collective-permute-start.4) | collective-permute-done | bytes 262176 | tf_op jit(solution)/shard_map/ppermute | solution.py:256
  16.9 2.5 %collective-permute-done.3.refs_2_ = bf16[256,512]{1,0:T(8,128)(2,1)S(1)} collective-permute-done((bf16[256,512]{1,0:T(8,128)(2,1)S(1)}, bf16[256,512]{1,0:T(8,128)(2,1)S(1)}, u32[]{:S(2)}, u32[]{:S(2)}) %collective-permute-start.3) | collective-permute-done | bytes 262176 | tf_op jit(solution)/shard_map/ppermute | solution.py:256
  19.5 0.0 collective-permute-start.5
  19.5 0.5 collective-permute-start.6
  20.0 2.0 %collective-permute-done.7.received.sooner = f32[32,2304]{1,0:T(8,128)S(1)} collective-permute-done((f32[32,2304]{1,0:T(8,128)S(1)}, f32[32,2304]{1,0:T(8,128)S(1)}, u32[]{:S(2)}, u32[]{:S(2)}) %collective-permute-start.7) | collective-permute-done | bytes 294944 | tf_op jit(solution)/shard_map/ppermute | solution.py:287
  22.0 0.0 collective-permute-done.5.refs_1_
  22.0 0.0 collective-permute-done.6.refs_3_
  22.0 0.1 join.3.refs_2_
  22.0 0.1 collective-permute-start.11
  22.1 0.0 copy-done.2
  22.1 0.5 collective-permute-start.10
  22.6 1.0 %collective-permute-start.12 = (bf16[1024,512]{1,0:T(8,128)(2,1)S(1)}, bf16[1024,512]{1,0:T(8,128)(2,1)S(1)}, u32[]{:S(2)}, u32[]{:S(2)}) collective-permute-start(bf16[1024,512]{1,0:T(8,128)(2,1)S(1)} %join.3.refs_2_), channel_id=1, source_target_pairs={{0,8},{1,17},{2,10},{3,19},{4,12},{5,21},{6,14},{7,23},{8,0},{9,25... | collective-permute-start | bytes 3145736 | tf_op jit(solution)/shard_map/ppermute | solution.py:287
  23.6 0.5 collective-permute-start.9
  24.1 8.1 %collective-permute-done.9.refs_0_ = bf16[256,512]{1,0:T(8,128)(2,1)S(1)} collective-permute-done((bf16[256,512]{1,0:T(8,128)(2,1)S(1)}, bf16[256,512]{1,0:T(8,128)(2,1)S(1)}, u32[]{:S(2)}, u32[]{:S(2)}) %collective-permute-start.9) | collective-permute-done | bytes 262176 | tf_op jit(solution)/shard_map/ppermute | solution.py:256
  32.2 0.0 collective-permute-done.10.refs_1_
  32.2 0.0 collective-permute-done.11.tokens_pair
  32.2 0.0 collective-permute-start.13
  32.2 0.5 collective-permute-start.16
  32.7 1.0 %collective-permute-done.13.refs_1_ = bf16[256,512]{1,0:T(8,128)(2,1)S(1)} collective-permute-done((bf16[256,512]{1,0:T(8,128)(2,1)S(1)}, bf16[256,512]{1,0:T(8,128)(2,1)S(1)}, u32[]{:S(2)}, u32[]{:S(2)}) %collective-permute-start.13) | collective-permute-done | bytes 262176 | tf_op jit(solution)/shard_map/ppermute | solution.py:256
  33.7 1.0 %collective-permute-start.14 = (bf16[512,512]{1,0:T(8,128)(2,1)S(1)}, bf16[512,512]{1,0:T(8,128)(2,1)S(1)}, u32[]{:S(2)}, u32[]{:S(2)}) collective-permute-start(bf16[512,512]{1,0:T(8,128)(2,1)S(1)} %join.4.refs_3_), channel_id=1, source_target_pairs={{0,8},{1,17},{2,10},{3,19},{4,12},{5,21},{6,14},{7,23},{8,0},{9,25... | collective-permute-start | bytes 1572872 | tf_op jit(solution)/shard_map/ppermute | solution.py:287
  34.8 0.6 collective-permute-start.8
  35.4 2.0 %collective-permute-done.12.value.refs_4_ = bf16[1024,512]{1,0:T(8,128)(2,1)S(1)} collective-permute-done((bf16[1024,512]{1,0:T(8,128)(2,1)S(1)}, bf16[1024,512]{1,0:T(8,128)(2,1)S(1)}, u32[]{:S(2)}, u32[]{:S(2)}) %collective-permute-start.12) | collective-permute-done | bytes 1048608 | tf_op jit(solution)/shard_map/ppermute | solution.py:287
  37.4 1.6 %collective-permute-start.15 = (bf16[256,512]{1,0:T(8,128)(2,1)S(1)}, bf16[256,512]{1,0:T(8,128)(2,1)S(1)}, u32[]{:S(2)}, u32[]{:S(2)}) collective-permute-start(bf16[256,512]{1,0:T(8,128)(2,1)S(1)} %take.1), channel_id=1, source_target_pairs={{0,16},{1,9},{2,18},{3,11},{4,20},{5,13},{6,22},{7,15},{8,24},{9,1... | collective-permute-start | bytes 786440 | tf_op jit(solution)/shard_map/ppermute | solution.py:287
  39.0 5.8 %collective-permute-done.8.later = f32[32,2304]{1,0:T(8,128)S(1)} collective-permute-done((f32[32,2304]{1,0:T(8,128)S(1)}, f32[32,2304]{1,0:T(8,128)S(1)}, u32[]{:S(2)}, u32[]{:S(2)}) %collective-permute-start.8) | collective-permute-done | bytes 294944 | tf_op jit(solution)/shard_map/ppermute | solution.py:287
  44.8 1.5 %low_rank.1 = (bf16[32,8192]{1,0:T(8,128)(2,1)S(1)}, f32[16,512]{1,0:T(8,128)S(1)}, f32[128,16]{1,0:T(8,128)S(1)}, f32[128,512]{1,0:T(8,128)S(1)}, f32[4,128]{1,0:T(4,128)S(1)}) custom-call(bf16[128,8192]{1,0:T(8,128)(2,1)S(1)} %copy-done, f32[4,128]{1,0:T(4,128)S(1)} %get-tuple-element.71.slots, f32[16,2304]{1,0:T(8,128)S(1)} %get-tuple-element.72.own, ...), custom_call_target="tpu_custom_call" | custom-call | bytes 12582912 | tf_op jit(solution)/shard_map/low_rank/pallas_call | solution.py:33
  46.4 0.9 %base.2 = (f32[128,512]{1,0:T(8,128)S(1)}, f32[128,512]{1,0:T(8,128)S(1)}) custom-call(bf16[128,8192]{1,0:T(8,128)(2,1)S(1)} %copy-done, bf16[128,8192]{1,0:T(8,128)(2,1)S(1)} %collective-permute-done.11.tokens_pair, f32[128,512]{1,0:T(8,128)S(1)} %get-tuple-element.88.before, f32[128,512]{1,0:T(8,128)S(1)} %broadcast_in_dim.3.before_pair, ...), custom_call_target="tpu_custom_call" | custom-call | tf_op jit(solution)/shard_map/base/pallas_call | solution.py:33
  47.3 1.4 %collective-permute-done.15.refs_2_.refs_7_ = bf16[256,512]{1,0:T(8,128)(2,1)S(1)} collective-permute-done((bf16[256,512]{1,0:T(8,128)(2,1)S(1)}, bf16[256,512]{1,0:T(8,128)(2,1)S(1)}, u32[]{:S(2)}, u32[]{:S(2)}) %collective-permute-start.15) | collective-permute-done | bytes 262176 | tf_op jit(solution)/shard_map/ppermute | solution.py:287
  48.7 0.0 collective-permute-done.16.refs_1_.refs_6_
  48.7 0.0 collective-permute-done.14.refs_0_.refs_5_
  48.7 0.5 base.3
  49.2 0.0 copy-start.4
  49.3 0.0 copy-start.6
  49.3 0.2 collective-permute-start.17
  49.4 0.1 join.5
  49.5 1.3 %collective-permute-done.17.refs_2_ = f32[128,512]{1,0:T(8,128)S(1)} collective-permute-done((f32[128,512]{1,0:T(8,128)S(1)}, f32[128,512]{1,0:T(8,128)S(1)}, u32[]{:S(2)}, u32[]{:S(2)}) %collective-permute-start.17) | collective-permute-done | bytes 262176 | tf_op jit(solution)/shard_map/ppermute | solution.py:256
  50.9 0.1 collective-permute-start.22
  51.0 0.4 collective-permute-start.21
  51.4 2.3 %key_norm.1 = (bf16[128,512]{1,0:T(8,128)(2,1)}, bf16[128,512]{1,0:T(8,128)(2,1)S(1)}, f32[128,16]{1,0:T(8,128)S(1)}, f32[16,2176]{1,0:T(8,128)S(1)}, bf16[16,21...) custom-call(f32[4,128]{1,0:T(4,128)S(1)} %get-tuple-element.78.told, ...), custom_call_target="tpu_custom_call" | custom-call | tf_op jit(solution)/shard_map/key_norm/pallas_call | solution.py:33
  53.7 1.5 %collective-permute-start.18 = (bf16[16,2176]{1,0:T(8,128)(2,1)S(1)}, bf16[16,2176]{1,0:T(8,128)(2,1)S(1)}, u32[]{:S(2)}, u32[]{:S(2)}) collective-permute-start(bf16[16,2176]{1,0:T(8,128)(2,1)S(1)} %get-tuple-element.102), channel_id=1, source_target_pairs={{0,8},{8,0},{16,24},{24,16},{1,9},{9,1},{17,25},{25,17},{2,10},{10... | collective-permute-start | bytes 208904 | tf_op jit(solution)/shard_map/ppermute | solution.py:256
  55.1 0.8 %collective-permute-start.19 = (bf16[16,2176]{1,0:T(8,128)(2,1)S(1)}, bf16[16,2176]{1,0:T(8,128)(2,1)S(1)}, u32[]{:S(2)}, u32[]{:S(2)}) collective-permute-start(bf16[16,2176]{1,0:T(8,128)(2,1)S(1)} %get-tuple-element.103), channel_id=1, source_target_pairs={{0,16},{8,24},{16,0},{24,8},{1,17},{9,25},{17,1},{25,9},{2,18},{10... | collective-permute-start | bytes 208904 | tf_op jit(solution)/shard_map/ppermute | solution.py:256
  55.9 1.3 %collective-permute-start.20 = (bf16[16,2176]{1,0:T(8,128)(2,1)S(1)}, bf16[16,2176]{1,0:T(8,128)(2,1)S(1)}, u32[]{:S(2)}, u32[]{:S(2)}) collective-permute-start(bf16[16,2176]{1,0:T(8,128)(2,1)S(1)} %get-tuple-element.104), channel_id=1, source_target_pairs={{0,24},{8,16},{16,8},{24,0},{1,25},{9,17},{17,9},{25,1},{2,26},{10... | collective-permute-start | bytes 208904 | tf_op jit(solution)/shard_map/ppermute | solution.py:256
  57.2 0.0 collective-permute-done.21.refs_8_
  57.2 0.0 collective-permute-done.22.refs_9_
  57.2 3.9 %input_grad.1 = bf16[128,8192]{1,0:T(8,128)(2,1)} custom-call(bf16[128,512]{1,0:T(8,128)(2,1)S(1)} %get-tuple-element.105.pre_low, f32[128,16]{1,0:T(8,128)S(1)} %get-tuple-element.106.low_grad, bf16[32,8192]{1,0:T(8,128)(2,1)S(1)} %get-tuple-element.107.split, bf16[1024,512]{1,0:T(8,128)(2,1)S(1)} %copy-done.2, ...), custom_call_target="tpu_custom_call" | custom-call | tf_op jit(solution)/shard_map/input_grad/pallas_call | solution.py:33
  61.1 0.0 collective-permute-done.18.refs_1_
  61.1 0.0 collective-permute-done.19.refs_2_
  61.1 0.0 collective-permute-done.20.refs_3_
  61.1 0.9 %grad_sum.1 = (f32[3,16,2048]{2,1,0:T(8,128)}, f32[3,16,128]{2,1,0:T(8,128)}) custom-call(f32[4,128]{1,0:T(4,128)S(1)} %get-tuple-element.78.told, f32[16,2176]{1,0:T(8,128)S(1)} %get-tuple-element.112.refs_0_, bf16[16,2176]{1,0:T(8,128)(2,1)S(1)} %collective-permute-done.18.refs_1_, bf16[16,2176]{1,0:T(8,128)(2,1)S(1)} %collective-permute-done.19.refs_2_, ...), custom_call_target="tpu_custom_call" | custom-call | tf_op jit(solution)/shard_map/grad_sum/pallas_call | solution.py:33
  (13 shorter events, 0.2 us)
Async XLA Ops:
  0.6 21.4 %copy-start = (bf16[128,8192]{1,0:T(8,128)(2,1)S(1)}, bf16[128,8192]{1,0:T(8,128)(2,1)}, u32[]{:S(2)}) copy-start(bf16[128,8192]{1,0:T(8,128)(2,1)} %refs_0_.8) | copy-start | bytes 6291460
  0.6 1.4 %copy-start.1 = (bf16[1024,512]{1,0:T(8,128)(2,1)S(1)}, bf16[1024,512]{1,0:T(8,128)(2,1)}, u32[]{:S(2)}) copy-start(bf16[1024,512]{1,0:T(8,128)(2,1)} %refs_0_.9) | copy-start | bytes 3145732
  2.0 20.1 %copy-start.2 = (bf16[1024,512]{1,0:T(8,128)(2,1)S(1)}, bf16[1024,512]{1,0:T(8,128)(2,1)}, u32[]{:S(2)}) copy-start(bf16[1024,512]{1,0:T(8,128)(2,1)} %refs_0_.9) | copy-start | bytes 3145732
  2.0 14.9 %collective-permute-start.4 = (bf16[256,512]{1,0:T(8,128)(2,1)S(1)}, bf16[256,512]{1,0:T(8,128)(2,1)S(1)}, u32[]{:S(2)}, u32[]{:S(2)}) collective-permute-start(bf16[256,512]{1,0:T(8,128)(2,1)S(1)} %near.1), channel_id=1, source_target_pairs={{0,2},{1,3},{2,0},{3,1},{4,6},{5,7},{6,4},{7,5},{8,10},{9,11},{10,... | collective-permute-start | bytes 786440 | tf_op jit(solution)/shard_map/ppermute | solution.py:256
  5.1 14.3 %collective-permute-start.3 = (bf16[256,512]{1,0:T(8,128)(2,1)S(1)}, bf16[256,512]{1,0:T(8,128)(2,1)S(1)}, u32[]{:S(2)}, u32[]{:S(2)}) collective-permute-start(bf16[256,512]{1,0:T(8,128)(2,1)S(1)} %near.1), channel_id=1, source_target_pairs={{0,4},{1,5},{2,6},{3,7},{4,0},{5,1},{6,2},{7,3},{8,12},{9,13},{10,... | collective-permute-start | bytes 786440 | tf_op jit(solution)/shard_map/ppermute | solution.py:256
  8.4 6.0 %collective-permute-start.2 = (f32[1,128]{1,0:T(1,128)S(1)}, f32[1,128]{1,0:T(1,128)S(1)}, u32[]{:S(2)}, u32[]{:S(2)}) collective-permute-start(f32[1,128]{1,0:T(1,128)S(1)} %info.1.refs_0_), channel_id=1, source_target_pairs={{0,24},{8,16},{16,8},{24,0},{1,25},{9,17},{17,9},{25,1},{2,26},{10... | collective-permute-start | bytes 1544 | tf_op jit(solution)/shard_map/ppermute | solution.py:256
  10.9 3.5 %collective-permute-start.1 = (f32[1,128]{1,0:T(1,128)S(1)}, f32[1,128]{1,0:T(1,128)S(1)}, u32[]{:S(2)}, u32[]{:S(2)}) collective-permute-start(f32[1,128]{1,0:T(1,128)S(1)} %info.1.refs_0_), channel_id=1, source_target_pairs={{0,16},{8,24},{16,0},{24,8},{1,17},{9,25},{17,1},{25,9},{2,18},{10... | collective-permute-start | bytes 1544 | tf_op jit(solution)/shard_map/ppermute | solution.py:256
  11.4 3.5 %collective-permute-start = (f32[1,128]{1,0:T(1,128)S(1)}, f32[1,128]{1,0:T(1,128)S(1)}, u32[]{:S(2)}, u32[]{:S(2)}) collective-permute-start(f32[1,128]{1,0:T(1,128)S(1)} %info.1.refs_0_), channel_id=1, source_target_pairs={{0,8},{8,0},{16,24},{24,16},{1,9},{9,1},{17,25},{25,17},{2,10},{10... | collective-permute-start | bytes 1544 | tf_op jit(solution)/shard_map/ppermute | solution.py:256
  12.6 1.0 %copy-start.3 = (f32[3,2048,16]{1,2,0:T(8,128)S(1)}, f32[3,2048,16]{1,2,0:T(8,128)}, u32[]{:S(2)}) copy-start(f32[3,2048,16]{1,2,0:T(8,128)} %param.10) | copy-start | bytes 1179652
  13.6 0.7 %copy-start.5 = (f32[3,16,128]{2,1,0:T(8,128)S(1)}, f32[3,16,128]{2,1,0:T(8,128)}, u32[]{:S(2)}) copy-start(f32[3,16,128]{2,1,0:T(8,128)} %up.1) | copy-start | bytes 73732
  15.2 6.8 %collective-permute-start.7 = (f32[32,2304]{1,0:T(8,128)S(1)}, f32[32,2304]{1,0:T(8,128)S(1)}, u32[]{:S(2)}, u32[]{:S(2)}) collective-permute-start(f32[32,2304]{1,0:T(8,128)S(1)} %get-tuple-element.73), channel_id=1, source_target_pairs={{0,8},{1,17},{2,10},{3,19},{4,12},{5,21},{6,14},{7,23},{8,0},{9,25... | collective-permute-start | bytes 884744 | tf_op jit(solution)/shard_map/ppermute | solution.py:287
  19.5 2.5 %collective-permute-start.5 = (bf16[256,512]{1,0:T(8,128)(2,1)S(1)}, bf16[256,512]{1,0:T(8,128)(2,1)S(1)}, u32[]{:S(2)}, u32[]{:S(2)}) collective-permute-start(bf16[256,512]{1,0:T(8,128)(2,1)S(1)} %collective-permute-done.4.refs_0_), channel_id=1, source_target_pairs={{0,1},{1,0},{2,3},{3,2},{4,5},{5,4},{6,7},{7,6},{8,9},{9,8},{10,11... | collective-permute-start | bytes 786440 | tf_op jit(solution)/shard_map/ppermute | solution.py:256
  19.5 2.5 %collective-permute-start.6 = (bf16[256,512]{1,0:T(8,128)(2,1)S(1)}, bf16[256,512]{1,0:T(8,128)(2,1)S(1)}, u32[]{:S(2)}, u32[]{:S(2)}) collective-permute-start(bf16[256,512]{1,0:T(8,128)(2,1)S(1)} %collective-permute-done.3.refs_2_), channel_id=1, source_target_pairs={{0,1},{1,0},{2,3},{3,2},{4,5},{5,4},{6,7},{7,6},{8,9},{9,8},{10,11... | collective-permute-start | bytes 786440 | tf_op jit(solution)/shard_map/ppermute | solution.py:256
  22.0 10.1 %collective-permute-start.11 = (bf16[128,8192]{1,0:T(8,128)(2,1)S(1)}, bf16[128,8192]{1,0:T(8,128)(2,1)S(1)}, u32[]{:S(2)}, u32[]{:S(2)}) collective-permute-start(bf16[128,8192]{1,0:T(8,128)(2,1)S(1)} %copy-done), channel_id=1, source_target_pairs={{0,1},{1,0},{2,3},{3,2},{4,5},{5,4},{6,7},{7,6},{8,9},{9,8},{10,11... | collective-permute-start | bytes 6291464 | tf_op jit(solution)/shard_map/ppermute | solution.py:256
  22.1 10.0 %collective-permute-start.10 = (bf16[1024,512]{1,0:T(8,128)(2,1)S(1)}, bf16[1024,512]{1,0:T(8,128)(2,1)S(1)}, u32[]{:S(2)}, u32[]{:S(2)}) collective-permute-start(bf16[1024,512]{1,0:T(8,128)(2,1)S(1)} %copy-done.2), channel_id=1, source_target_pairs={{0,1},{1,0},{2,3},{3,2},{4,5},{5,4},{6,7},{7,6},{8,9},{9,8},{10,11... | collective-permute-start | bytes 3145736 | tf_op jit(solution)/shard_map/ppermute | solution.py:256
  22.6 14.8 %collective-permute-start.12 = (bf16[1024,512]{1,0:T(8,128)(2,1)S(1)}, bf16[1024,512]{1,0:T(8,128)(2,1)S(1)}, u32[]{:S(2)}, u32[]{:S(2)}) collective-permute-start(bf16[1024,512]{1,0:T(8,128)(2,1)S(1)} %join.3.refs_2_), channel_id=1, source_target_pairs={{0,8},{1,17},{2,10},{3,19},{4,12},{5,21},{6,14},{7,23},{8,0},{9,25... | collective-permute-start | bytes 3145736 | tf_op jit(solution)/shard_map/ppermute | solution.py:287
  23.6 8.6 %collective-permute-start.9 = (bf16[256,512]{1,0:T(8,128)(2,1)S(1)}, bf16[256,512]{1,0:T(8,128)(2,1)S(1)}, u32[]{:S(2)}, u32[]{:S(2)}) collective-permute-start(bf16[256,512]{1,0:T(8,128)(2,1)S(1)} %collective-permute-done.3.refs_2_), channel_id=1, source_target_pairs={{0,2},{1,3},{2,0},{3,1},{4,6},{5,7},{6,4},{7,5},{8,10},{9,11},{10,... | collective-permute-start | bytes 786440 | tf_op jit(solution)/shard_map/ppermute | solution.py:256
  32.2 1.5 %collective-permute-start.13 = (bf16[256,512]{1,0:T(8,128)(2,1)S(1)}, bf16[256,512]{1,0:T(8,128)(2,1)S(1)}, u32[]{:S(2)}, u32[]{:S(2)}) collective-permute-start(bf16[256,512]{1,0:T(8,128)(2,1)S(1)} %collective-permute-done.9.refs_0_), channel_id=1, source_target_pairs={{0,1},{1,0},{2,3},{3,2},{4,5},{5,4},{6,7},{7,6},{8,9},{9,8},{10,11... | collective-permute-start | bytes 786440 | tf_op jit(solution)/shard_map/ppermute | solution.py:256
  32.2 16.5 %collective-permute-start.16 = (bf16[512,512]{1,0:T(8,128)(2,1)S(1)}, bf16[512,512]{1,0:T(8,128)(2,1)S(1)}, u32[]{:S(2)}, u32[]{:S(2)}) collective-permute-start(bf16[512,512]{1,0:T(8,128)(2,1)S(1)} %far.1), channel_id=1, source_target_pairs={{0,2},{1,7},{2,0},{3,5},{4,6},{5,3},{6,4},{7,1},{8,10},{9,15},{10,... | collective-permute-start | bytes 1572872 | tf_op jit(solution)/shard_map/ppermute | solution.py:287
  33.7 15.0 %collective-permute-start.14 = (bf16[512,512]{1,0:T(8,128)(2,1)S(1)}, bf16[512,512]{1,0:T(8,128)(2,1)S(1)}, u32[]{:S(2)}, u32[]{:S(2)}) collective-permute-start(bf16[512,512]{1,0:T(8,128)(2,1)S(1)} %join.4.refs_3_), channel_id=1, source_target_pairs={{0,8},{1,17},{2,10},{3,19},{4,12},{5,21},{6,14},{7,23},{8,0},{9,25... | collective-permute-start | bytes 1572872 | tf_op jit(solution)/shard_map/ppermute | solution.py:287
  34.8 10.0 %collective-permute-start.8 = (f32[32,2304]{1,0:T(8,128)S(1)}, f32[32,2304]{1,0:T(8,128)S(1)}, u32[]{:S(2)}, u32[]{:S(2)}) collective-permute-start(f32[32,2304]{1,0:T(8,128)S(1)} %pass_on.1), channel_id=1, source_target_pairs={{0,16},{1,9},{2,18},{3,11},{4,20},{5,13},{6,22},{7,15},{8,24},{9,1... | collective-permute-start | bytes 884744 | tf_op jit(solution)/shard_map/ppermute | solution.py:287
  37.4 11.3 %collective-permute-start.15 = (bf16[256,512]{1,0:T(8,128)(2,1)S(1)}, bf16[256,512]{1,0:T(8,128)(2,1)S(1)}, u32[]{:S(2)}, u32[]{:S(2)}) collective-permute-start(bf16[256,512]{1,0:T(8,128)(2,1)S(1)} %take.1), channel_id=1, source_target_pairs={{0,16},{1,9},{2,18},{3,11},{4,20},{5,13},{6,22},{7,15},{8,24},{9,1... | collective-permute-start | bytes 786440 | tf_op jit(solution)/shard_map/ppermute | solution.py:287
  49.2 2.1 %copy-start.4 = (bf16[128,512]{1,0:T(8,128)(2,1)S(1)}, bf16[128,512]{1,0:T(8,128)(2,1)}, u32[]{:S(2)}) copy-start(bf16[128,512]{1,0:T(8,128)(2,1)} %refs_3_.1) | copy-start | bytes 393220
  49.3 2.1 %copy-start.6 = (f32[128]{0:T(128)S(1)}, f32[128]{0:T(128)}, u32[]{:S(2)}) copy-start(f32[128]{0:T(128)} %param.12) | copy-start | bytes 1540
  49.3 1.6 %collective-permute-start.17 = (f32[128,512]{1,0:T(8,128)S(1)}, f32[128,512]{1,0:T(8,128)S(1)}, u32[]{:S(2)}, u32[]{:S(2)}) collective-permute-start(f32[128,512]{1,0:T(8,128)S(1)} %get-tuple-element.97), channel_id=1, source_target_pairs={{0,1},{1,0},{2,3},{3,2},{4,5},{5,4},{6,7},{7,6},{8,9},{9,8},{10,11... | collective-permute-start | bytes 786440 | tf_op jit(solution)/shard_map/ppermute | solution.py:256
  50.9 6.3 %collective-permute-start.22 = (bf16[1280,512]{1,0:T(8,128)(2,1)S(1)}, bf16[1280,512]{1,0:T(8,128)(2,1)S(1)}, u32[]{:S(2)}, u32[]{:S(2)}) collective-permute-start(bf16[1280,512]{1,0:T(8,128)(2,1)S(1)} %join.5), channel_id=1, source_target_pairs={{0,1},{1,0},{2,3},{3,2},{4,5},{5,4},{6,7},{7,6},{8,9},{9,8},{10,11... | collective-permute-start | bytes 3932168 | tf_op jit(solution)/shard_map/ppermute | solution.py:256
  51.0 6.1 %collective-permute-start.21 = (bf16[1024,512]{1,0:T(8,128)(2,1)S(1)}, bf16[1024,512]{1,0:T(8,128)(2,1)S(1)}, u32[]{:S(2)}, u32[]{:S(2)}) collective-permute-start(bf16[1024,512]{1,0:T(8,128)(2,1)S(1)} %collective-permute-done.12.value.refs_4_), channel_id=1, source_target_pairs={{0,1},{1,0},{2,3},{3,2},{4,5},{5,4},{6,7},{7,6},{8,9},{9,8},{10,11... | collective-permute-start | bytes 3145736 | tf_op jit(solution)/shard_map/ppermute | solution.py:256
  53.7 7.4 %collective-permute-start.18 = (bf16[16,2176]{1,0:T(8,128)(2,1)S(1)}, bf16[16,2176]{1,0:T(8,128)(2,1)S(1)}, u32[]{:S(2)}, u32[]{:S(2)}) collective-permute-start(bf16[16,2176]{1,0:T(8,128)(2,1)S(1)} %get-tuple-element.102), channel_id=1, source_target_pairs={{0,8},{8,0},{16,24},{24,16},{1,9},{9,1},{17,25},{25,17},{2,10},{10... | collective-permute-start | bytes 208904 | tf_op jit(solution)/shard_map/ppermute | solution.py:256
  55.1 5.9 %collective-permute-start.19 = (bf16[16,2176]{1,0:T(8,128)(2,1)S(1)}, bf16[16,2176]{1,0:T(8,128)(2,1)S(1)}, u32[]{:S(2)}, u32[]{:S(2)}) collective-permute-start(bf16[16,2176]{1,0:T(8,128)(2,1)S(1)} %get-tuple-element.103), channel_id=1, source_target_pairs={{0,16},{8,24},{16,0},{24,8},{1,17},{9,25},{17,1},{25,9},{2,18},{10... | collective-permute-start | bytes 208904 | tf_op jit(solution)/shard_map/ppermute | solution.py:256
  55.9 5.2 %collective-permute-start.20 = (bf16[16,2176]{1,0:T(8,128)(2,1)S(1)}, bf16[16,2176]{1,0:T(8,128)(2,1)S(1)}, u32[]{:S(2)}, u32[]{:S(2)}) collective-permute-start(bf16[16,2176]{1,0:T(8,128)(2,1)S(1)} %get-tuple-element.104), channel_id=1, source_target_pairs={{0,24},{8,16},{16,8},{24,0},{1,25},{9,17},{17,9},{25,1},{2,26},{10... | collective-permute-start | bytes 208904 | tf_op jit(solution)/shard_map/ppermute | solution.py:256

commit v5 on v4

--- a/solution.py
+++ b/solution.py
@@ -34,7 +34,7 @@
         kernel,
         out_shape=[jax.ShapeDtypeStruct(shape, dtype) for shape, dtype in outs],
         in_specs=[spec for spec, _ in ins],
-        out_specs=[out] * len(outs),
+        out_specs=out if isinstance(out, list) else [out] * len(outs),
         scratch_shapes=scratch,
         compiler_params=pltpu.CompilerParams(vmem_limit_bytes=VMEM_LIMIT),
         cost_estimate=pl.CostEstimate(flops=0, bytes_accessed=moved, transcendentals=0),
@@ -164,7 +164,7 @@
 def middle_kernel(parts, told, *refs):
     place = position()
     (tokens, own, received, cotangent, gain, low_rank, up), refs = refs[:7], refs[7:]
-    (keys, pre_low, low_grad), grads = refs[:3], refs[3:]
+    (keys, pre_low, low_grad), grads, (held, copied) = refs[:3], refs[3:-2], refs[-2:]
     projected = own[...] + received[...]
     rows, width = projected.shape
     gains = gain[...]
@@ -179,10 +179,12 @@
         values = projected[:, columns]
         inverse = lax.rsqrt(jnp.mean(values * values, axis=-1, keepdims=True) + norm_eps)
         normed = values * inverse
-        keys[:, columns] = (normed * gains).astype(BF16)
+        held[:, columns] = (normed * gains).astype(BF16)
         scaled = cotangent[:, columns].astype(F32) * weight * gains
         along = jnp.mean(scaled * normed, axis=-1, keepdims=True)
         heads.append(inverse * (scaled - normed * along))
+    copy = pltpu.make_async_copy(held, keys, copied)
+    copy.start()
     pre = jnp.concatenate(heads, axis=-1)
     pre_low[...] = pre.astype(BF16)
     (pre_high, pre_rest), (up_high, up_rest), (low_high, low_rest) = map(split_two, (pre, up[...], low_rank[...]))
@@ -213,6 +215,7 @@
             @pl.when(part == other)
             def _():
                 out[:, down_width:] = up_grad[:, other * up_width : (other + 1) * up_width].astype(out.dtype)
+    copy.wait()
 
 
 def input_grad_kernel(pieces, sizes, pre_low, low_grad, split, *refs):
@@ -237,15 +240,21 @@
 
 
 def sum_kernel(told, *refs):
-    grads, (down, up) = refs[:-2], refs[-2:]
+    grads, (down, up, down_held, up_held, copied) = refs[:-5], refs[-5:]
     width = down.shape[2]
+    copies = []
     for stored in range(down.shape[0]):
         total = jnp.zeros(grads[0].shape, F32)
         for partner, grad in enumerate(grads):
             slot = told[partner : partner + 1, :1]
             total = total + jnp.where(slot == stored, grad[...].astype(F32), 0.0)
-        down[stored] = total[:, :width]
-        up[stored] = total[:, width:]
+        down_held[stored] = total[:, :width]
+        up_held[stored] = total[:, width:]
+        for source, target in ((down_held, down), (up_held, up)):
+            copies.append(pltpu.make_async_copy(source.at[stored], target.at[stored], copied.at[len(copies)]))
+            copies[-1].start()
+    for copy in copies:
+        copy.wait()
 
 
 def ordered(value, *earlier):
@@ -400,6 +409,8 @@
             for value in (told, tokens, total, received, cotangent, key_norm_gain.reshape(1, HD), low_rank, up)
         ],
         "key_norm",
+        out=[hbm] + [vmem] * (2 + parts),
+        scratch=[pltpu.VMEM((rows, key_width), BF16), pltpu.SemaphoreType.DMA],
     )
     others = [
         (xy12_pair, two(1, (2, 1), 1) + two(2, (2, 1), 1, last)),
@@ -421,6 +432,12 @@
         [((stored, rank, down_width), F32), ((stored, rank, up_width), F32)],
         [(vmem, told)] + [(vmem, value) for value in received],
         "grad_sum",
+        out=hbm,
+        scratch=[
+            pltpu.VMEM((stored, rank, down_width), F32),
+            pltpu.VMEM((stored, rank, up_width), F32),
+            pltpu.SemaphoreType.DMA((2 * stored,)),
+        ],
     )
     return keys, input_grad, jnp.swapaxes(down_sum, 1, 2), up_sum
 

time: 62.3 us -> 61.7 us (level)
  Pallas kernels: 10.7 us -> 10 us
    pallas_call x16, Pallas kernels: 10.7 us -> 10 us  [call(): pl.pallas_call(kernel, out_shape=[jax.ShapeDtypeStruct(shape, dtype) for...]
  transfers between devices with their start and end apart: 23 -> 23, of which waited for: 10 -> 10; matrix products, arithmetic and copies ran while one was open for 0% -> 0% of each run, Pallas kernels for 15% -> 14%
where the time goes in v5:
time: 61.7 us; the launch traced here: 61.4 us
  waiting for transfers between devices  25.5 us (41%)
  starting transfers between devices  20.6 us (33%)
  Pallas kernels  10 us (16%)
  local copies, waits for them, and re-layouts  3.13 us (5%)
  between operations  2.13 us (3%)
    ppermute x17, starting transfers between devices, flip(): return lax.ppermute(value, axis, [(i, i ^ bits) for i in range(size)])  14.9 us
    ppermute x17, waiting for transfers between devices, flip(): return lax.ppermute(value, axis, [(i, i ^ bits) for i in range(size)])  14.2 us
    ppermute x6, waiting for transfers between devices, over_split(): return lax.ppermute(value, ('dp', 'fsdp'), pairs)  11.2 us
    pallas_call x16, Pallas kernels, call(): pl.pallas_call(kernel, out_shape=[jax.ShapeDtypeStruct(shape, dtype) for...  10 us
    ppermute x6, starting transfers between devices, over_split(): return lax.ppermute(value, ('dp', 'fsdp'), pairs)  5.7 us
    unnamed x14, local copies, waits for them, and re-layouts  3.11 us
  transfers between devices with their start and end apart: 23, of which 10 were waited for; matrix products, arithmetic and copies ran while one was open for 0% of the time, Pallas kernels for 14%

profile of v5, /device:TPU:0, one launch (start us, length us, event | category | flops | bytes accessed | tf_op | source)
XLA Modules:
  0.0 61.4 jit_solution(11293590844906972480)
XLA Ops:
  0.6 0.0 copy-start
  0.7 1.4 %copy-done.1 = bf16[1024,512]{1,0:T(8,128)(2,1)S(1)} copy-done((bf16[1024,512]{1,0:T(8,128)(2,1)S(1)}, bf16[1024,512]{1,0:T(8,128)(2,1)}, u32[]{:S(2)}) %copy-start.1) | copy-done | bytes 1048600
  2.0 3.1 %collective-permute-start.4 = (bf16[256,512]{1,0:T(8,128)(2,1)S(1)}, bf16[256,512]{1,0:T(8,128)(2,1)S(1)}, u32[]{:S(2)}, u32[]{:S(2)}) collective-permute-start(bf16[256,512]{1,0:T(8,128)(2,1)S(1)} %near.1), channel_id=1, source_target_pairs={{0,2},{1,3},{2,0},{3,1},{4,6},{5,7},{6,4},{7,5},{8,10},{9,11},{10,... | collective-permute-start | bytes 786440 | tf_op jit(solution)/shard_map/ppermute | solution.py:265
  5.1 2.6 %collective-permute-start.3 = (bf16[256,512]{1,0:T(8,128)(2,1)S(1)}, bf16[256,512]{1,0:T(8,128)(2,1)S(1)}, u32[]{:S(2)}, u32[]{:S(2)}) collective-permute-start(bf16[256,512]{1,0:T(8,128)(2,1)S(1)} %near.1), channel_id=1, source_target_pairs={{0,4},{1,5},{2,6},{3,7},{4,0},{5,1},{6,2},{7,3},{8,12},{9,13},{10,... | collective-permute-start | bytes 786440 | tf_op jit(solution)/shard_map/ppermute | solution.py:265
  8.4 0.1 info.1.refs_0_
  8.4 2.4 %collective-permute-start.2 = (f32[1,128]{1,0:T(1,128)S(1)}, f32[1,128]{1,0:T(1,128)S(1)}, u32[]{:S(2)}, u32[]{:S(2)}) collective-permute-start(f32[1,128]{1,0:T(1,128)S(1)} %info.1.refs_0_), channel_id=1, source_target_pairs={{0,24},{8,16},{16,8},{24,0},{1,25},{9,17},{17,9},{25,1},{2,26},{10... | collective-permute-start | bytes 1544 | tf_op jit(solution)/shard_map/ppermute | solution.py:265
  10.9 0.5 collective-permute-start.1
  11.4 0.5 collective-permute-start
  12.6 0.0 copy-start.3
  12.6 1.0 %copy-done.3 = f32[3,2048,16]{1,2,0:T(8,128)S(1)} copy-done((f32[3,2048,16]{1,2,0:T(8,128)S(1)}, f32[3,2048,16]{1,2,0:T(8,128)}, u32[]{:S(2)}) %copy-start.3) | copy-done | bytes 393240
  13.6 0.7 %copy-done.5 = f32[3,16,128]{2,1,0:T(8,128)S(1)} copy-done((f32[3,16,128]{2,1,0:T(8,128)S(1)}, f32[3,16,128]{2,1,0:T(8,128)}, u32[]{:S(2)}) %copy-start.5) | copy-done | bytes 24600
  14.3 0.1 hold.1
  14.4 0.0 collective-permute-done.2.refs_3_
  14.4 0.0 collective-permute-done.1.refs_2_
  14.4 0.5 collective-permute-done.refs_1_
  14.9 0.2 adapter_messages.1
  15.2 1.0 %collective-permute-start.7 = (f32[32,2304]{1,0:T(8,128)S(1)}, f32[32,2304]{1,0:T(8,128)S(1)}, u32[]{:S(2)}, u32[]{:S(2)}) collective-permute-start(f32[32,2304]{1,0:T(8,128)S(1)} %get-tuple-element.73), channel_id=1, source_target_pairs={{0,8},{1,17},{2,10},{3,19},{4,12},{5,21},{6,14},{7,23},{8,0},{9,25... | collective-permute-start | bytes 884744 | tf_op jit(solution)/shard_map/ppermute | solution.py:296
  16.2 0.7 %collective-permute-done.4.refs_0_ = bf16[256,512]{1,0:T(8,128)(2,1)S(1)} collective-permute-done((bf16[256,512]{1,0:T(8,128)(2,1)S(1)}, bf16[256,512]{1,0:T(8,128)(2,1)S(1)}, u32[]{:S(2)}, u32[]{:S(2)}) %collective-permute-start.4) | collective-permute-done | bytes 262176 | tf_op jit(solution)/shard_map/ppermute | solution.py:265
  16.9 2.5 %collective-permute-done.3.refs_2_ = bf16[256,512]{1,0:T(8,128)(2,1)S(1)} collective-permute-done((bf16[256,512]{1,0:T(8,128)(2,1)S(1)}, bf16[256,512]{1,0:T(8,128)(2,1)S(1)}, u32[]{:S(2)}, u32[]{:S(2)}) %collective-permute-start.3) | collective-permute-done | bytes 262176 | tf_op jit(solution)/shard_map/ppermute | solution.py:265
  19.5 0.0 collective-permute-start.5
  19.5 0.5 collective-permute-start.6
  20.0 2.0 %collective-permute-done.7.received.sooner = f32[32,2304]{1,0:T(8,128)S(1)} collective-permute-done((f32[32,2304]{1,0:T(8,128)S(1)}, f32[32,2304]{1,0:T(8,128)S(1)}, u32[]{:S(2)}, u32[]{:S(2)}) %collective-permute-start.7) | collective-permute-done | bytes 294944 | tf_op jit(solution)/shard_map/ppermute | solution.py:296
  22.0 0.0 collective-permute-done.5.refs_1_
  22.0 0.0 collective-permute-done.6.refs_3_
  22.0 0.1 join.3.refs_2_
  22.0 0.1 collective-permute-start.11
  22.1 0.5 collective-permute-start.10
  22.6 1.0 %collective-permute-start.12 = (bf16[1024,512]{1,0:T(8,128)(2,1)S(1)}, bf16[1024,512]{1,0:T(8,128)(2,1)S(1)}, u32[]{:S(2)}, u32[]{:S(2)}) collective-permute-start(bf16[1024,512]{1,0:T(8,128)(2,1)S(1)} %join.3.refs_2_), channel_id=1, source_target_pairs={{0,8},{1,17},{2,10},{3,19},{4,12},{5,21},{6,14},{7,23},{8,0},{9,25... | collective-permute-start | bytes 3145736 | tf_op jit(solution)/shard_map/ppermute | solution.py:296
  23.6 0.5 collective-permute-start.9
  24.1 8.1 %collective-permute-done.9.refs_0_ = bf16[256,512]{1,0:T(8,128)(2,1)S(1)} collective-permute-done((bf16[256,512]{1,0:T(8,128)(2,1)S(1)}, bf16[256,512]{1,0:T(8,128)(2,1)S(1)}, u32[]{:S(2)}, u32[]{:S(2)}) %collective-permute-start.9) | collective-permute-done | bytes 262176 | tf_op jit(solution)/shard_map/ppermute | solution.py:265
  32.2 0.0 collective-permute-done.10.refs_1_
  32.2 0.0 collective-permute-done.11.tokens_pair
  32.2 0.0 collective-permute-start.13
  32.2 0.5 collective-permute-start.16
  32.7 1.0 %collective-permute-done.13.refs_1_ = bf16[256,512]{1,0:T(8,128)(2,1)S(1)} collective-permute-done((bf16[256,512]{1,0:T(8,128)(2,1)S(1)}, bf16[256,512]{1,0:T(8,128)(2,1)S(1)}, u32[]{:S(2)}, u32[]{:S(2)}) %collective-permute-start.13) | collective-permute-done | bytes 262176 | tf_op jit(solution)/shard_map/ppermute | solution.py:265
  33.7 1.0 %collective-permute-start.14 = (bf16[512,512]{1,0:T(8,128)(2,1)S(1)}, bf16[512,512]{1,0:T(8,128)(2,1)S(1)}, u32[]{:S(2)}, u32[]{:S(2)}) collective-permute-start(bf16[512,512]{1,0:T(8,128)(2,1)S(1)} %join.4.refs_3_), channel_id=1, source_target_pairs={{0,8},{1,17},{2,10},{3,19},{4,12},{5,21},{6,14},{7,23},{8,0},{9,25... | collective-permute-start | bytes 1572872 | tf_op jit(solution)/shard_map/ppermute | solution.py:296
  34.8 0.6 collective-permute-start.8
  35.4 2.0 %collective-permute-done.12.value.refs_4_ = bf16[1024,512]{1,0:T(8,128)(2,1)S(1)} collective-permute-done((bf16[1024,512]{1,0:T(8,128)(2,1)S(1)}, bf16[1024,512]{1,0:T(8,128)(2,1)S(1)}, u32[]{:S(2)}, u32[]{:S(2)}) %collective-permute-start.12) | collective-permute-done | bytes 1048608 | tf_op jit(solution)/shard_map/ppermute | solution.py:296
  37.4 1.6 %collective-permute-start.15 = (bf16[256,512]{1,0:T(8,128)(2,1)S(1)}, bf16[256,512]{1,0:T(8,128)(2,1)S(1)}, u32[]{:S(2)}, u32[]{:S(2)}) collective-permute-start(bf16[256,512]{1,0:T(8,128)(2,1)S(1)} %take.1), channel_id=1, source_target_pairs={{0,16},{1,9},{2,18},{3,11},{4,20},{5,13},{6,22},{7,15},{8,24},{9,1... | collective-permute-start | bytes 786440 | tf_op jit(solution)/shard_map/ppermute | solution.py:296
  39.0 5.8 %collective-permute-done.8.later = f32[32,2304]{1,0:T(8,128)S(1)} collective-permute-done((f32[32,2304]{1,0:T(8,128)S(1)}, f32[32,2304]{1,0:T(8,128)S(1)}, u32[]{:S(2)}, u32[]{:S(2)}) %collective-permute-start.8) | collective-permute-done | bytes 294944 | tf_op jit(solution)/shard_map/ppermute | solution.py:296
  44.8 1.5 %low_rank.1 = (bf16[32,8192]{1,0:T(8,128)(2,1)S(1)}, f32[16,512]{1,0:T(8,128)S(1)}, f32[128,16]{1,0:T(8,128)S(1)}, f32[128,512]{1,0:T(8,128)S(1)}, f32[4,128]{1,0:T(4,128)S(1)}) custom-call(bf16[128,8192]{1,0:T(8,128)(2,1)S(1)} %copy-done, f32[4,128]{1,0:T(4,128)S(1)} %get-tuple-element.71.slots, f32[16,2304]{1,0:T(8,128)S(1)} %get-tuple-element.72.own, ...), custom_call_target="tpu_custom_call" | custom-call | bytes 12582912 | tf_op jit(solution)/shard_map/low_rank/pallas_call | solution.py:33
  46.4 0.9 %base.2 = (f32[128,512]{1,0:T(8,128)S(1)}, f32[128,512]{1,0:T(8,128)S(1)}) custom-call(bf16[128,8192]{1,0:T(8,128)(2,1)S(1)} %copy-done, bf16[128,8192]{1,0:T(8,128)(2,1)S(1)} %collective-permute-done.11.tokens_pair, f32[128,512]{1,0:T(8,128)S(1)} %get-tuple-element.88.before, f32[128,512]{1,0:T(8,128)S(1)} %broadcast_in_dim.3.before_pair, ...), custom_call_target="tpu_custom_call" | custom-call | tf_op jit(solution)/shard_map/base/pallas_call | solution.py:33
  47.3 1.4 %collective-permute-done.15.refs_2_.refs_7_ = bf16[256,512]{1,0:T(8,128)(2,1)S(1)} collective-permute-done((bf16[256,512]{1,0:T(8,128)(2,1)S(1)}, bf16[256,512]{1,0:T(8,128)(2,1)S(1)}, u32[]{:S(2)}, u32[]{:S(2)}) %collective-permute-start.15) | collective-permute-done | bytes 262176 | tf_op jit(solution)/shard_map/ppermute | solution.py:296
  48.7 0.0 collective-permute-done.16.refs_1_.refs_6_
  48.7 0.0 collective-permute-done.14.refs_0_.refs_5_
  48.7 0.5 base.3
  49.2 0.0 copy-start.4
  49.3 0.0 copy-start.6
  49.3 0.2 collective-permute-start.17
  49.4 0.1 join.5
  49.5 1.3 %collective-permute-done.17.refs_2_ = f32[128,512]{1,0:T(8,128)S(1)} collective-permute-done((f32[128,512]{1,0:T(8,128)S(1)}, f32[128,512]{1,0:T(8,128)S(1)}, u32[]{:S(2)}, u32[]{:S(2)}) %collective-permute-start.17) | collective-permute-done | bytes 262176 | tf_op jit(solution)/shard_map/ppermute | solution.py:265
  50.9 0.1 collective-permute-start.22
  51.0 0.4 collective-permute-start.21
  51.4 1.6 %key_norm.1 = (bf16[128,512]{1,0:T(8,128)(2,1)}, bf16[128,512]{1,0:T(8,128)(2,1)S(1)}, f32[128,16]{1,0:T(8,128)S(1)}, f32[16,2176]{1,0:T(8,128)S(1)}, bf16[16,21...) custom-call(f32[4,128]{1,0:T(4,128)S(1)} %get-tuple-element.78.told, ...), custom_call_target="tpu_custom_call" | custom-call | tf_op jit(solution)/shard_map/key_norm/pallas_call | solution.py:33
  53.0 1.5 %collective-permute-start.18 = (bf16[16,2176]{1,0:T(8,128)(2,1)S(1)}, bf16[16,2176]{1,0:T(8,128)(2,1)S(1)}, u32[]{:S(2)}, u32[]{:S(2)}) collective-permute-start(bf16[16,2176]{1,0:T(8,128)(2,1)S(1)} %get-tuple-element.102), channel_id=1, source_target_pairs={{0,8},{8,0},{16,24},{24,16},{1,9},{9,1},{17,25},{25,17},{2,10},{10... | collective-permute-start | bytes 208904 | tf_op jit(solution)/shard_map/ppermute | solution.py:265
  54.6 0.8 %collective-permute-start.19 = (bf16[16,2176]{1,0:T(8,128)(2,1)S(1)}, bf16[16,2176]{1,0:T(8,128)(2,1)S(1)}, u32[]{:S(2)}, u32[]{:S(2)}) collective-permute-start(bf16[16,2176]{1,0:T(8,128)(2,1)S(1)} %get-tuple-element.103), channel_id=1, source_target_pairs={{0,16},{8,24},{16,0},{24,8},{1,17},{9,25},{17,1},{25,9},{2,18},{10... | collective-permute-start | bytes 208904 | tf_op jit(solution)/shard_map/ppermute | solution.py:265
  55.3 1.3 %collective-permute-start.20 = (bf16[16,2176]{1,0:T(8,128)(2,1)S(1)}, bf16[16,2176]{1,0:T(8,128)(2,1)S(1)}, u32[]{:S(2)}, u32[]{:S(2)}) collective-permute-start(bf16[16,2176]{1,0:T(8,128)(2,1)S(1)} %get-tuple-element.104), channel_id=1, source_target_pairs={{0,24},{8,16},{16,8},{24,0},{1,25},{9,17},{17,9},{25,1},{2,26},{10... | collective-permute-start | bytes 208904 | tf_op jit(solution)/shard_map/ppermute | solution.py:265
  56.6 0.0 collective-permute-done.21.refs_8_
  56.6 0.0 collective-permute-done.22.refs_9_
  56.6 3.9 %input_grad.1 = bf16[128,8192]{1,0:T(8,128)(2,1)} custom-call(bf16[128,512]{1,0:T(8,128)(2,1)S(1)} %get-tuple-element.105.pre_low, f32[128,16]{1,0:T(8,128)S(1)} %get-tuple-element.106.low_grad, bf16[32,8192]{1,0:T(8,128)(2,1)S(1)} %get-tuple-element.107.split, bf16[1024,512]{1,0:T(8,128)(2,1)S(1)} %copy-done.2, ...), custom_call_target="tpu_custom_call" | custom-call | tf_op jit(solution)/shard_map/input_grad/pallas_call | solution.py:33
  60.5 0.0 collective-permute-done.18.refs_1_
  60.5 0.0 collective-permute-done.19.refs_2_
  60.5 0.0 collective-permute-done.20.refs_3_
  60.5 0.9 %grad_sum.1 = (f32[3,16,2048]{2,1,0:T(8,128)}, f32[3,16,128]{2,1,0:T(8,128)}) custom-call(f32[4,128]{1,0:T(4,128)S(1)} %get-tuple-element.78.told, f32[16,2176]{1,0:T(8,128)S(1)} %get-tuple-element.112.refs_0_, bf16[16,2176]{1,0:T(8,128)(2,1)S(1)} %collective-permute-done.18.refs_1_, bf16[16,2176]{1,0:T(8,128)(2,1)S(1)} %collective-permute-done.19.refs_2_, ...), custom_call_target="tpu_custom_call" | custom-call | tf_op jit(solution)/shard_map/grad_sum/pallas_call | solution.py:33
  (13 shorter events, 0.2 us)
Async XLA Ops:
  0.6 21.4 %copy-start = (bf16[128,8192]{1,0:T(8,128)(2,1)S(1)}, bf16[128,8192]{1,0:T(8,128)(2,1)}, u32[]{:S(2)}) copy-start(bf16[128,8192]{1,0:T(8,128)(2,1)} %refs_0_.8) | copy-start | bytes 6291460
  0.6 1.4 %copy-start.1 = (bf16[1024,512]{1,0:T(8,128)(2,1)S(1)}, bf16[1024,512]{1,0:T(8,128)(2,1)}, u32[]{:S(2)}) copy-start(bf16[1024,512]{1,0:T(8,128)(2,1)} %refs_0_.9) | copy-start | bytes 3145732
  2.0 20.1 %copy-start.2 = (bf16[1024,512]{1,0:T(8,128)(2,1)S(1)}, bf16[1024,512]{1,0:T(8,128)(2,1)}, u32[]{:S(2)}) copy-start(bf16[1024,512]{1,0:T(8,128)(2,1)} %refs_0_.9) | copy-start | bytes 3145732
  2.0 14.9 %collective-permute-start.4 = (bf16[256,512]{1,0:T(8,128)(2,1)S(1)}, bf16[256,512]{1,0:T(8,128)(2,1)S(1)}, u32[]{:S(2)}, u32[]{:S(2)}) collective-permute-start(bf16[256,512]{1,0:T(8,128)(2,1)S(1)} %near.1), channel_id=1, source_target_pairs={{0,2},{1,3},{2,0},{3,1},{4,6},{5,7},{6,4},{7,5},{8,10},{9,11},{10,... | collective-permute-start | bytes 786440 | tf_op jit(solution)/shard_map/ppermute | solution.py:265
  5.1 14.3 %collective-permute-start.3 = (bf16[256,512]{1,0:T(8,128)(2,1)S(1)}, bf16[256,512]{1,0:T(8,128)(2,1)S(1)}, u32[]{:S(2)}, u32[]{:S(2)}) collective-permute-start(bf16[256,512]{1,0:T(8,128)(2,1)S(1)} %near.1), channel_id=1, source_target_pairs={{0,4},{1,5},{2,6},{3,7},{4,0},{5,1},{6,2},{7,3},{8,12},{9,13},{10,... | collective-permute-start | bytes 786440 | tf_op jit(solution)/shard_map/ppermute | solution.py:265
  8.4 6.0 %collective-permute-start.2 = (f32[1,128]{1,0:T(1,128)S(1)}, f32[1,128]{1,0:T(1,128)S(1)}, u32[]{:S(2)}, u32[]{:S(2)}) collective-permute-start(f32[1,128]{1,0:T(1,128)S(1)} %info.1.refs_0_), channel_id=1, source_target_pairs={{0,24},{8,16},{16,8},{24,0},{1,25},{9,17},{17,9},{25,1},{2,26},{10... | collective-permute-start | bytes 1544 | tf_op jit(solution)/shard_map/ppermute | solution.py:265
  10.9 3.5 %collective-permute-start.1 = (f32[1,128]{1,0:T(1,128)S(1)}, f32[1,128]{1,0:T(1,128)S(1)}, u32[]{:S(2)}, u32[]{:S(2)}) collective-permute-start(f32[1,128]{1,0:T(1,128)S(1)} %info.1.refs_0_), channel_id=1, source_target_pairs={{0,16},{8,24},{16,0},{24,8},{1,17},{9,25},{17,1},{25,9},{2,18},{10... | collective-permute-start | bytes 1544 | tf_op jit(solution)/shard_map/ppermute | solution.py:265
  11.4 3.5 %collective-permute-start = (f32[1,128]{1,0:T(1,128)S(1)}, f32[1,128]{1,0:T(1,128)S(1)}, u32[]{:S(2)}, u32[]{:S(2)}) collective-permute-start(f32[1,128]{1,0:T(1,128)S(1)} %info.1.refs_0_), channel_id=1, source_target_pairs={{0,8},{8,0},{16,24},{24,16},{1,9},{9,1},{17,25},{25,17},{2,10},{10... | collective-permute-start | bytes 1544 | tf_op jit(solution)/shard_map/ppermute | solution.py:265
  12.6 1.0 %copy-start.3 = (f32[3,2048,16]{1,2,0:T(8,128)S(1)}, f32[3,2048,16]{1,2,0:T(8,128)}, u32[]{:S(2)}) copy-start(f32[3,2048,16]{1,2,0:T(8,128)} %param.10) | copy-start | bytes 1179652
  13.6 0.7 %copy-start.5 = (f32[3,16,128]{2,1,0:T(8,128)S(1)}, f32[3,16,128]{2,1,0:T(8,128)}, u32[]{:S(2)}) copy-start(f32[3,16,128]{2,1,0:T(8,128)} %up.1) | copy-start | bytes 73732
  15.2 6.8 %collective-permute-start.7 = (f32[32,2304]{1,0:T(8,128)S(1)}, f32[32,2304]{1,0:T(8,128)S(1)}, u32[]{:S(2)}, u32[]{:S(2)}) collective-permute-start(f32[32,2304]{1,0:T(8,128)S(1)} %get-tuple-element.73), channel_id=1, source_target_pairs={{0,8},{1,17},{2,10},{3,19},{4,12},{5,21},{6,14},{7,23},{8,0},{9,25... | collective-permute-start | bytes 884744 | tf_op jit(solution)/shard_map/ppermute | solution.py:296
  19.5 2.5 %collective-permute-start.5 = (bf16[256,512]{1,0:T(8,128)(2,1)S(1)}, bf16[256,512]{1,0:T(8,128)(2,1)S(1)}, u32[]{:S(2)}, u32[]{:S(2)}) collective-permute-start(bf16[256,512]{1,0:T(8,128)(2,1)S(1)} %collective-permute-done.4.refs_0_), channel_id=1, source_target_pairs={{0,1},{1,0},{2,3},{3,2},{4,5},{5,4},{6,7},{7,6},{8,9},{9,8},{10,11... | collective-permute-start | bytes 786440 | tf_op jit(solution)/shard_map/ppermute | solution.py:265
  19.5 2.5 %collective-permute-start.6 = (bf16[256,512]{1,0:T(8,128)(2,1)S(1)}, bf16[256,512]{1,0:T(8,128)(2,1)S(1)}, u32[]{:S(2)}, u32[]{:S(2)}) collective-permute-start(bf16[256,512]{1,0:T(8,128)(2,1)S(1)} %collective-permute-done.3.refs_2_), channel_id=1, source_target_pairs={{0,1},{1,0},{2,3},{3,2},{4,5},{5,4},{6,7},{7,6},{8,9},{9,8},{10,11... | collective-permute-start | bytes 786440 | tf_op jit(solution)/shard_map/ppermute | solution.py:265
  22.0 10.1 %collective-permute-start.11 = (bf16[128,8192]{1,0:T(8,128)(2,1)S(1)}, bf16[128,8192]{1,0:T(8,128)(2,1)S(1)}, u32[]{:S(2)}, u32[]{:S(2)}) collective-permute-start(bf16[128,8192]{1,0:T(8,128)(2,1)S(1)} %copy-done), channel_id=1, source_target_pairs={{0,1},{1,0},{2,3},{3,2},{4,5},{5,4},{6,7},{7,6},{8,9},{9,8},{10,11... | collective-permute-start | bytes 6291464 | tf_op jit(solution)/shard_map/ppermute | solution.py:265
  22.1 10.0 %collective-permute-start.10 = (bf16[1024,512]{1,0:T(8,128)(2,1)S(1)}, bf16[1024,512]{1,0:T(8,128)(2,1)S(1)}, u32[]{:S(2)}, u32[]{:S(2)}) collective-permute-start(bf16[1024,512]{1,0:T(8,128)(2,1)S(1)} %copy-done.2), channel_id=1, source_target_pairs={{0,1},{1,0},{2,3},{3,2},{4,5},{5,4},{6,7},{7,6},{8,9},{9,8},{10,11... | collective-permute-start | bytes 3145736 | tf_op jit(solution)/shard_map/ppermute | solution.py:265
  22.6 14.8 %collective-permute-start.12 = (bf16[1024,512]{1,0:T(8,128)(2,1)S(1)}, bf16[1024,512]{1,0:T(8,128)(2,1)S(1)}, u32[]{:S(2)}, u32[]{:S(2)}) collective-permute-start(bf16[1024,512]{1,0:T(8,128)(2,1)S(1)} %join.3.refs_2_), channel_id=1, source_target_pairs={{0,8},{1,17},{2,10},{3,19},{4,12},{5,21},{6,14},{7,23},{8,0},{9,25... | collective-permute-start | bytes 3145736 | tf_op jit(solution)/shard_map/ppermute | solution.py:296
  23.6 8.6 %collective-permute-start.9 = (bf16[256,512]{1,0:T(8,128)(2,1)S(1)}, bf16[256,512]{1,0:T(8,128)(2,1)S(1)}, u32[]{:S(2)}, u32[]{:S(2)}) collective-permute-start(bf16[256,512]{1,0:T(8,128)(2,1)S(1)} %collective-permute-done.3.refs_2_), channel_id=1, source_target_pairs={{0,2},{1,3},{2,0},{3,1},{4,6},{5,7},{6,4},{7,5},{8,10},{9,11},{10,... | collective-permute-start | bytes 786440 | tf_op jit(solution)/shard_map/ppermute | solution.py:265
  32.2 1.5 %collective-permute-start.13 = (bf16[256,512]{1,0:T(8,128)(2,1)S(1)}, bf16[256,512]{1,0:T(8,128)(2,1)S(1)}, u32[]{:S(2)}, u32[]{:S(2)}) collective-permute-start(bf16[256,512]{1,0:T(8,128)(2,1)S(1)} %collective-permute-done.9.refs_0_), channel_id=1, source_target_pairs={{0,1},{1,0},{2,3},{3,2},{4,5},{5,4},{6,7},{7,6},{8,9},{9,8},{10,11... | collective-permute-start | bytes 786440 | tf_op jit(solution)/shard_map/ppermute | solution.py:265
  32.2 16.5 %collective-permute-start.16 = (bf16[512,512]{1,0:T(8,128)(2,1)S(1)}, bf16[512,512]{1,0:T(8,128)(2,1)S(1)}, u32[]{:S(2)}, u32[]{:S(2)}) collective-permute-start(bf16[512,512]{1,0:T(8,128)(2,1)S(1)} %far.1), channel_id=1, source_target_pairs={{0,2},{1,7},{2,0},{3,5},{4,6},{5,3},{6,4},{7,1},{8,10},{9,15},{10,... | collective-permute-start | bytes 1572872 | tf_op jit(solution)/shard_map/ppermute | solution.py:296
  33.7 15.0 %collective-permute-start.14 = (bf16[512,512]{1,0:T(8,128)(2,1)S(1)}, bf16[512,512]{1,0:T(8,128)(2,1)S(1)}, u32[]{:S(2)}, u32[]{:S(2)}) collective-permute-start(bf16[512,512]{1,0:T(8,128)(2,1)S(1)} %join.4.refs_3_), channel_id=1, source_target_pairs={{0,8},{1,17},{2,10},{3,19},{4,12},{5,21},{6,14},{7,23},{8,0},{9,25... | collective-permute-start | bytes 1572872 | tf_op jit(solution)/shard_map/ppermute | solution.py:296
  34.8 10.0 %collective-permute-start.8 = (f32[32,2304]{1,0:T(8,128)S(1)}, f32[32,2304]{1,0:T(8,128)S(1)}, u32[]{:S(2)}, u32[]{:S(2)}) collective-permute-start(f32[32,2304]{1,0:T(8,128)S(1)} %pass_on.1), channel_id=1, source_target_pairs={{0,16},{1,9},{2,18},{3,11},{4,20},{5,13},{6,22},{7,15},{8,24},{9,1... | collective-permute-start | bytes 884744 | tf_op jit(solution)/shard_map/ppermute | solution.py:296
  37.4 11.3 %collective-permute-start.15 = (bf16[256,512]{1,0:T(8,128)(2,1)S(1)}, bf16[256,512]{1,0:T(8,128)(2,1)S(1)}, u32[]{:S(2)}, u32[]{:S(2)}) collective-permute-start(bf16[256,512]{1,0:T(8,128)(2,1)S(1)} %take.1), channel_id=1, source_target_pairs={{0,16},{1,9},{2,18},{3,11},{4,20},{5,13},{6,22},{7,15},{8,24},{9,1... | collective-permute-start | bytes 786440 | tf_op jit(solution)/shard_map/ppermute | solution.py:296
  49.2 2.1 %copy-start.4 = (bf16[128,512]{1,0:T(8,128)(2,1)S(1)}, bf16[128,512]{1,0:T(8,128)(2,1)}, u32[]{:S(2)}) copy-start(bf16[128,512]{1,0:T(8,128)(2,1)} %refs_3_.1) | copy-start | bytes 393220
  49.3 2.1 %copy-start.6 = (f32[128]{0:T(128)S(1)}, f32[128]{0:T(128)}, u32[]{:S(2)}) copy-start(f32[128]{0:T(128)} %param.12) | copy-start | bytes 1540
  49.3 1.6 %collective-permute-start.17 = (f32[128,512]{1,0:T(8,128)S(1)}, f32[128,512]{1,0:T(8,128)S(1)}, u32[]{:S(2)}, u32[]{:S(2)}) collective-permute-start(f32[128,512]{1,0:T(8,128)S(1)} %get-tuple-element.97), channel_id=1, source_target_pairs={{0,1},{1,0},{2,3},{3,2},{4,5},{5,4},{6,7},{7,6},{8,9},{9,8},{10,11... | collective-permute-start | bytes 786440 | tf_op jit(solution)/shard_map/ppermute | solution.py:265
  50.9 5.7 %collective-permute-start.22 = (bf16[1280,512]{1,0:T(8,128)(2,1)S(1)}, bf16[1280,512]{1,0:T(8,128)(2,1)S(1)}, u32[]{:S(2)}, u32[]{:S(2)}) collective-permute-start(bf16[1280,512]{1,0:T(8,128)(2,1)S(1)} %join.5), channel_id=1, source_target_pairs={{0,1},{1,0},{2,3},{3,2},{4,5},{5,4},{6,7},{7,6},{8,9},{9,8},{10,11... | collective-permute-start | bytes 3932168 | tf_op jit(solution)/shard_map/ppermute | solution.py:265
  51.0 5.6 %collective-permute-start.21 = (bf16[1024,512]{1,0:T(8,128)(2,1)S(1)}, bf16[1024,512]{1,0:T(8,128)(2,1)S(1)}, u32[]{:S(2)}, u32[]{:S(2)}) collective-permute-start(bf16[1024,512]{1,0:T(8,128)(2,1)S(1)} %collective-permute-done.12.value.refs_4_), channel_id=1, source_target_pairs={{0,1},{1,0},{2,3},{3,2},{4,5},{5,4},{6,7},{7,6},{8,9},{9,8},{10,11... | collective-permute-start | bytes 3145736 | tf_op jit(solution)/shard_map/ppermute | solution.py:265
  53.0 7.5 %collective-permute-start.18 = (bf16[16,2176]{1,0:T(8,128)(2,1)S(1)}, bf16[16,2176]{1,0:T(8,128)(2,1)S(1)}, u32[]{:S(2)}, u32[]{:S(2)}) collective-permute-start(bf16[16,2176]{1,0:T(8,128)(2,1)S(1)} %get-tuple-element.102), channel_id=1, source_target_pairs={{0,8},{8,0},{16,24},{24,16},{1,9},{9,1},{17,25},{25,17},{2,10},{10... | collective-permute-start | bytes 208904 | tf_op jit(solution)/shard_map/ppermute | solution.py:265
  54.6 5.9 %collective-permute-start.19 = (bf16[16,2176]{1,0:T(8,128)(2,1)S(1)}, bf16[16,2176]{1,0:T(8,128)(2,1)S(1)}, u32[]{:S(2)}, u32[]{:S(2)}) collective-permute-start(bf16[16,2176]{1,0:T(8,128)(2,1)S(1)} %get-tuple-element.103), channel_id=1, source_target_pairs={{0,16},{8,24},{16,0},{24,8},{1,17},{9,25},{17,1},{25,9},{2,18},{10... | collective-permute-start | bytes 208904 | tf_op jit(solution)/shard_map/ppermute | solution.py:265
  55.3 5.2 %collective-permute-start.20 = (bf16[16,2176]{1,0:T(8,128)(2,1)S(1)}, bf16[16,2176]{1,0:T(8,128)(2,1)S(1)}, u32[]{:S(2)}, u32[]{:S(2)}) collective-permute-start(bf16[16,2176]{1,0:T(8,128)(2,1)S(1)} %get-tuple-element.104), channel_id=1, source_target_pairs={{0,24},{8,16},{16,8},{24,0},{1,25},{9,17},{17,9},{25,1},{2,26},{10... | collective-permute-start | bytes 208904 | tf_op jit(solution)/shard_map/ppermute | solution.py:265

commit v6 on v5

--- a/solution.py
+++ b/solution.py
@@ -227,10 +227,11 @@
     turned = pre_low[...].T
     copies = []
     for index, piece in enumerate(pieces):
+        if index == 0 or piece["buffer"] != pieces[index - 1]["buffer"]:
+            whole = jnp.dot(buffers[piece["buffer"]][...], turned, preferred_element_type=F32).T
         columns = pl.ds(column_of(place, piece, *sizes), piece["rows"])
-        rows = pl.ds(piece["first"], piece["rows"])
-        value = jnp.dot(buffers[piece["buffer"]][rows, :], turned, preferred_element_type=F32).T
         right = jnp.concatenate([split[:, columns], split[:rank, columns]], axis=0)
+        value = whole[:, piece["first"] : piece["first"] + piece["rows"]]
         value = value + jnp.dot(left, right, preferred_element_type=F32)
         held[:, columns] = value.astype(BF16)
         copies.append(pltpu.make_async_copy(held.at[:, columns], out.at[:, columns], copied.at[index]))
@@ -304,8 +305,8 @@
 
     matrix = frozen_key_matrix
     part = ((part_rows, key_width), BF16)
-    (near,) = call(functools.partial(part_kernel, 0), [part], [(vmem, matrix)], "near")
-    z2, z1 = over_z(near, 2), over_z(near, 1)
+    near = lax.dynamic_slice_in_dim(matrix, lax.axis_index("dp") * part_rows, part_rows, 0)
+    z1, z2 = over_z(near, 1), over_z(near, 2)
     (info,) = call(info_kernel, [((1, HD), F32)], [(vmem, adapter_offset)], "info")
     offsets = [info] + [over_dp(info, bits) for bits in range(1, parts)]
     held = call(
@@ -322,7 +323,7 @@
         [(vmem, value) for value in (*offsets, *held)],
         "adapter_messages",
     )
-    z2, z1 = ordered((z2, z1), sooner)
+    z1, z2 = ordered((z1, z2), sooner)
     sooner = over_split(sooner, (1, 2), (0, 0))
     z3 = over_z(z2, 1)
     z1_pair, z2_pair, sooner = lax.optimization_barrier((over_core(z1), over_core(z2), sooner))
@@ -392,13 +393,13 @@
     late = [(xy3, two(3, (1, 2))), (d13, two((1, 3), 3)), (xy4, [piece(2, 3, 0)])]
     total, total_pair = base(totals, [], late)
     received = over_core(total_pair)
-    lone = call(
+    (lone,) = call(
         functools.partial(join_kernel, None),
-        [((5 * part_rows, key_width), BF16)],
-        [(vmem, value) for value in (xy3, d13, xy4)],
+        [((9 * part_rows, key_width), BF16)],
+        [(vmem, value) for value in (xy12, xy3, d13, xy4)],
         "join",
-    )[0]
-    xy12_pair, lone_pair = over_core(ordered(xy12, received)), over_core(ordered(lone, received))
+    )
+    lone_pair = over_core(ordered(lone, received))
     keys, pre_low, low_grad, *grads = call(
         functools.partial(middle_kernel, parts),
         [((rows, key_width), BF16), ((rows, key_width), BF16), ((rows, rank), F32)]
@@ -412,10 +413,8 @@
         out=[hbm] + [vmem] * (2 + parts),
         scratch=[pltpu.VMEM((rows, key_width), BF16), pltpu.SemaphoreType.DMA],
     )
-    others = [
-        (xy12_pair, two(1, (2, 1), 1) + two(2, (2, 1), 1, last)),
-        (lone_pair, two(3, (2, 1), 1) + two((3, 1), 3, 1, last) + [piece(2, 3, 1, first=2 * last)]),
-    ]
+    others = two(1, (2, 1), 1) + two(2, (2, 1), 1, last) + two(3, (2, 1), 1, 2 * last) + two((3, 1), 3, 1, 3 * last)
+    others = [(lone_pair, others + [piece(2, 3, 1, first=4 * last)])]
     received = [grads[0]] + [over_dp(grads[bits], bits) for bits in range(1, parts)]
     buffers, pieces = flat(shared + early + late + others)
     (input_grad,) = call(

time: 61.7 us -> 61.3 us (level)
    unnamed x14 -> x12, local copies, waits for them, and re-layouts: 3.11 us -> 1.75 us
    ppermute x6, waiting for transfers between devices: 11.2 us -> 12.5 us  [over_split(): return lax.ppermute(value, ('dp', 'fsdp'), pairs)]
    dynamic_slice x0 -> x1, local copies, waits for them, and re-layouts: none -> 1.12 us  [on_device_lines(): lax.dynamic_slice_in_dim(matrix, lax.axis_index('dp') * part_rows, part_r...]
    ppermute x17 -> x16, waiting for transfers between devices: 14.2 us -> 13.2 us  [flip(): return lax.ppermute(value, axis, [(i, i ^ bits) for i in range(size)])]
    ppermute x17 -> x16, starting transfers between devices: 14.9 us -> 14.6 us  [flip(): return lax.ppermute(value, axis, [(i, i ^ bits) for i in range(size)])]
    pallas_call x16 -> x15, Pallas kernels: 10 us -> 10 us  [call(): pl.pallas_call(kernel, out_shape=[jax.ShapeDtypeStruct(shape, dtype) for...]
  transfers between devices with their start and end apart: 23 -> 22, of which waited for: 10 -> 12; matrix products, arithmetic and copies ran while one was open for 0% -> 0% of each run, Pallas kernels for 14% -> 14%
where the time goes in v6:
time: 61.3 us; the launch traced here: 61 us
  waiting for transfers between devices  25.7 us (42%)
  starting transfers between devices  20.3 us (33%)
  Pallas kernels  10 us (16%)
  local copies, waits for them, and re-layouts  2.89 us (5%)
  between operations  2.13 us (3%)
    ppermute x16, starting transfers between devices, flip(): return lax.ppermute(value, axis, [(i, i ^ bits) for i in range(size)])  14.6 us
    ppermute x16, waiting for transfers between devices, flip(): return lax.ppermute(value, axis, [(i, i ^ bits) for i in range(size)])  13.2 us
    ppermute x6, waiting for transfers between devices, over_split(): return lax.ppermute(value, ('dp', 'fsdp'), pairs)  12.5 us
    pallas_call x15, Pallas kernels, call(): pl.pallas_call(kernel, out_shape=[jax.ShapeDtypeStruct(shape, dtype) for...  10 us
    ppermute x6, starting transfers between devices, over_split(): return lax.ppermute(value, ('dp', 'fsdp'), pairs)  5.7 us
    unnamed x12, local copies, waits for them, and re-layouts  1.75 us
  transfers between devices with their start and end apart: 22, of which 12 were waited for; matrix products, arithmetic and copies ran while one was open for 0% of the time, Pallas kernels for 14%

profile of v6, /device:TPU:0, one launch (start us, length us, event | category | flops | bytes accessed | tf_op | source)
XLA Modules:
  0.0 61.0 jit_solution(12006771050406581064)
XLA Ops:
  0.6 0.0 copy-start.1
  0.7 1.1 %constant_dynamic-slice_fusion = bf16[256,512]{1,0:T(8,128)(2,1)S(1)} fusion(bf16[1024,512]{1,0:T(8,128)(2,1)} %refs_0_.7, s32[]{:T(128)S(6)} %select_n.3), kind=kLoop, calls=%fused_computation | loop fusion | bytes 524292 | tf_op jit(solution)/shard_map/dynamic_slice | solution.py:308
  1.8 4.1 %collective-permute-start.4 = (bf16[256,512]{1,0:T(8,128)(2,1)S(1)}, bf16[256,512]{1,0:T(8,128)(2,1)S(1)}, u32[]{:S(2)}, u32[]{:S(2)}) collective-permute-start(bf16[256,512]{1,0:T(8,128)(2,1)S(1)} %constant_dynamic-slice_fusion), channel_id=1, source_target_pairs={{0,4},{1,5},{2,6},{3,7},{4,0},{5,1},{6,2},{7,3},{8,12},{9,13},{10,... | collective-permute-start | bytes 786440 | tf_op jit(solution)/shard_map/ppermute | solution.py:266
  5.9 1.6 %collective-permute-start.3 = (bf16[256,512]{1,0:T(8,128)(2,1)S(1)}, bf16[256,512]{1,0:T(8,128)(2,1)S(1)}, u32[]{:S(2)}, u32[]{:S(2)}) collective-permute-start(bf16[256,512]{1,0:T(8,128)(2,1)S(1)} %constant_dynamic-slice_fusion), channel_id=1, source_target_pairs={{0,2},{1,3},{2,0},{3,1},{4,6},{5,7},{6,4},{7,5},{8,10},{9,11},{10,... | collective-permute-start | bytes 786440 | tf_op jit(solution)/shard_map/ppermute | solution.py:266
  8.1 0.1 info.1.refs_0_
  8.2 2.4 %collective-permute-start.2 = (f32[1,128]{1,0:T(1,128)S(1)}, f32[1,128]{1,0:T(1,128)S(1)}, u32[]{:S(2)}, u32[]{:S(2)}) collective-permute-start(f32[1,128]{1,0:T(1,128)S(1)} %info.1.refs_0_), channel_id=1, source_target_pairs={{0,24},{8,16},{16,8},{24,0},{1,25},{9,17},{17,9},{25,1},{2,26},{10... | collective-permute-start | bytes 1544 | tf_op jit(solution)/shard_map/ppermute | solution.py:266
  10.6 0.5 collective-permute-start.1
  11.1 0.5 collective-permute-start
  12.3 0.0 copy-start.2
  12.3 1.0 %copy-done.2 = f32[3,2048,16]{1,2,0:T(8,128)S(1)} copy-done((f32[3,2048,16]{1,2,0:T(8,128)S(1)}, f32[3,2048,16]{1,2,0:T(8,128)}, u32[]{:S(2)}) %copy-start.2) | copy-done | bytes 393240
  13.3 0.7 %copy-done.4 = f32[3,16,128]{2,1,0:T(8,128)S(1)} copy-done((f32[3,16,128]{2,1,0:T(8,128)S(1)}, f32[3,16,128]{2,1,0:T(8,128)}, u32[]{:S(2)}) %copy-start.4) | copy-done | bytes 24600
  14.1 0.1 hold.1
  14.1 0.0 collective-permute-done.2.refs_3_
  14.1 0.0 collective-permute-done.1.refs_2_
  14.2 0.5 collective-permute-done.refs_1_
  14.7 0.2 adapter_messages.1
  14.9 1.0 %collective-permute-start.7 = (f32[32,2304]{1,0:T(8,128)S(1)}, f32[32,2304]{1,0:T(8,128)S(1)}, u32[]{:S(2)}, u32[]{:S(2)}) collective-permute-start(f32[32,2304]{1,0:T(8,128)S(1)} %get-tuple-element.72), channel_id=1, source_target_pairs={{0,8},{1,17},{2,10},{3,19},{4,12},{5,21},{6,14},{7,23},{8,0},{9,25... | collective-permute-start | bytes 884744 | tf_op jit(solution)/shard_map/ppermute | solution.py:297
  15.9 2.0 %collective-permute-done.4.refs_2_ = bf16[256,512]{1,0:T(8,128)(2,1)S(1)} collective-permute-done((bf16[256,512]{1,0:T(8,128)(2,1)S(1)}, bf16[256,512]{1,0:T(8,128)(2,1)S(1)}, u32[]{:S(2)}, u32[]{:S(2)}) %collective-permute-start.4) | collective-permute-done | bytes 262176 | tf_op jit(solution)/shard_map/ppermute | solution.py:266
  17.9 0.2 collective-permute-done.3.refs_0_
  18.1 0.0 collective-permute-start.5
  18.1 0.5 collective-permute-start.6
  18.6 3.1 %collective-permute-done.7.received.sooner = f32[32,2304]{1,0:T(8,128)S(1)} collective-permute-done((f32[32,2304]{1,0:T(8,128)S(1)}, f32[32,2304]{1,0:T(8,128)S(1)}, u32[]{:S(2)}, u32[]{:S(2)}) %collective-permute-start.7) | collective-permute-done | bytes 294944 | tf_op jit(solution)/shard_map/ppermute | solution.py:297
  21.7 0.0 collective-permute-done.5.refs_1_
  21.7 0.0 collective-permute-done.6.refs_3_
  21.7 0.1 join.3.refs_2_
  21.8 0.0 copy-done
  21.8 0.1 collective-permute-start.11
  21.9 0.5 collective-permute-start.10
  22.4 1.0 %collective-permute-start.12 = (bf16[1024,512]{1,0:T(8,128)(2,1)S(1)}, bf16[1024,512]{1,0:T(8,128)(2,1)S(1)}, u32[]{:S(2)}, u32[]{:S(2)}) collective-permute-start(bf16[1024,512]{1,0:T(8,128)(2,1)S(1)} %join.3.refs_2_), channel_id=1, source_target_pairs={{0,8},{1,17},{2,10},{3,19},{4,12},{5,21},{6,14},{7,23},{8,0},{9,25... | collective-permute-start | bytes 3145736 | tf_op jit(solution)/shard_map/ppermute | solution.py:297
  23.3 0.5 collective-permute-start.9
  23.8 8.1 %collective-permute-done.9.refs_0_ = bf16[256,512]{1,0:T(8,128)(2,1)S(1)} collective-permute-done((bf16[256,512]{1,0:T(8,128)(2,1)S(1)}, bf16[256,512]{1,0:T(8,128)(2,1)S(1)}, u32[]{:S(2)}, u32[]{:S(2)}) %collective-permute-start.9) | collective-permute-done | bytes 262176 | tf_op jit(solution)/shard_map/ppermute | solution.py:266
  31.9 0.0 collective-permute-done.10.refs_1_
  31.9 0.0 collective-permute-done.11.tokens_pair
  31.9 0.0 collective-permute-start.13
  32.0 0.5 collective-permute-start.16
  32.5 1.0 %collective-permute-done.13.refs_1_ = bf16[256,512]{1,0:T(8,128)(2,1)S(1)} collective-permute-done((bf16[256,512]{1,0:T(8,128)(2,1)S(1)}, bf16[256,512]{1,0:T(8,128)(2,1)S(1)}, u32[]{:S(2)}, u32[]{:S(2)}) %collective-permute-start.13) | collective-permute-done | bytes 262176 | tf_op jit(solution)/shard_map/ppermute | solution.py:266
  33.5 1.0 %collective-permute-start.14 = (bf16[512,512]{1,0:T(8,128)(2,1)S(1)}, bf16[512,512]{1,0:T(8,128)(2,1)S(1)}, u32[]{:S(2)}, u32[]{:S(2)}) collective-permute-start(bf16[512,512]{1,0:T(8,128)(2,1)S(1)} %join.4.refs_3_), channel_id=1, source_target_pairs={{0,8},{1,17},{2,10},{3,19},{4,12},{5,21},{6,14},{7,23},{8,0},{9,25... | collective-permute-start | bytes 1572872 | tf_op jit(solution)/shard_map/ppermute | solution.py:297
  34.5 0.6 collective-permute-start.8
  35.1 2.3 %collective-permute-done.12.value.refs_4_.refs_0_ = bf16[1024,512]{1,0:T(8,128)(2,1)S(1)} collective-permute-done((bf16[1024,512]{1,0:T(8,128)(2,1)S(1)}, bf16[1024,512]{1,0:T(8,128)(2,1)S(1)}, u32[]{:S(2)}, u32[]{:S(2)}) %collective-permute-start.12) | collective-permute-done | bytes 1048608 | tf_op jit(solution)/shard_map/ppermute | solution.py:297
  37.4 1.6 %collective-permute-start.15 = (bf16[256,512]{1,0:T(8,128)(2,1)S(1)}, bf16[256,512]{1,0:T(8,128)(2,1)S(1)}, u32[]{:S(2)}, u32[]{:S(2)}) collective-permute-start(bf16[256,512]{1,0:T(8,128)(2,1)S(1)} %take.1), channel_id=1, source_target_pairs={{0,16},{1,9},{2,18},{3,11},{4,20},{5,13},{6,22},{7,15},{8,24},{9,1... | collective-permute-start | bytes 786440 | tf_op jit(solution)/shard_map/ppermute | solution.py:297
  39.0 5.6 %collective-permute-done.8.later = f32[32,2304]{1,0:T(8,128)S(1)} collective-permute-done((f32[32,2304]{1,0:T(8,128)S(1)}, f32[32,2304]{1,0:T(8,128)S(1)}, u32[]{:S(2)}, u32[]{:S(2)}) %collective-permute-start.8) | collective-permute-done | bytes 294944 | tf_op jit(solution)/shard_map/ppermute | solution.py:297
  44.6 1.5 %low_rank.1 = (bf16[32,8192]{1,0:T(8,128)(2,1)S(1)}, f32[16,512]{1,0:T(8,128)S(1)}, f32[128,16]{1,0:T(8,128)S(1)}, f32[128,512]{1,0:T(8,128)S(1)}, f32[4,128]{1,0:T(4,128)S(1)}) custom-call(bf16[128,8192]{1,0:T(8,128)(2,1)S(1)} %copy-done, f32[4,128]{1,0:T(4,128)S(1)} %get-tuple-element.70.slots, f32[16,2304]{1,0:T(8,128)S(1)} %get-tuple-element.71.own, ...), custom_call_target="tpu_custom_call" | custom-call | bytes 12582912 | tf_op jit(solution)/shard_map/low_rank/pallas_call | solution.py:33
  46.1 0.9 %base.2 = (f32[128,512]{1,0:T(8,128)S(1)}, f32[128,512]{1,0:T(8,128)S(1)}) custom-call(bf16[128,8192]{1,0:T(8,128)(2,1)S(1)} %copy-done, bf16[128,8192]{1,0:T(8,128)(2,1)S(1)} %collective-permute-done.11.tokens_pair, f32[128,512]{1,0:T(8,128)S(1)} %get-tuple-element.87.before, f32[128,512]{1,0:T(8,128)S(1)} %broadcast_in_dim.3.before_pair, ...), custom_call_target="tpu_custom_call" | custom-call | tf_op jit(solution)/shard_map/base/pallas_call | solution.py:33
  47.1 1.1 %collective-permute-done.15.refs_2_.refs_3_.refs_7_ = bf16[256,512]{1,0:T(8,128)(2,1)S(1)} collective-permute-done((bf16[256,512]{1,0:T(8,128)(2,1)S(1)}, bf16[256,512]{1,0:T(8,128)(2,1)S(1)}, u32[]{:S(2)}, u32[]{:S(2)}) %collective-permute-start.15) | collective-permute-done | bytes 262176 | tf_op jit(solution)/shard_map/ppermute | solution.py:297
  48.1 0.0 collective-permute-done.16.refs_1_.refs_2_.refs_6_
  48.1 0.5 collective-permute-done.14.refs_0_.refs_1_.refs_5_
  48.6 0.5 base.3
  49.1 0.0 copy-start.3
  49.2 0.0 copy-start.5
  49.2 0.2 collective-permute-start.17
  49.3 0.2 join.5
  49.5 1.3 %collective-permute-done.17.refs_2_ = f32[128,512]{1,0:T(8,128)S(1)} collective-permute-done((f32[128,512]{1,0:T(8,128)S(1)}, f32[128,512]{1,0:T(8,128)S(1)}, u32[]{:S(2)}, u32[]{:S(2)}) %collective-permute-start.17) | collective-permute-done | bytes 262176 | tf_op jit(solution)/shard_map/ppermute | solution.py:266
  50.8 0.1 collective-permute-start.21
  50.9 0.0 copy-done.3
  50.9 1.6 %key_norm.1 = (bf16[128,512]{1,0:T(8,128)(2,1)}, bf16[128,512]{1,0:T(8,128)(2,1)S(1)}, f32[128,16]{1,0:T(8,128)S(1)}, f32[16,2176]{1,0:T(8,128)S(1)}, bf16[16,21...) custom-call(f32[4,128]{1,0:T(4,128)S(1)} %get-tuple-element.77.told, ...), custom_call_target="tpu_custom_call" | custom-call | tf_op jit(solution)/shard_map/key_norm/pallas_call | solution.py:33
  52.5 1.1 %collective-permute-start.18 = (bf16[16,2176]{1,0:T(8,128)(2,1)S(1)}, bf16[16,2176]{1,0:T(8,128)(2,1)S(1)}, u32[]{:S(2)}, u32[]{:S(2)}) collective-permute-start(bf16[16,2176]{1,0:T(8,128)(2,1)S(1)} %get-tuple-element.101), channel_id=1, source_target_pairs={{0,8},{8,0},{16,24},{24,16},{1,9},{9,1},{17,25},{25,17},{2,10},{10... | collective-permute-start | bytes 208904 | tf_op jit(solution)/shard_map/ppermute | solution.py:266
  53.6 1.3 %collective-permute-start.19 = (bf16[16,2176]{1,0:T(8,128)(2,1)S(1)}, bf16[16,2176]{1,0:T(8,128)(2,1)S(1)}, u32[]{:S(2)}, u32[]{:S(2)}) collective-permute-start(bf16[16,2176]{1,0:T(8,128)(2,1)S(1)} %get-tuple-element.102), channel_id=1, source_target_pairs={{0,16},{8,24},{16,0},{24,8},{1,17},{9,25},{17,1},{25,9},{2,18},{10... | collective-permute-start | bytes 208904 | tf_op jit(solution)/shard_map/ppermute | solution.py:266
  54.9 1.2 %collective-permute-start.20 = (bf16[16,2176]{1,0:T(8,128)(2,1)S(1)}, bf16[16,2176]{1,0:T(8,128)(2,1)S(1)}, u32[]{:S(2)}, u32[]{:S(2)}) collective-permute-start(bf16[16,2176]{1,0:T(8,128)(2,1)S(1)} %get-tuple-element.103), channel_id=1, source_target_pairs={{0,24},{8,16},{16,8},{24,0},{1,25},{9,17},{17,9},{25,1},{2,26},{10... | collective-permute-start | bytes 208904 | tf_op jit(solution)/shard_map/ppermute | solution.py:266
  56.1 0.0 collective-permute-done.21.refs_8_
  56.1 3.8 %input_grad.1 = bf16[128,8192]{1,0:T(8,128)(2,1)} custom-call(bf16[128,512]{1,0:T(8,128)(2,1)S(1)} %get-tuple-element.104.pre_low, f32[128,16]{1,0:T(8,128)S(1)} %get-tuple-element.105.low_grad, bf16[32,8192]{1,0:T(8,128)(2,1)S(1)} %get-tuple-element.106.split, bf16[1024,512]{1,0:T(8,128)(2,1)S(1)} %copy-done.1, ...), custom_call_target="tpu_custom_call" | custom-call | tf_op jit(solution)/shard_map/input_grad/pallas_call | solution.py:33
  60.0 0.0 collective-permute-done.18.refs_1_
  60.0 0.0 collective-permute-done.19.refs_2_
  60.0 0.1 collective-permute-done.20.refs_3_
  60.1 0.9 %grad_sum.1 = (f32[3,16,2048]{2,1,0:T(8,128)}, f32[3,16,128]{2,1,0:T(8,128)}) custom-call(f32[4,128]{1,0:T(4,128)S(1)} %get-tuple-element.77.told, f32[16,2176]{1,0:T(8,128)S(1)} %get-tuple-element.110.refs_0_, bf16[16,2176]{1,0:T(8,128)(2,1)S(1)} %collective-permute-done.18.refs_1_, bf16[16,2176]{1,0:T(8,128)(2,1)S(1)} %collective-permute-done.19.refs_2_, ...), custom_call_target="tpu_custom_call" | custom-call | tf_op jit(solution)/shard_map/grad_sum/pallas_call | solution.py:33
  (9 shorter events, 0.1 us)
Async XLA Ops:
  0.6 21.2 %copy-start.1 = (bf16[1024,512]{1,0:T(8,128)(2,1)S(1)}, bf16[1024,512]{1,0:T(8,128)(2,1)}, u32[]{:S(2)}) copy-start(bf16[1024,512]{1,0:T(8,128)(2,1)} %refs_0_.7) | copy-start | bytes 3145732
  0.6 21.1 %copy-start = (bf16[128,8192]{1,0:T(8,128)(2,1)S(1)}, bf16[128,8192]{1,0:T(8,128)(2,1)}, u32[]{:S(2)}) copy-start(bf16[128,8192]{1,0:T(8,128)(2,1)} %refs_0_.6) | copy-start | bytes 6291460
  1.8 16.1 %collective-permute-start.4 = (bf16[256,512]{1,0:T(8,128)(2,1)S(1)}, bf16[256,512]{1,0:T(8,128)(2,1)S(1)}, u32[]{:S(2)}, u32[]{:S(2)}) collective-permute-start(bf16[256,512]{1,0:T(8,128)(2,1)S(1)} %constant_dynamic-slice_fusion), channel_id=1, source_target_pairs={{0,4},{1,5},{2,6},{3,7},{4,0},{5,1},{6,2},{7,3},{8,12},{9,13},{10,... | collective-permute-start | bytes 786440 | tf_op jit(solution)/shard_map/ppermute | solution.py:266
  5.9 12.2 %collective-permute-start.3 = (bf16[256,512]{1,0:T(8,128)(2,1)S(1)}, bf16[256,512]{1,0:T(8,128)(2,1)S(1)}, u32[]{:S(2)}, u32[]{:S(2)}) collective-permute-start(bf16[256,512]{1,0:T(8,128)(2,1)S(1)} %constant_dynamic-slice_fusion), channel_id=1, source_target_pairs={{0,2},{1,3},{2,0},{3,1},{4,6},{5,7},{6,4},{7,5},{8,10},{9,11},{10,... | collective-permute-start | bytes 786440 | tf_op jit(solution)/shard_map/ppermute | solution.py:266
  8.2 6.0 %collective-permute-start.2 = (f32[1,128]{1,0:T(1,128)S(1)}, f32[1,128]{1,0:T(1,128)S(1)}, u32[]{:S(2)}, u32[]{:S(2)}) collective-permute-start(f32[1,128]{1,0:T(1,128)S(1)} %info.1.refs_0_), channel_id=1, source_target_pairs={{0,24},{8,16},{16,8},{24,0},{1,25},{9,17},{17,9},{25,1},{2,26},{10... | collective-permute-start | bytes 1544 | tf_op jit(solution)/shard_map/ppermute | solution.py:266
  10.6 3.5 %collective-permute-start.1 = (f32[1,128]{1,0:T(1,128)S(1)}, f32[1,128]{1,0:T(1,128)S(1)}, u32[]{:S(2)}, u32[]{:S(2)}) collective-permute-start(f32[1,128]{1,0:T(1,128)S(1)} %info.1.refs_0_), channel_id=1, source_target_pairs={{0,16},{8,24},{16,0},{24,8},{1,17},{9,25},{17,1},{25,9},{2,18},{10... | collective-permute-start | bytes 1544 | tf_op jit(solution)/shard_map/ppermute | solution.py:266
  11.1 3.5 %collective-permute-start = (f32[1,128]{1,0:T(1,128)S(1)}, f32[1,128]{1,0:T(1,128)S(1)}, u32[]{:S(2)}, u32[]{:S(2)}) collective-permute-start(f32[1,128]{1,0:T(1,128)S(1)} %info.1.refs_0_), channel_id=1, source_target_pairs={{0,8},{8,0},{16,24},{24,16},{1,9},{9,1},{17,25},{25,17},{2,10},{10... | collective-permute-start | bytes 1544 | tf_op jit(solution)/shard_map/ppermute | solution.py:266
  12.3 1.0 %copy-start.2 = (f32[3,2048,16]{1,2,0:T(8,128)S(1)}, f32[3,2048,16]{1,2,0:T(8,128)}, u32[]{:S(2)}) copy-start(f32[3,2048,16]{1,2,0:T(8,128)} %param.10) | copy-start | bytes 1179652
  13.3 0.7 %copy-start.4 = (f32[3,16,128]{2,1,0:T(8,128)S(1)}, f32[3,16,128]{2,1,0:T(8,128)}, u32[]{:S(2)}) copy-start(f32[3,16,128]{2,1,0:T(8,128)} %up.1) | copy-start | bytes 73732
  14.9 6.8 %collective-permute-start.7 = (f32[32,2304]{1,0:T(8,128)S(1)}, f32[32,2304]{1,0:T(8,128)S(1)}, u32[]{:S(2)}, u32[]{:S(2)}) collective-permute-start(f32[32,2304]{1,0:T(8,128)S(1)} %get-tuple-element.72), channel_id=1, source_target_pairs={{0,8},{1,17},{2,10},{3,19},{4,12},{5,21},{6,14},{7,23},{8,0},{9,25... | collective-permute-start | bytes 884744 | tf_op jit(solution)/shard_map/ppermute | solution.py:297
  18.1 3.6 %collective-permute-start.5 = (bf16[256,512]{1,0:T(8,128)(2,1)S(1)}, bf16[256,512]{1,0:T(8,128)(2,1)S(1)}, u32[]{:S(2)}, u32[]{:S(2)}) collective-permute-start(bf16[256,512]{1,0:T(8,128)(2,1)S(1)} %collective-permute-done.3.refs_0_), channel_id=1, source_target_pairs={{0,1},{1,0},{2,3},{3,2},{4,5},{5,4},{6,7},{7,6},{8,9},{9,8},{10,11... | collective-permute-start | bytes 786440 | tf_op jit(solution)/shard_map/ppermute | solution.py:266
  18.1 3.6 %collective-permute-start.6 = (bf16[256,512]{1,0:T(8,128)(2,1)S(1)}, bf16[256,512]{1,0:T(8,128)(2,1)S(1)}, u32[]{:S(2)}, u32[]{:S(2)}) collective-permute-start(bf16[256,512]{1,0:T(8,128)(2,1)S(1)} %collective-permute-done.4.refs_2_), channel_id=1, source_target_pairs={{0,1},{1,0},{2,3},{3,2},{4,5},{5,4},{6,7},{7,6},{8,9},{9,8},{10,11... | collective-permute-start | bytes 786440 | tf_op jit(solution)/shard_map/ppermute | solution.py:266
  21.8 10.1 %collective-permute-start.11 = (bf16[128,8192]{1,0:T(8,128)(2,1)S(1)}, bf16[128,8192]{1,0:T(8,128)(2,1)S(1)}, u32[]{:S(2)}, u32[]{:S(2)}) collective-permute-start(bf16[128,8192]{1,0:T(8,128)(2,1)S(1)} %copy-done), channel_id=1, source_target_pairs={{0,1},{1,0},{2,3},{3,2},{4,5},{5,4},{6,7},{7,6},{8,9},{9,8},{10,11... | collective-permute-start | bytes 6291464 | tf_op jit(solution)/shard_map/ppermute | solution.py:266
  21.9 10.0 %collective-permute-start.10 = (bf16[1024,512]{1,0:T(8,128)(2,1)S(1)}, bf16[1024,512]{1,0:T(8,128)(2,1)S(1)}, u32[]{:S(2)}, u32[]{:S(2)}) collective-permute-start(bf16[1024,512]{1,0:T(8,128)(2,1)S(1)} %copy-done.1), channel_id=1, source_target_pairs={{0,1},{1,0},{2,3},{3,2},{4,5},{5,4},{6,7},{7,6},{8,9},{9,8},{10,11... | collective-permute-start | bytes 3145736 | tf_op jit(solution)/shard_map/ppermute | solution.py:266
  22.4 15.0 %collective-permute-start.12 = (bf16[1024,512]{1,0:T(8,128)(2,1)S(1)}, bf16[1024,512]{1,0:T(8,128)(2,1)S(1)}, u32[]{:S(2)}, u32[]{:S(2)}) collective-permute-start(bf16[1024,512]{1,0:T(8,128)(2,1)S(1)} %join.3.refs_2_), channel_id=1, source_target_pairs={{0,8},{1,17},{2,10},{3,19},{4,12},{5,21},{6,14},{7,23},{8,0},{9,25... | collective-permute-start | bytes 3145736 | tf_op jit(solution)/shard_map/ppermute | solution.py:297
  23.3 8.6 %collective-permute-start.9 = (bf16[256,512]{1,0:T(8,128)(2,1)S(1)}, bf16[256,512]{1,0:T(8,128)(2,1)S(1)}, u32[]{:S(2)}, u32[]{:S(2)}) collective-permute-start(bf16[256,512]{1,0:T(8,128)(2,1)S(1)} %collective-permute-done.4.refs_2_), channel_id=1, source_target_pairs={{0,2},{1,3},{2,0},{3,1},{4,6},{5,7},{6,4},{7,5},{8,10},{9,11},{10,... | collective-permute-start | bytes 786440 | tf_op jit(solution)/shard_map/ppermute | solution.py:266
  31.9 1.5 %collective-permute-start.13 = (bf16[256,512]{1,0:T(8,128)(2,1)S(1)}, bf16[256,512]{1,0:T(8,128)(2,1)S(1)}, u32[]{:S(2)}, u32[]{:S(2)}) collective-permute-start(bf16[256,512]{1,0:T(8,128)(2,1)S(1)} %collective-permute-done.9.refs_0_), channel_id=1, source_target_pairs={{0,1},{1,0},{2,3},{3,2},{4,5},{5,4},{6,7},{7,6},{8,9},{9,8},{10,11... | collective-permute-start | bytes 786440 | tf_op jit(solution)/shard_map/ppermute | solution.py:266
  32.0 16.2 %collective-permute-start.16 = (bf16[512,512]{1,0:T(8,128)(2,1)S(1)}, bf16[512,512]{1,0:T(8,128)(2,1)S(1)}, u32[]{:S(2)}, u32[]{:S(2)}) collective-permute-start(bf16[512,512]{1,0:T(8,128)(2,1)S(1)} %far.1), channel_id=1, source_target_pairs={{0,2},{1,7},{2,0},{3,5},{4,6},{5,3},{6,4},{7,1},{8,10},{9,15},{10,... | collective-permute-start | bytes 1572872 | tf_op jit(solution)/shard_map/ppermute | solution.py:297
  33.5 15.1 %collective-permute-start.14 = (bf16[512,512]{1,0:T(8,128)(2,1)S(1)}, bf16[512,512]{1,0:T(8,128)(2,1)S(1)}, u32[]{:S(2)}, u32[]{:S(2)}) collective-permute-start(bf16[512,512]{1,0:T(8,128)(2,1)S(1)} %join.4.refs_3_), channel_id=1, source_target_pairs={{0,8},{1,17},{2,10},{3,19},{4,12},{5,21},{6,14},{7,23},{8,0},{9,25... | collective-permute-start | bytes 1572872 | tf_op jit(solution)/shard_map/ppermute | solution.py:297
  34.5 10.0 %collective-permute-start.8 = (f32[32,2304]{1,0:T(8,128)S(1)}, f32[32,2304]{1,0:T(8,128)S(1)}, u32[]{:S(2)}, u32[]{:S(2)}) collective-permute-start(f32[32,2304]{1,0:T(8,128)S(1)} %pass_on.1), channel_id=1, source_target_pairs={{0,16},{1,9},{2,18},{3,11},{4,20},{5,13},{6,22},{7,15},{8,24},{9,1... | collective-permute-start | bytes 884744 | tf_op jit(solution)/shard_map/ppermute | solution.py:297
  37.4 10.7 %collective-permute-start.15 = (bf16[256,512]{1,0:T(8,128)(2,1)S(1)}, bf16[256,512]{1,0:T(8,128)(2,1)S(1)}, u32[]{:S(2)}, u32[]{:S(2)}) collective-permute-start(bf16[256,512]{1,0:T(8,128)(2,1)S(1)} %take.1), channel_id=1, source_target_pairs={{0,16},{1,9},{2,18},{3,11},{4,20},{5,13},{6,22},{7,15},{8,24},{9,1... | collective-permute-start | bytes 786440 | tf_op jit(solution)/shard_map/ppermute | solution.py:297
  49.1 1.8 %copy-start.3 = (bf16[128,512]{1,0:T(8,128)(2,1)S(1)}, bf16[128,512]{1,0:T(8,128)(2,1)}, u32[]{:S(2)}) copy-start(bf16[128,512]{1,0:T(8,128)(2,1)} %refs_3_.1) | copy-start | bytes 393220
  49.2 1.8 %copy-start.5 = (f32[128]{0:T(128)S(1)}, f32[128]{0:T(128)}, u32[]{:S(2)}) copy-start(f32[128]{0:T(128)} %param.12) | copy-start | bytes 1540
  49.2 1.6 %collective-permute-start.17 = (f32[128,512]{1,0:T(8,128)S(1)}, f32[128,512]{1,0:T(8,128)S(1)}, u32[]{:S(2)}, u32[]{:S(2)}) collective-permute-start(f32[128,512]{1,0:T(8,128)S(1)} %get-tuple-element.96), channel_id=1, source_target_pairs={{0,1},{1,0},{2,3},{3,2},{4,5},{5,4},{6,7},{7,6},{8,9},{9,8},{10,11... | collective-permute-start | bytes 786440 | tf_op jit(solution)/shard_map/ppermute | solution.py:266
  50.8 5.4 %collective-permute-start.21 = (bf16[2304,512]{1,0:T(8,128)(2,1)S(1)}, bf16[2304,512]{1,0:T(8,128)(2,1)S(1)}, u32[]{:S(2)}, u32[]{:S(2)}) collective-permute-start(bf16[2304,512]{1,0:T(8,128)(2,1)S(1)} %join.5), channel_id=1, source_target_pairs={{0,1},{1,0},{2,3},{3,2},{4,5},{5,4},{6,7},{7,6},{8,9},{9,8},{10,11... | collective-permute-start | bytes 7077896 | tf_op jit(solution)/shard_map/ppermute | solution.py:266
  52.5 7.4 %collective-permute-start.18 = (bf16[16,2176]{1,0:T(8,128)(2,1)S(1)}, bf16[16,2176]{1,0:T(8,128)(2,1)S(1)}, u32[]{:S(2)}, u32[]{:S(2)}) collective-permute-start(bf16[16,2176]{1,0:T(8,128)(2,1)S(1)} %get-tuple-element.101), channel_id=1, source_target_pairs={{0,8},{8,0},{16,24},{24,16},{1,9},{9,1},{17,25},{25,17},{2,10},{10... | collective-permute-start | bytes 208904 | tf_op jit(solution)/shard_map/ppermute | solution.py:266
  53.6 6.3 %collective-permute-start.19 = (bf16[16,2176]{1,0:T(8,128)(2,1)S(1)}, bf16[16,2176]{1,0:T(8,128)(2,1)S(1)}, u32[]{:S(2)}, u32[]{:S(2)}) collective-permute-start(bf16[16,2176]{1,0:T(8,128)(2,1)S(1)} %get-tuple-element.102), channel_id=1, source_target_pairs={{0,16},{8,24},{16,0},{24,8},{1,17},{9,25},{17,1},{25,9},{2,18},{10... | collective-permute-start | bytes 208904 | tf_op jit(solution)/shard_map/ppermute | solution.py:266
  54.9 5.2 %collective-permute-start.20 = (bf16[16,2176]{1,0:T(8,128)(2,1)S(1)}, bf16[16,2176]{1,0:T(8,128)(2,1)S(1)}, u32[]{:S(2)}, u32[]{:S(2)}) collective-permute-start(bf16[16,2176]{1,0:T(8,128)(2,1)S(1)} %get-tuple-element.103), channel_id=1, source_target_pairs={{0,24},{8,16},{16,8},{24,0},{1,25},{9,17},{17,9},{25,1},{2,26},{10... | collective-permute-start | bytes 208904 | tf_op jit(solution)/shard_map/ppermute | solution.py:266

commit v7 on v6

--- a/solution.py
+++ b/solution.py
@@ -123,10 +123,13 @@
         columns = pl.ds(pl.multiple_of(part * down_width, 128), down_width)
         high, low = split_two(message[:, :down_width])
         split[:rank, columns] = high
-        split[rank:, columns] = low
+        split[rank : 2 * rank, columns] = low
+        split[2 * rank :, columns] = high
         columns = pl.ds(pl.multiple_of(part * up_width, 128), up_width)
         up[:, columns] = message[:, down_width : down_width + up_width]
-    both = lax.dot_general(tokens[...], split[...], (((1,), (1,)), ((), ())), preferred_element_type=F32)
+    both = lax.dot_general(
+        tokens[...], split[: 2 * rank, :], (((1,), (1,)), ((), ())), preferred_element_type=F32
+    )
     low_rank[...] = both[:, :rank] + both[:, rank:]
     total[...] = adapter_scale * jnp.dot(low_rank[...], up[...], precision=HIGHEST, preferred_element_type=F32)
 
@@ -230,9 +233,8 @@
         if index == 0 or piece["buffer"] != pieces[index - 1]["buffer"]:
             whole = jnp.dot(buffers[piece["buffer"]][...], turned, preferred_element_type=F32).T
         columns = pl.ds(column_of(place, piece, *sizes), piece["rows"])
-        right = jnp.concatenate([split[:, columns], split[:rank, columns]], axis=0)
         value = whole[:, piece["first"] : piece["first"] + piece["rows"]]
-        value = value + jnp.dot(left, right, preferred_element_type=F32)
+        value = value + jnp.dot(left, split[:, columns], preferred_element_type=F32)
         held[:, columns] = value.astype(BF16)
         copies.append(pltpu.make_async_copy(held.at[:, columns], out.at[:, columns], copied.at[index]))
         copies[-1].start()
@@ -370,7 +372,7 @@
     split, up, low_rank, total, told = call(
         low_rank_kernel,
         [
-            ((2 * rank, model_width), BF16),
+            ((3 * rank, model_width), BF16),
             ((rank, key_width), F32),
             ((rows, rank), F32),
             ((rows, key_width), F32),

time: 61.3 us -> 61.3 us (level)
  no operation moved by 1% of the time
where the time goes in v7:
time: 61.3 us; the launch traced here: 61 us
  waiting for transfers between devices  25.6 us (42%)
  starting transfers between devices  20.3 us (33%)
  Pallas kernels  10.1 us (16%)
  local copies, waits for them, and re-layouts  2.89 us (5%)
  between operations  2.13 us (3%)
    ppermute x16, starting transfers between devices, flip(): return lax.ppermute(value, axis, [(i, i ^ bits) for i in range(size)])  14.6 us
    ppermute x16, waiting for transfers between devices, flip(): return lax.ppermute(value, axis, [(i, i ^ bits) for i in range(size)])  13.2 us
    ppermute x6, waiting for transfers between devices, over_split(): return lax.ppermute(value, ('dp', 'fsdp'), pairs)  12.5 us
    pallas_call x15, Pallas kernels, call(): pl.pallas_call(kernel, out_shape=[jax.ShapeDtypeStruct(shape, dtype) for...  10.1 us
    ppermute x6, starting transfers between devices, over_split(): return lax.ppermute(value, ('dp', 'fsdp'), pairs)  5.7 us
    unnamed x12, local copies, waits for them, and re-layouts  1.75 us
  transfers between devices with their start and end apart: 22, of which 12 were waited for; matrix products, arithmetic and copies ran while one was open for 0% of the time, Pallas kernels for 14%

profile of v7, /device:TPU:0, one launch (start us, length us, event | category | flops | bytes accessed | tf_op | source)
XLA Modules:
  0.0 61.0 jit_solution(13376401185104524805)
XLA Ops:
  0.6 0.0 copy-start.1
  0.6 0.0 copy-start
  0.7 1.1 %constant_dynamic-slice_fusion = bf16[256,512]{1,0:T(8,128)(2,1)S(1)} fusion(bf16[1024,512]{1,0:T(8,128)(2,1)} %refs_0_.7, s32[]{:T(128)S(6)} %select_n.3), kind=kLoop, calls=%fused_computation | loop fusion | bytes 524292 | tf_op jit(solution)/shard_map/dynamic_slice | solution.py:310
  1.8 4.1 %collective-permute-start.4 = (bf16[256,512]{1,0:T(8,128)(2,1)S(1)}, bf16[256,512]{1,0:T(8,128)(2,1)S(1)}, u32[]{:S(2)}, u32[]{:S(2)}) collective-permute-start(bf16[256,512]{1,0:T(8,128)(2,1)S(1)} %constant_dynamic-slice_fusion), channel_id=1, source_target_pairs={{0,4},{1,5},{2,6},{3,7},{4,0},{5,1},{6,2},{7,3},{8,12},{9,13},{10,... | collective-permute-start | bytes 786440 | tf_op jit(solution)/shard_map/ppermute | solution.py:268
  5.9 1.6 %collective-permute-start.3 = (bf16[256,512]{1,0:T(8,128)(2,1)S(1)}, bf16[256,512]{1,0:T(8,128)(2,1)S(1)}, u32[]{:S(2)}, u32[]{:S(2)}) collective-permute-start(bf16[256,512]{1,0:T(8,128)(2,1)S(1)} %constant_dynamic-slice_fusion), channel_id=1, source_target_pairs={{0,2},{1,3},{2,0},{3,1},{4,6},{5,7},{6,4},{7,5},{8,10},{9,11},{10,... | collective-permute-start | bytes 786440 | tf_op jit(solution)/shard_map/ppermute | solution.py:268
  8.1 0.1 info.1.refs_0_
  8.2 2.4 %collective-permute-start.2 = (f32[1,128]{1,0:T(1,128)S(1)}, f32[1,128]{1,0:T(1,128)S(1)}, u32[]{:S(2)}, u32[]{:S(2)}) collective-permute-start(f32[1,128]{1,0:T(1,128)S(1)} %info.1.refs_0_), channel_id=1, source_target_pairs={{0,24},{8,16},{16,8},{24,0},{1,25},{9,17},{17,9},{25,1},{2,26},{10... | collective-permute-start | bytes 1544 | tf_op jit(solution)/shard_map/ppermute | solution.py:268
  10.6 0.5 collective-permute-start.1
  11.1 0.5 collective-permute-start
  12.3 0.0 copy-start.2
  12.3 1.0 %copy-done.2 = f32[3,2048,16]{1,2,0:T(8,128)S(1)} copy-done((f32[3,2048,16]{1,2,0:T(8,128)S(1)}, f32[3,2048,16]{1,2,0:T(8,128)}, u32[]{:S(2)}) %copy-start.2) | copy-done | bytes 393240
  13.3 0.7 %copy-done.4 = f32[3,16,128]{2,1,0:T(8,128)S(1)} copy-done((f32[3,16,128]{2,1,0:T(8,128)S(1)}, f32[3,16,128]{2,1,0:T(8,128)}, u32[]{:S(2)}) %copy-start.4) | copy-done | bytes 24600
  14.1 0.1 hold.1
  14.1 0.0 collective-permute-done.2.refs_3_
  14.1 0.0 collective-permute-done.1.refs_2_
  14.2 0.5 collective-permute-done.refs_1_
  14.7 0.2 adapter_messages.1
  14.9 1.0 %collective-permute-start.7 = (f32[32,2304]{1,0:T(8,128)S(1)}, f32[32,2304]{1,0:T(8,128)S(1)}, u32[]{:S(2)}, u32[]{:S(2)}) collective-permute-start(f32[32,2304]{1,0:T(8,128)S(1)} %get-tuple-element.72), channel_id=1, source_target_pairs={{0,8},{1,17},{2,10},{3,19},{4,12},{5,21},{6,14},{7,23},{8,0},{9,25... | collective-permute-start | bytes 884744 | tf_op jit(solution)/shard_map/ppermute | solution.py:299
  15.9 2.0 %collective-permute-done.4.refs_2_ = bf16[256,512]{1,0:T(8,128)(2,1)S(1)} collective-permute-done((bf16[256,512]{1,0:T(8,128)(2,1)S(1)}, bf16[256,512]{1,0:T(8,128)(2,1)S(1)}, u32[]{:S(2)}, u32[]{:S(2)}) %collective-permute-start.4) | collective-permute-done | bytes 262176 | tf_op jit(solution)/shard_map/ppermute | solution.py:268
  17.9 0.2 collective-permute-done.3.refs_0_
  18.1 0.0 collective-permute-start.5
  18.1 0.5 collective-permute-start.6
  18.6 3.1 %collective-permute-done.7.received.sooner = f32[32,2304]{1,0:T(8,128)S(1)} collective-permute-done((f32[32,2304]{1,0:T(8,128)S(1)}, f32[32,2304]{1,0:T(8,128)S(1)}, u32[]{:S(2)}, u32[]{:S(2)}) %collective-permute-start.7) | collective-permute-done | bytes 294944 | tf_op jit(solution)/shard_map/ppermute | solution.py:299
  21.7 0.0 collective-permute-done.5.refs_1_
  21.7 0.0 collective-permute-done.6.refs_3_
  21.7 0.1 join.3.refs_2_
  21.8 0.1 collective-permute-start.11
  21.9 0.0 copy-done.1
  21.9 0.5 collective-permute-start.10
  22.4 1.0 %collective-permute-start.12 = (bf16[1024,512]{1,0:T(8,128)(2,1)S(1)}, bf16[1024,512]{1,0:T(8,128)(2,1)S(1)}, u32[]{:S(2)}, u32[]{:S(2)}) collective-permute-start(bf16[1024,512]{1,0:T(8,128)(2,1)S(1)} %join.3.refs_2_), channel_id=1, source_target_pairs={{0,8},{1,17},{2,10},{3,19},{4,12},{5,21},{6,14},{7,23},{8,0},{9,25... | collective-permute-start | bytes 3145736 | tf_op jit(solution)/shard_map/ppermute | solution.py:299
  23.3 0.5 collective-permute-start.9
  23.8 8.1 %collective-permute-done.9.refs_0_ = bf16[256,512]{1,0:T(8,128)(2,1)S(1)} collective-permute-done((bf16[256,512]{1,0:T(8,128)(2,1)S(1)}, bf16[256,512]{1,0:T(8,128)(2,1)S(1)}, u32[]{:S(2)}, u32[]{:S(2)}) %collective-permute-start.9) | collective-permute-done | bytes 262176 | tf_op jit(solution)/shard_map/ppermute | solution.py:268
  31.9 0.0 collective-permute-done.10.refs_1_
  31.9 0.0 collective-permute-done.11.tokens_pair
  31.9 0.0 collective-permute-start.13
  32.0 0.5 collective-permute-start.16
  32.5 1.0 %collective-permute-done.13.refs_1_ = bf16[256,512]{1,0:T(8,128)(2,1)S(1)} collective-permute-done((bf16[256,512]{1,0:T(8,128)(2,1)S(1)}, bf16[256,512]{1,0:T(8,128)(2,1)S(1)}, u32[]{:S(2)}, u32[]{:S(2)}) %collective-permute-start.13) | collective-permute-done | bytes 262176 | tf_op jit(solution)/shard_map/ppermute | solution.py:268
  33.5 1.0 %collective-permute-start.14 = (bf16[512,512]{1,0:T(8,128)(2,1)S(1)}, bf16[512,512]{1,0:T(8,128)(2,1)S(1)}, u32[]{:S(2)}, u32[]{:S(2)}) collective-permute-start(bf16[512,512]{1,0:T(8,128)(2,1)S(1)} %join.4.refs_3_), channel_id=1, source_target_pairs={{0,8},{1,17},{2,10},{3,19},{4,12},{5,21},{6,14},{7,23},{8,0},{9,25... | collective-permute-start | bytes 1572872 | tf_op jit(solution)/shard_map/ppermute | solution.py:299
  34.5 0.6 collective-permute-start.8
  35.1 2.3 %collective-permute-done.12.value.refs_4_.refs_0_ = bf16[1024,512]{1,0:T(8,128)(2,1)S(1)} collective-permute-done((bf16[1024,512]{1,0:T(8,128)(2,1)S(1)}, bf16[1024,512]{1,0:T(8,128)(2,1)S(1)}, u32[]{:S(2)}, u32[]{:S(2)}) %collective-permute-start.12) | collective-permute-done | bytes 1048608 | tf_op jit(solution)/shard_map/ppermute | solution.py:299
  37.4 1.6 %collective-permute-start.15 = (bf16[256,512]{1,0:T(8,128)(2,1)S(1)}, bf16[256,512]{1,0:T(8,128)(2,1)S(1)}, u32[]{:S(2)}, u32[]{:S(2)}) collective-permute-start(bf16[256,512]{1,0:T(8,128)(2,1)S(1)} %take.1), channel_id=1, source_target_pairs={{0,16},{1,9},{2,18},{3,11},{4,20},{5,13},{6,22},{7,15},{8,24},{9,1... | collective-permute-start | bytes 786440 | tf_op jit(solution)/shard_map/ppermute | solution.py:299
  39.0 5.6 %collective-permute-done.8.later = f32[32,2304]{1,0:T(8,128)S(1)} collective-permute-done((f32[32,2304]{1,0:T(8,128)S(1)}, f32[32,2304]{1,0:T(8,128)S(1)}, u32[]{:S(2)}, u32[]{:S(2)}) %collective-permute-start.8) | collective-permute-done | bytes 294944 | tf_op jit(solution)/shard_map/ppermute | solution.py:299
  44.6 1.6 %low_rank.1 = (bf16[48,8192]{1,0:T(8,128)(2,1)S(1)}, f32[16,512]{1,0:T(8,128)S(1)}, f32[128,16]{1,0:T(8,128)S(1)}, f32[128,512]{1,0:T(8,128)S(1)}, f32[4,128]{1,0:T(4,128)S(1)}) custom-call(bf16[128,8192]{1,0:T(8,128)(2,1)S(1)} %copy-done, f32[4,128]{1,0:T(4,128)S(1)} %get-tuple-element.70.slots, f32[16,2304]{1,0:T(8,128)S(1)} %get-tuple-element.71.own, ...), custom_call_target="tpu_custom_call" | custom-call | bytes 12582912 | tf_op jit(solution)/shard_map/low_rank/pallas_call | solution.py:33
  46.1 0.9 %base.2 = (f32[128,512]{1,0:T(8,128)S(1)}, f32[128,512]{1,0:T(8,128)S(1)}) custom-call(bf16[128,8192]{1,0:T(8,128)(2,1)S(1)} %copy-done, bf16[128,8192]{1,0:T(8,128)(2,1)S(1)} %collective-permute-done.11.tokens_pair, f32[128,512]{1,0:T(8,128)S(1)} %get-tuple-element.87.before, f32[128,512]{1,0:T(8,128)S(1)} %broadcast_in_dim.3.before_pair, ...), custom_call_target="tpu_custom_call" | custom-call | tf_op jit(solution)/shard_map/base/pallas_call | solution.py:33
  47.1 1.1 %collective-permute-done.15.refs_2_.refs_3_.refs_7_ = bf16[256,512]{1,0:T(8,128)(2,1)S(1)} collective-permute-done((bf16[256,512]{1,0:T(8,128)(2,1)S(1)}, bf16[256,512]{1,0:T(8,128)(2,1)S(1)}, u32[]{:S(2)}, u32[]{:S(2)}) %collective-permute-start.15) | collective-permute-done | bytes 262176 | tf_op jit(solution)/shard_map/ppermute | solution.py:299
  48.1 0.0 collective-permute-done.16.refs_1_.refs_2_.refs_6_
  48.1 0.5 collective-permute-done.14.refs_0_.refs_1_.refs_5_
  48.6 0.5 base.3
  49.1 0.0 copy-start.3
  49.2 0.0 copy-start.5
  49.2 0.2 collective-permute-start.17
  49.3 0.2 join.5
  49.5 1.3 %collective-permute-done.17.refs_2_ = f32[128,512]{1,0:T(8,128)S(1)} collective-permute-done((f32[128,512]{1,0:T(8,128)S(1)}, f32[128,512]{1,0:T(8,128)S(1)}, u32[]{:S(2)}, u32[]{:S(2)}) %collective-permute-start.17) | collective-permute-done | bytes 262176 | tf_op jit(solution)/shard_map/ppermute | solution.py:268
  50.8 0.1 collective-permute-start.21
  50.9 1.6 %key_norm.1 = (bf16[128,512]{1,0:T(8,128)(2,1)}, bf16[128,512]{1,0:T(8,128)(2,1)S(1)}, f32[128,16]{1,0:T(8,128)S(1)}, f32[16,2176]{1,0:T(8,128)S(1)}, bf16[16,21...) custom-call(f32[4,128]{1,0:T(4,128)S(1)} %get-tuple-element.77.told, ...), custom_call_target="tpu_custom_call" | custom-call | tf_op jit(solution)/shard_map/key_norm/pallas_call | solution.py:33
  52.5 1.1 %collective-permute-start.18 = (bf16[16,2176]{1,0:T(8,128)(2,1)S(1)}, bf16[16,2176]{1,0:T(8,128)(2,1)S(1)}, u32[]{:S(2)}, u32[]{:S(2)}) collective-permute-start(bf16[16,2176]{1,0:T(8,128)(2,1)S(1)} %get-tuple-element.101), channel_id=1, source_target_pairs={{0,8},{8,0},{16,24},{24,16},{1,9},{9,1},{17,25},{25,17},{2,10},{10... | collective-permute-start | bytes 208904 | tf_op jit(solution)/shard_map/ppermute | solution.py:268
  53.6 1.3 %collective-permute-start.19 = (bf16[16,2176]{1,0:T(8,128)(2,1)S(1)}, bf16[16,2176]{1,0:T(8,128)(2,1)S(1)}, u32[]{:S(2)}, u32[]{:S(2)}) collective-permute-start(bf16[16,2176]{1,0:T(8,128)(2,1)S(1)} %get-tuple-element.102), channel_id=1, source_target_pairs={{0,16},{8,24},{16,0},{24,8},{1,17},{9,25},{17,1},{25,9},{2,18},{10... | collective-permute-start | bytes 208904 | tf_op jit(solution)/shard_map/ppermute | solution.py:268
  54.9 1.2 %collective-permute-start.20 = (bf16[16,2176]{1,0:T(8,128)(2,1)S(1)}, bf16[16,2176]{1,0:T(8,128)(2,1)S(1)}, u32[]{:S(2)}, u32[]{:S(2)}) collective-permute-start(bf16[16,2176]{1,0:T(8,128)(2,1)S(1)} %get-tuple-element.103), channel_id=1, source_target_pairs={{0,24},{8,16},{16,8},{24,0},{1,25},{9,17},{17,9},{25,1},{2,26},{10... | collective-permute-start | bytes 208904 | tf_op jit(solution)/shard_map/ppermute | solution.py:268
  56.1 0.0 collective-permute-done.21.refs_8_
  56.1 3.8 %input_grad.1 = bf16[128,8192]{1,0:T(8,128)(2,1)} custom-call(bf16[128,512]{1,0:T(8,128)(2,1)S(1)} %get-tuple-element.104.pre_low, f32[128,16]{1,0:T(8,128)S(1)} %get-tuple-element.105.low_grad, bf16[48,8192]{1,0:T(8,128)(2,1)S(1)} %get-tuple-element.106.split, bf16[1024,512]{1,0:T(8,128)(2,1)S(1)} %copy-done.1, ...), custom_call_target="tpu_custom_call" | custom-call | tf_op jit(solution)/shard_map/input_grad/pallas_call | solution.py:33
  60.0 0.0 collective-permute-done.18.refs_1_
  60.0 0.0 collective-permute-done.19.refs_2_
  60.0 0.1 collective-permute-done.20.refs_3_
  60.1 0.9 %grad_sum.1 = (f32[3,16,2048]{2,1,0:T(8,128)}, f32[3,16,128]{2,1,0:T(8,128)}) custom-call(f32[4,128]{1,0:T(4,128)S(1)} %get-tuple-element.77.told, f32[16,2176]{1,0:T(8,128)S(1)} %get-tuple-element.110.refs_0_, bf16[16,2176]{1,0:T(8,128)(2,1)S(1)} %collective-permute-done.18.refs_1_, bf16[16,2176]{1,0:T(8,128)(2,1)S(1)} %collective-permute-done.19.refs_2_, ...), custom_call_target="tpu_custom_call" | custom-call | tf_op jit(solution)/shard_map/grad_sum/pallas_call | solution.py:33
  (9 shorter events, 0.1 us)
Async XLA Ops:
  0.6 21.2 %copy-start.1 = (bf16[1024,512]{1,0:T(8,128)(2,1)S(1)}, bf16[1024,512]{1,0:T(8,128)(2,1)}, u32[]{:S(2)}) copy-start(bf16[1024,512]{1,0:T(8,128)(2,1)} %refs_0_.7) | copy-start | bytes 3145732
  0.6 21.1 %copy-start = (bf16[128,8192]{1,0:T(8,128)(2,1)S(1)}, bf16[128,8192]{1,0:T(8,128)(2,1)}, u32[]{:S(2)}) copy-start(bf16[128,8192]{1,0:T(8,128)(2,1)} %refs_0_.6) | copy-start | bytes 6291460
  1.8 16.1 %collective-permute-start.4 = (bf16[256,512]{1,0:T(8,128)(2,1)S(1)}, bf16[256,512]{1,0:T(8,128)(2,1)S(1)}, u32[]{:S(2)}, u32[]{:S(2)}) collective-permute-start(bf16[256,512]{1,0:T(8,128)(2,1)S(1)} %constant_dynamic-slice_fusion), channel_id=1, source_target_pairs={{0,4},{1,5},{2,6},{3,7},{4,0},{5,1},{6,2},{7,3},{8,12},{9,13},{10,... | collective-permute-start | bytes 786440 | tf_op jit(solution)/shard_map/ppermute | solution.py:268
  5.9 12.2 %collective-permute-start.3 = (bf16[256,512]{1,0:T(8,128)(2,1)S(1)}, bf16[256,512]{1,0:T(8,128)(2,1)S(1)}, u32[]{:S(2)}, u32[]{:S(2)}) collective-permute-start(bf16[256,512]{1,0:T(8,128)(2,1)S(1)} %constant_dynamic-slice_fusion), channel_id=1, source_target_pairs={{0,2},{1,3},{2,0},{3,1},{4,6},{5,7},{6,4},{7,5},{8,10},{9,11},{10,... | collective-permute-start | bytes 786440 | tf_op jit(solution)/shard_map/ppermute | solution.py:268
  8.2 6.0 %collective-permute-start.2 = (f32[1,128]{1,0:T(1,128)S(1)}, f32[1,128]{1,0:T(1,128)S(1)}, u32[]{:S(2)}, u32[]{:S(2)}) collective-permute-start(f32[1,128]{1,0:T(1,128)S(1)} %info.1.refs_0_), channel_id=1, source_target_pairs={{0,24},{8,16},{16,8},{24,0},{1,25},{9,17},{17,9},{25,1},{2,26},{10... | collective-permute-start | bytes 1544 | tf_op jit(solution)/shard_map/ppermute | solution.py:268
  10.6 3.5 %collective-permute-start.1 = (f32[1,128]{1,0:T(1,128)S(1)}, f32[1,128]{1,0:T(1,128)S(1)}, u32[]{:S(2)}, u32[]{:S(2)}) collective-permute-start(f32[1,128]{1,0:T(1,128)S(1)} %info.1.refs_0_), channel_id=1, source_target_pairs={{0,16},{8,24},{16,0},{24,8},{1,17},{9,25},{17,1},{25,9},{2,18},{10... | collective-permute-start | bytes 1544 | tf_op jit(solution)/shard_map/ppermute | solution.py:268
  11.1 3.5 %collective-permute-start = (f32[1,128]{1,0:T(1,128)S(1)}, f32[1,128]{1,0:T(1,128)S(1)}, u32[]{:S(2)}, u32[]{:S(2)}) collective-permute-start(f32[1,128]{1,0:T(1,128)S(1)} %info.1.refs_0_), channel_id=1, source_target_pairs={{0,8},{8,0},{16,24},{24,16},{1,9},{9,1},{17,25},{25,17},{2,10},{10... | collective-permute-start | bytes 1544 | tf_op jit(solution)/shard_map/ppermute | solution.py:268
  12.3 1.0 %copy-start.2 = (f32[3,2048,16]{1,2,0:T(8,128)S(1)}, f32[3,2048,16]{1,2,0:T(8,128)}, u32[]{:S(2)}) copy-start(f32[3,2048,16]{1,2,0:T(8,128)} %param.10) | copy-start | bytes 1179652
  13.3 0.7 %copy-start.4 = (f32[3,16,128]{2,1,0:T(8,128)S(1)}, f32[3,16,128]{2,1,0:T(8,128)}, u32[]{:S(2)}) copy-start(f32[3,16,128]{2,1,0:T(8,128)} %up.1) | copy-start | bytes 73732
  14.9 6.8 %collective-permute-start.7 = (f32[32,2304]{1,0:T(8,128)S(1)}, f32[32,2304]{1,0:T(8,128)S(1)}, u32[]{:S(2)}, u32[]{:S(2)}) collective-permute-start(f32[32,2304]{1,0:T(8,128)S(1)} %get-tuple-element.72), channel_id=1, source_target_pairs={{0,8},{1,17},{2,10},{3,19},{4,12},{5,21},{6,14},{7,23},{8,0},{9,25... | collective-permute-start | bytes 884744 | tf_op jit(solution)/shard_map/ppermute | solution.py:299
  18.1 3.6 %collective-permute-start.5 = (bf16[256,512]{1,0:T(8,128)(2,1)S(1)}, bf16[256,512]{1,0:T(8,128)(2,1)S(1)}, u32[]{:S(2)}, u32[]{:S(2)}) collective-permute-start(bf16[256,512]{1,0:T(8,128)(2,1)S(1)} %collective-permute-done.3.refs_0_), channel_id=1, source_target_pairs={{0,1},{1,0},{2,3},{3,2},{4,5},{5,4},{6,7},{7,6},{8,9},{9,8},{10,11... | collective-permute-start | bytes 786440 | tf_op jit(solution)/shard_map/ppermute | solution.py:268
  18.1 3.6 %collective-permute-start.6 = (bf16[256,512]{1,0:T(8,128)(2,1)S(1)}, bf16[256,512]{1,0:T(8,128)(2,1)S(1)}, u32[]{:S(2)}, u32[]{:S(2)}) collective-permute-start(bf16[256,512]{1,0:T(8,128)(2,1)S(1)} %collective-permute-done.4.refs_2_), channel_id=1, source_target_pairs={{0,1},{1,0},{2,3},{3,2},{4,5},{5,4},{6,7},{7,6},{8,9},{9,8},{10,11... | collective-permute-start | bytes 786440 | tf_op jit(solution)/shard_map/ppermute | solution.py:268
  21.8 10.1 %collective-permute-start.11 = (bf16[128,8192]{1,0:T(8,128)(2,1)S(1)}, bf16[128,8192]{1,0:T(8,128)(2,1)S(1)}, u32[]{:S(2)}, u32[]{:S(2)}) collective-permute-start(bf16[128,8192]{1,0:T(8,128)(2,1)S(1)} %copy-done), channel_id=1, source_target_pairs={{0,1},{1,0},{2,3},{3,2},{4,5},{5,4},{6,7},{7,6},{8,9},{9,8},{10,11... | collective-permute-start | bytes 6291464 | tf_op jit(solution)/shard_map/ppermute | solution.py:268
  21.9 10.0 %collective-permute-start.10 = (bf16[1024,512]{1,0:T(8,128)(2,1)S(1)}, bf16[1024,512]{1,0:T(8,128)(2,1)S(1)}, u32[]{:S(2)}, u32[]{:S(2)}) collective-permute-start(bf16[1024,512]{1,0:T(8,128)(2,1)S(1)} %copy-done.1), channel_id=1, source_target_pairs={{0,1},{1,0},{2,3},{3,2},{4,5},{5,4},{6,7},{7,6},{8,9},{9,8},{10,11... | collective-permute-start | bytes 3145736 | tf_op jit(solution)/shard_map/ppermute | solution.py:268
  22.4 15.0 %collective-permute-start.12 = (bf16[1024,512]{1,0:T(8,128)(2,1)S(1)}, bf16[1024,512]{1,0:T(8,128)(2,1)S(1)}, u32[]{:S(2)}, u32[]{:S(2)}) collective-permute-start(bf16[1024,512]{1,0:T(8,128)(2,1)S(1)} %join.3.refs_2_), channel_id=1, source_target_pairs={{0,8},{1,17},{2,10},{3,19},{4,12},{5,21},{6,14},{7,23},{8,0},{9,25... | collective-permute-start | bytes 3145736 | tf_op jit(solution)/shard_map/ppermute | solution.py:299
  23.3 8.6 %collective-permute-start.9 = (bf16[256,512]{1,0:T(8,128)(2,1)S(1)}, bf16[256,512]{1,0:T(8,128)(2,1)S(1)}, u32[]{:S(2)}, u32[]{:S(2)}) collective-permute-start(bf16[256,512]{1,0:T(8,128)(2,1)S(1)} %collective-permute-done.4.refs_2_), channel_id=1, source_target_pairs={{0,2},{1,3},{2,0},{3,1},{4,6},{5,7},{6,4},{7,5},{8,10},{9,11},{10,... | collective-permute-start | bytes 786440 | tf_op jit(solution)/shard_map/ppermute | solution.py:268
  31.9 1.5 %collective-permute-start.13 = (bf16[256,512]{1,0:T(8,128)(2,1)S(1)}, bf16[256,512]{1,0:T(8,128)(2,1)S(1)}, u32[]{:S(2)}, u32[]{:S(2)}) collective-permute-start(bf16[256,512]{1,0:T(8,128)(2,1)S(1)} %collective-permute-done.9.refs_0_), channel_id=1, source_target_pairs={{0,1},{1,0},{2,3},{3,2},{4,5},{5,4},{6,7},{7,6},{8,9},{9,8},{10,11... | collective-permute-start | bytes 786440 | tf_op jit(solution)/shard_map/ppermute | solution.py:268
  32.0 16.2 %collective-permute-start.16 = (bf16[512,512]{1,0:T(8,128)(2,1)S(1)}, bf16[512,512]{1,0:T(8,128)(2,1)S(1)}, u32[]{:S(2)}, u32[]{:S(2)}) collective-permute-start(bf16[512,512]{1,0:T(8,128)(2,1)S(1)} %far.1), channel_id=1, source_target_pairs={{0,2},{1,7},{2,0},{3,5},{4,6},{5,3},{6,4},{7,1},{8,10},{9,15},{10,... | collective-permute-start | bytes 1572872 | tf_op jit(solution)/shard_map/ppermute | solution.py:299
  33.5 15.1 %collective-permute-start.14 = (bf16[512,512]{1,0:T(8,128)(2,1)S(1)}, bf16[512,512]{1,0:T(8,128)(2,1)S(1)}, u32[]{:S(2)}, u32[]{:S(2)}) collective-permute-start(bf16[512,512]{1,0:T(8,128)(2,1)S(1)} %join.4.refs_3_), channel_id=1, source_target_pairs={{0,8},{1,17},{2,10},{3,19},{4,12},{5,21},{6,14},{7,23},{8,0},{9,25... | collective-permute-start | bytes 1572872 | tf_op jit(solution)/shard_map/ppermute | solution.py:299
  34.5 10.0 %collective-permute-start.8 = (f32[32,2304]{1,0:T(8,128)S(1)}, f32[32,2304]{1,0:T(8,128)S(1)}, u32[]{:S(2)}, u32[]{:S(2)}) collective-permute-start(f32[32,2304]{1,0:T(8,128)S(1)} %pass_on.1), channel_id=1, source_target_pairs={{0,16},{1,9},{2,18},{3,11},{4,20},{5,13},{6,22},{7,15},{8,24},{9,1... | collective-permute-start | bytes 884744 | tf_op jit(solution)/shard_map/ppermute | solution.py:299
  37.4 10.7 %collective-permute-start.15 = (bf16[256,512]{1,0:T(8,128)(2,1)S(1)}, bf16[256,512]{1,0:T(8,128)(2,1)S(1)}, u32[]{:S(2)}, u32[]{:S(2)}) collective-permute-start(bf16[256,512]{1,0:T(8,128)(2,1)S(1)} %take.1), channel_id=1, source_target_pairs={{0,16},{1,9},{2,18},{3,11},{4,20},{5,13},{6,22},{7,15},{8,24},{9,1... | collective-permute-start | bytes 786440 | tf_op jit(solution)/shard_map/ppermute | solution.py:299
  49.1 1.8 %copy-start.3 = (bf16[128,512]{1,0:T(8,128)(2,1)S(1)}, bf16[128,512]{1,0:T(8,128)(2,1)}, u32[]{:S(2)}) copy-start(bf16[128,512]{1,0:T(8,128)(2,1)} %refs_3_.1) | copy-start | bytes 393220
  49.2 1.8 %copy-start.5 = (f32[128]{0:T(128)S(1)}, f32[128]{0:T(128)}, u32[]{:S(2)}) copy-start(f32[128]{0:T(128)} %param.12) | copy-start | bytes 1540
  49.2 1.6 %collective-permute-start.17 = (f32[128,512]{1,0:T(8,128)S(1)}, f32[128,512]{1,0:T(8,128)S(1)}, u32[]{:S(2)}, u32[]{:S(2)}) collective-permute-start(f32[128,512]{1,0:T(8,128)S(1)} %get-tuple-element.96), channel_id=1, source_target_pairs={{0,1},{1,0},{2,3},{3,2},{4,5},{5,4},{6,7},{7,6},{8,9},{9,8},{10,11... | collective-permute-start | bytes 786440 | tf_op jit(solution)/shard_map/ppermute | solution.py:268
  50.8 5.3 %collective-permute-start.21 = (bf16[2304,512]{1,0:T(8,128)(2,1)S(1)}, bf16[2304,512]{1,0:T(8,128)(2,1)S(1)}, u32[]{:S(2)}, u32[]{:S(2)}) collective-permute-start(bf16[2304,512]{1,0:T(8,128)(2,1)S(1)} %join.5), channel_id=1, source_target_pairs={{0,1},{1,0},{2,3},{3,2},{4,5},{5,4},{6,7},{7,6},{8,9},{9,8},{10,11... | collective-permute-start | bytes 7077896 | tf_op jit(solution)/shard_map/ppermute | solution.py:268
  52.5 7.4 %collective-permute-start.18 = (bf16[16,2176]{1,0:T(8,128)(2,1)S(1)}, bf16[16,2176]{1,0:T(8,128)(2,1)S(1)}, u32[]{:S(2)}, u32[]{:S(2)}) collective-permute-start(bf16[16,2176]{1,0:T(8,128)(2,1)S(1)} %get-tuple-element.101), channel_id=1, source_target_pairs={{0,8},{8,0},{16,24},{24,16},{1,9},{9,1},{17,25},{25,17},{2,10},{10... | collective-permute-start | bytes 208904 | tf_op jit(solution)/shard_map/ppermute | solution.py:268
  53.6 6.3 %collective-permute-start.19 = (bf16[16,2176]{1,0:T(8,128)(2,1)S(1)}, bf16[16,2176]{1,0:T(8,128)(2,1)S(1)}, u32[]{:S(2)}, u32[]{:S(2)}) collective-permute-start(bf16[16,2176]{1,0:T(8,128)(2,1)S(1)} %get-tuple-element.102), channel_id=1, source_target_pairs={{0,16},{8,24},{16,0},{24,8},{1,17},{9,25},{17,1},{25,9},{2,18},{10... | collective-permute-start | bytes 208904 | tf_op jit(solution)/shard_map/ppermute | solution.py:268
  54.9 5.2 %collective-permute-start.20 = (bf16[16,2176]{1,0:T(8,128)(2,1)S(1)}, bf16[16,2176]{1,0:T(8,128)(2,1)S(1)}, u32[]{:S(2)}, u32[]{:S(2)}) collective-permute-start(bf16[16,2176]{1,0:T(8,128)(2,1)S(1)} %get-tuple-element.103), channel_id=1, source_target_pairs={{0,24},{8,16},{16,8},{24,0},{1,25},{9,17},{17,9},{25,1},{2,26},{10... | collective-permute-start | bytes 208904 | tf_op jit(solution)/shard_map/ppermute | solution.py:268

commit v8 on v7

--- a/solution.py
+++ b/solution.py
@@ -418,7 +418,7 @@
     others = two(1, (2, 1), 1) + two(2, (2, 1), 1, last) + two(3, (2, 1), 1, 2 * last) + two((3, 1), 3, 1, 3 * last)
     others = [(lone_pair, others + [piece(2, 3, 1, first=4 * last)])]
     received = [grads[0]] + [over_dp(grads[bits], bits) for bits in range(1, parts)]
-    buffers, pieces = flat(shared + early + late + others)
+    buffers, pieces = flat(shared + others + early + late)
     (input_grad,) = call(
         functools.partial(input_grad_kernel, pieces, (part_rows, parts)),
         [((rows, model_width), BF16)],

time: 61.3 us -> 61.2 us (level)
  transfers between devices with their start and end apart: 22 -> 22, of which waited for: 12 -> 11; matrix products, arithmetic and copies ran while one was open for 0% -> 0% of each run, Pallas kernels for 14% -> 14%
where the time goes in v8:
time: 61.2 us; the launch traced here: 61 us
  waiting for transfers between devices  25.5 us (42%)
  starting transfers between devices  20.3 us (33%)
  Pallas kernels  10.2 us (17%)
  local copies, waits for them, and re-layouts  2.89 us (5%)
  between operations  2.13 us (3%)
    ppermute x16, starting transfers between devices, flip(): return lax.ppermute(value, axis, [(i, i ^ bits) for i in range(size)])  14.6 us
    ppermute x16, waiting for transfers between devices, flip(): return lax.ppermute(value, axis, [(i, i ^ bits) for i in range(size)])  13.1 us
    ppermute x6, waiting for transfers between devices, over_split(): return lax.ppermute(value, ('dp', 'fsdp'), pairs)  12.5 us
    pallas_call x15, Pallas kernels, call(): pl.pallas_call(kernel, out_shape=[jax.ShapeDtypeStruct(shape, dtype) for...  10.2 us
    ppermute x6, starting transfers between devices, over_split(): return lax.ppermute(value, ('dp', 'fsdp'), pairs)  5.7 us
    unnamed x12, local copies, waits for them, and re-layouts  1.75 us
  transfers between devices with their start and end apart: 22, of which 11 were waited for; matrix products, arithmetic and copies ran while one was open for 0% of the time, Pallas kernels for 14%

profile of v8, /device:TPU:0, one launch (start us, length us, event | category | flops | bytes accessed | tf_op | source)
XLA Modules:
  0.0 61.0 jit_solution(13762953265168573482)
XLA Ops:
  0.6 0.0 copy-start.1
  0.6 0.0 copy-start
  0.7 1.1 %constant_dynamic-slice_fusion = bf16[256,512]{1,0:T(8,128)(2,1)S(1)} fusion(bf16[1024,512]{1,0:T(8,128)(2,1)} %refs_0_.7, s32[]{:T(128)S(6)} %select_n.3), kind=kLoop, calls=%fused_computation | loop fusion | bytes 524292 | tf_op jit(solution)/shard_map/dynamic_slice | solution.py:310
  1.8 4.1 %collective-permute-start.4 = (bf16[256,512]{1,0:T(8,128)(2,1)S(1)}, bf16[256,512]{1,0:T(8,128)(2,1)S(1)}, u32[]{:S(2)}, u32[]{:S(2)}) collective-permute-start(bf16[256,512]{1,0:T(8,128)(2,1)S(1)} %constant_dynamic-slice_fusion), channel_id=1, source_target_pairs={{0,4},{1,5},{2,6},{3,7},{4,0},{5,1},{6,2},{7,3},{8,12},{9,13},{10,... | collective-permute-start | bytes 786440 | tf_op jit(solution)/shard_map/ppermute | solution.py:268
  5.9 1.6 %collective-permute-start.3 = (bf16[256,512]{1,0:T(8,128)(2,1)S(1)}, bf16[256,512]{1,0:T(8,128)(2,1)S(1)}, u32[]{:S(2)}, u32[]{:S(2)}) collective-permute-start(bf16[256,512]{1,0:T(8,128)(2,1)S(1)} %constant_dynamic-slice_fusion), channel_id=1, source_target_pairs={{0,2},{1,3},{2,0},{3,1},{4,6},{5,7},{6,4},{7,5},{8,10},{9,11},{10,... | collective-permute-start | bytes 786440 | tf_op jit(solution)/shard_map/ppermute | solution.py:268
  8.1 0.1 info.1.refs_0_
  8.2 2.4 %collective-permute-start.2 = (f32[1,128]{1,0:T(1,128)S(1)}, f32[1,128]{1,0:T(1,128)S(1)}, u32[]{:S(2)}, u32[]{:S(2)}) collective-permute-start(f32[1,128]{1,0:T(1,128)S(1)} %info.1.refs_0_), channel_id=1, source_target_pairs={{0,24},{8,16},{16,8},{24,0},{1,25},{9,17},{17,9},{25,1},{2,26},{10... | collective-permute-start | bytes 1544 | tf_op jit(solution)/shard_map/ppermute | solution.py:268
  10.6 0.5 collective-permute-start.1
  11.1 0.5 collective-permute-start
  12.3 0.0 copy-start.2
  12.3 1.0 %copy-done.2 = f32[3,2048,16]{1,2,0:T(8,128)S(1)} copy-done((f32[3,2048,16]{1,2,0:T(8,128)S(1)}, f32[3,2048,16]{1,2,0:T(8,128)}, u32[]{:S(2)}) %copy-start.2) | copy-done | bytes 393240
  13.3 0.7 %copy-done.4 = f32[3,16,128]{2,1,0:T(8,128)S(1)} copy-done((f32[3,16,128]{2,1,0:T(8,128)S(1)}, f32[3,16,128]{2,1,0:T(8,128)}, u32[]{:S(2)}) %copy-start.4) | copy-done | bytes 24600
  14.1 0.1 hold.1
  14.1 0.0 collective-permute-done.2.refs_3_
  14.1 0.0 collective-permute-done.1.refs_2_
  14.2 0.5 collective-permute-done.refs_1_
  14.7 0.2 adapter_messages.1
  14.9 1.0 %collective-permute-start.7 = (f32[32,2304]{1,0:T(8,128)S(1)}, f32[32,2304]{1,0:T(8,128)S(1)}, u32[]{:S(2)}, u32[]{:S(2)}) collective-permute-start(f32[32,2304]{1,0:T(8,128)S(1)} %get-tuple-element.72), channel_id=1, source_target_pairs={{0,8},{1,17},{2,10},{3,19},{4,12},{5,21},{6,14},{7,23},{8,0},{9,25... | collective-permute-start | bytes 884744 | tf_op jit(solution)/shard_map/ppermute | solution.py:299
  15.9 2.0 %collective-permute-done.4.refs_2_ = bf16[256,512]{1,0:T(8,128)(2,1)S(1)} collective-permute-done((bf16[256,512]{1,0:T(8,128)(2,1)S(1)}, bf16[256,512]{1,0:T(8,128)(2,1)S(1)}, u32[]{:S(2)}, u32[]{:S(2)}) %collective-permute-start.4) | collective-permute-done | bytes 262176 | tf_op jit(solution)/shard_map/ppermute | solution.py:268
  17.9 0.2 collective-permute-done.3.refs_0_
  18.1 0.0 collective-permute-start.5
  18.1 0.5 collective-permute-start.6
  18.6 3.1 %collective-permute-done.7.received.sooner = f32[32,2304]{1,0:T(8,128)S(1)} collective-permute-done((f32[32,2304]{1,0:T(8,128)S(1)}, f32[32,2304]{1,0:T(8,128)S(1)}, u32[]{:S(2)}, u32[]{:S(2)}) %collective-permute-start.7) | collective-permute-done | bytes 294944 | tf_op jit(solution)/shard_map/ppermute | solution.py:299
  21.7 0.0 collective-permute-done.5.refs_1_
  21.7 0.0 collective-permute-done.6.refs_3_
  21.7 0.1 join.3.refs_2_
  21.8 0.0 copy-done
  21.8 0.1 collective-permute-start.11
  21.9 0.5 collective-permute-start.10
  22.4 1.0 %collective-permute-start.12 = (bf16[1024,512]{1,0:T(8,128)(2,1)S(1)}, bf16[1024,512]{1,0:T(8,128)(2,1)S(1)}, u32[]{:S(2)}, u32[]{:S(2)}) collective-permute-start(bf16[1024,512]{1,0:T(8,128)(2,1)S(1)} %join.3.refs_2_), channel_id=1, source_target_pairs={{0,8},{1,17},{2,10},{3,19},{4,12},{5,21},{6,14},{7,23},{8,0},{9,25... | collective-permute-start | bytes 3145736 | tf_op jit(solution)/shard_map/ppermute | solution.py:299
  23.3 0.5 collective-permute-start.9
  23.8 8.1 %collective-permute-done.9.refs_0_ = bf16[256,512]{1,0:T(8,128)(2,1)S(1)} collective-permute-done((bf16[256,512]{1,0:T(8,128)(2,1)S(1)}, bf16[256,512]{1,0:T(8,128)(2,1)S(1)}, u32[]{:S(2)}, u32[]{:S(2)}) %collective-permute-start.9) | collective-permute-done | bytes 262176 | tf_op jit(solution)/shard_map/ppermute | solution.py:268
  31.9 0.0 collective-permute-done.10.refs_1_
  31.9 0.0 collective-permute-done.11.tokens_pair
  31.9 0.0 collective-permute-start.13
  32.0 0.5 collective-permute-start.16
  32.5 1.0 %collective-permute-done.13.refs_1_ = bf16[256,512]{1,0:T(8,128)(2,1)S(1)} collective-permute-done((bf16[256,512]{1,0:T(8,128)(2,1)S(1)}, bf16[256,512]{1,0:T(8,128)(2,1)S(1)}, u32[]{:S(2)}, u32[]{:S(2)}) %collective-permute-start.13) | collective-permute-done | bytes 262176 | tf_op jit(solution)/shard_map/ppermute | solution.py:268
  33.5 1.0 %collective-permute-start.14 = (bf16[512,512]{1,0:T(8,128)(2,1)S(1)}, bf16[512,512]{1,0:T(8,128)(2,1)S(1)}, u32[]{:S(2)}, u32[]{:S(2)}) collective-permute-start(bf16[512,512]{1,0:T(8,128)(2,1)S(1)} %join.4.refs_3_), channel_id=1, source_target_pairs={{0,8},{1,17},{2,10},{3,19},{4,12},{5,21},{6,14},{7,23},{8,0},{9,25... | collective-permute-start | bytes 1572872 | tf_op jit(solution)/shard_map/ppermute | solution.py:299
  34.5 0.6 collective-permute-start.8
  35.1 2.3 %collective-permute-done.12.value.refs_4_.refs_0_.refs_5_ = bf16[1024,512]{1,0:T(8,128)(2,1)S(1)} collective-permute-done((bf16[1024,512]{1,0:T(8,128)(2,1)S(1)}, bf16[1024,512]{1,0:T(8,128)(2,1)S(1)}, u32[]{:S(2)}, u32[]{:S(2)}) %collective-permute-start.12) | collective-permute-done | bytes 1048608 | tf_op jit(solution)/shard_map/ppermute | solution.py:299
  37.4 1.6 %collective-permute-start.15 = (bf16[256,512]{1,0:T(8,128)(2,1)S(1)}, bf16[256,512]{1,0:T(8,128)(2,1)S(1)}, u32[]{:S(2)}, u32[]{:S(2)}) collective-permute-start(bf16[256,512]{1,0:T(8,128)(2,1)S(1)} %take.1), channel_id=1, source_target_pairs={{0,16},{1,9},{2,18},{3,11},{4,20},{5,13},{6,22},{7,15},{8,24},{9,1... | collective-permute-start | bytes 786440 | tf_op jit(solution)/shard_map/ppermute | solution.py:299
  39.0 5.6 %collective-permute-done.8.later = f32[32,2304]{1,0:T(8,128)S(1)} collective-permute-done((f32[32,2304]{1,0:T(8,128)S(1)}, f32[32,2304]{1,0:T(8,128)S(1)}, u32[]{:S(2)}, u32[]{:S(2)}) %collective-permute-start.8) | collective-permute-done | bytes 294944 | tf_op jit(solution)/shard_map/ppermute | solution.py:299
  44.6 1.6 %low_rank.1 = (bf16[48,8192]{1,0:T(8,128)(2,1)S(1)}, f32[16,512]{1,0:T(8,128)S(1)}, f32[128,16]{1,0:T(8,128)S(1)}, f32[128,512]{1,0:T(8,128)S(1)}, f32[4,128]{1,0:T(4,128)S(1)}) custom-call(bf16[128,8192]{1,0:T(8,128)(2,1)S(1)} %copy-done, f32[4,128]{1,0:T(4,128)S(1)} %get-tuple-element.70.slots, f32[16,2304]{1,0:T(8,128)S(1)} %get-tuple-element.71.own, ...), custom_call_target="tpu_custom_call" | custom-call | bytes 12582912 | tf_op jit(solution)/shard_map/low_rank/pallas_call | solution.py:33
  46.1 0.9 %base.2 = (f32[128,512]{1,0:T(8,128)S(1)}, f32[128,512]{1,0:T(8,128)S(1)}) custom-call(bf16[128,8192]{1,0:T(8,128)(2,1)S(1)} %copy-done, bf16[128,8192]{1,0:T(8,128)(2,1)S(1)} %collective-permute-done.11.tokens_pair, f32[128,512]{1,0:T(8,128)S(1)} %get-tuple-element.87.before, f32[128,512]{1,0:T(8,128)S(1)} %broadcast_in_dim.3.before_pair, ...), custom_call_target="tpu_custom_call" | custom-call | tf_op jit(solution)/shard_map/base/pallas_call | solution.py:33
  47.1 1.1 %collective-permute-done.15.refs_2_.refs_3_.refs_8_ = bf16[256,512]{1,0:T(8,128)(2,1)S(1)} collective-permute-done((bf16[256,512]{1,0:T(8,128)(2,1)S(1)}, bf16[256,512]{1,0:T(8,128)(2,1)S(1)}, u32[]{:S(2)}, u32[]{:S(2)}) %collective-permute-start.15) | collective-permute-done | bytes 262176 | tf_op jit(solution)/shard_map/ppermute | solution.py:299
  48.1 0.0 collective-permute-done.16.refs_1_.refs_2_.refs_7_
  48.1 0.5 collective-permute-done.14.refs_0_.refs_1_.refs_6_
  48.6 0.5 base.3
  49.1 0.0 copy-start.3
  49.2 0.0 copy-start.5
  49.2 0.2 collective-permute-start.17
  49.3 0.2 join.5
  49.5 1.3 %collective-permute-done.17.refs_2_ = f32[128,512]{1,0:T(8,128)S(1)} collective-permute-done((f32[128,512]{1,0:T(8,128)S(1)}, f32[128,512]{1,0:T(8,128)S(1)}, u32[]{:S(2)}, u32[]{:S(2)}) %collective-permute-start.17) | collective-permute-done | bytes 262176 | tf_op jit(solution)/shard_map/ppermute | solution.py:268
  50.8 0.1 collective-permute-start.21
  50.9 1.6 %key_norm.1 = (bf16[128,512]{1,0:T(8,128)(2,1)}, bf16[128,512]{1,0:T(8,128)(2,1)S(1)}, f32[128,16]{1,0:T(8,128)S(1)}, f32[16,2176]{1,0:T(8,128)S(1)}, bf16[16,21...) custom-call(f32[4,128]{1,0:T(4,128)S(1)} %get-tuple-element.77.told, ...), custom_call_target="tpu_custom_call" | custom-call | tf_op jit(solution)/shard_map/key_norm/pallas_call | solution.py:33
  52.5 1.1 %collective-permute-start.18 = (bf16[16,2176]{1,0:T(8,128)(2,1)S(1)}, bf16[16,2176]{1,0:T(8,128)(2,1)S(1)}, u32[]{:S(2)}, u32[]{:S(2)}) collective-permute-start(bf16[16,2176]{1,0:T(8,128)(2,1)S(1)} %get-tuple-element.101), channel_id=1, source_target_pairs={{0,8},{8,0},{16,24},{24,16},{1,9},{9,1},{17,25},{25,17},{2,10},{10... | collective-permute-start | bytes 208904 | tf_op jit(solution)/shard_map/ppermute | solution.py:268
  53.6 1.3 %collective-permute-start.19 = (bf16[16,2176]{1,0:T(8,128)(2,1)S(1)}, bf16[16,2176]{1,0:T(8,128)(2,1)S(1)}, u32[]{:S(2)}, u32[]{:S(2)}) collective-permute-start(bf16[16,2176]{1,0:T(8,128)(2,1)S(1)} %get-tuple-element.102), channel_id=1, source_target_pairs={{0,16},{8,24},{16,0},{24,8},{1,17},{9,25},{17,1},{25,9},{2,18},{10... | collective-permute-start | bytes 208904 | tf_op jit(solution)/shard_map/ppermute | solution.py:268
  54.9 1.2 %collective-permute-start.20 = (bf16[16,2176]{1,0:T(8,128)(2,1)S(1)}, bf16[16,2176]{1,0:T(8,128)(2,1)S(1)}, u32[]{:S(2)}, u32[]{:S(2)}) collective-permute-start(bf16[16,2176]{1,0:T(8,128)(2,1)S(1)} %get-tuple-element.103), channel_id=1, source_target_pairs={{0,24},{8,16},{16,8},{24,0},{1,25},{9,17},{17,9},{25,1},{2,26},{10... | collective-permute-start | bytes 208904 | tf_op jit(solution)/shard_map/ppermute | solution.py:268
  56.1 0.0 collective-permute-done.21.refs_4_
  56.1 3.9 %input_grad.1 = bf16[128,8192]{1,0:T(8,128)(2,1)} custom-call(bf16[128,512]{1,0:T(8,128)(2,1)S(1)} %get-tuple-element.104.pre_low, f32[128,16]{1,0:T(8,128)S(1)} %get-tuple-element.105.low_grad, bf16[48,8192]{1,0:T(8,128)(2,1)S(1)} %get-tuple-element.106.split, bf16[1024,512]{1,0:T(8,128)(2,1)S(1)} %copy-done.1, ...), custom_call_target="tpu_custom_call" | custom-call | tf_op jit(solution)/shard_map/input_grad/pallas_call | solution.py:33
  60.1 0.0 collective-permute-done.18.refs_1_
  60.1 0.0 collective-permute-done.19.refs_2_
  60.1 0.0 collective-permute-done.20.refs_3_
  60.1 0.9 %grad_sum.1 = (f32[3,16,2048]{2,1,0:T(8,128)}, f32[3,16,128]{2,1,0:T(8,128)}) custom-call(f32[4,128]{1,0:T(4,128)S(1)} %get-tuple-element.77.told, f32[16,2176]{1,0:T(8,128)S(1)} %get-tuple-element.110.refs_0_, bf16[16,2176]{1,0:T(8,128)(2,1)S(1)} %collective-permute-done.18.refs_1_, bf16[16,2176]{1,0:T(8,128)(2,1)S(1)} %collective-permute-done.19.refs_2_, ...), custom_call_target="tpu_custom_call" | custom-call | tf_op jit(solution)/shard_map/grad_sum/pallas_call | solution.py:33
  (9 shorter events, 0.1 us)
Async XLA Ops:
  0.6 21.2 %copy-start.1 = (bf16[1024,512]{1,0:T(8,128)(2,1)S(1)}, bf16[1024,512]{1,0:T(8,128)(2,1)}, u32[]{:S(2)}) copy-start(bf16[1024,512]{1,0:T(8,128)(2,1)} %refs_0_.7) | copy-start | bytes 3145732
  0.6 21.1 %copy-start = (bf16[128,8192]{1,0:T(8,128)(2,1)S(1)}, bf16[128,8192]{1,0:T(8,128)(2,1)}, u32[]{:S(2)}) copy-start(bf16[128,8192]{1,0:T(8,128)(2,1)} %refs_0_.6) | copy-start | bytes 6291460
  1.8 16.1 %collective-permute-start.4 = (bf16[256,512]{1,0:T(8,128)(2,1)S(1)}, bf16[256,512]{1,0:T(8,128)(2,1)S(1)}, u32[]{:S(2)}, u32[]{:S(2)}) collective-permute-start(bf16[256,512]{1,0:T(8,128)(2,1)S(1)} %constant_dynamic-slice_fusion), channel_id=1, source_target_pairs={{0,4},{1,5},{2,6},{3,7},{4,0},{5,1},{6,2},{7,3},{8,12},{9,13},{10,... | collective-permute-start | bytes 786440 | tf_op jit(solution)/shard_map/ppermute | solution.py:268
  5.9 12.2 %collective-permute-start.3 = (bf16[256,512]{1,0:T(8,128)(2,1)S(1)}, bf16[256,512]{1,0:T(8,128)(2,1)S(1)}, u32[]{:S(2)}, u32[]{:S(2)}) collective-permute-start(bf16[256,512]{1,0:T(8,128)(2,1)S(1)} %constant_dynamic-slice_fusion), channel_id=1, source_target_pairs={{0,2},{1,3},{2,0},{3,1},{4,6},{5,7},{6,4},{7,5},{8,10},{9,11},{10,... | collective-permute-start | bytes 786440 | tf_op jit(solution)/shard_map/ppermute | solution.py:268
  8.2 6.0 %collective-permute-start.2 = (f32[1,128]{1,0:T(1,128)S(1)}, f32[1,128]{1,0:T(1,128)S(1)}, u32[]{:S(2)}, u32[]{:S(2)}) collective-permute-start(f32[1,128]{1,0:T(1,128)S(1)} %info.1.refs_0_), channel_id=1, source_target_pairs={{0,24},{8,16},{16,8},{24,0},{1,25},{9,17},{17,9},{25,1},{2,26},{10... | collective-permute-start | bytes 1544 | tf_op jit(solution)/shard_map/ppermute | solution.py:268
  10.6 3.5 %collective-permute-start.1 = (f32[1,128]{1,0:T(1,128)S(1)}, f32[1,128]{1,0:T(1,128)S(1)}, u32[]{:S(2)}, u32[]{:S(2)}) collective-permute-start(f32[1,128]{1,0:T(1,128)S(1)} %info.1.refs_0_), channel_id=1, source_target_pairs={{0,16},{8,24},{16,0},{24,8},{1,17},{9,25},{17,1},{25,9},{2,18},{10... | collective-permute-start | bytes 1544 | tf_op jit(solution)/shard_map/ppermute | solution.py:268
  11.1 3.5 %collective-permute-start = (f32[1,128]{1,0:T(1,128)S(1)}, f32[1,128]{1,0:T(1,128)S(1)}, u32[]{:S(2)}, u32[]{:S(2)}) collective-permute-start(f32[1,128]{1,0:T(1,128)S(1)} %info.1.refs_0_), channel_id=1, source_target_pairs={{0,8},{8,0},{16,24},{24,16},{1,9},{9,1},{17,25},{25,17},{2,10},{10... | collective-permute-start | bytes 1544 | tf_op jit(solution)/shard_map/ppermute | solution.py:268
  12.3 1.0 %copy-start.2 = (f32[3,2048,16]{1,2,0:T(8,128)S(1)}, f32[3,2048,16]{1,2,0:T(8,128)}, u32[]{:S(2)}) copy-start(f32[3,2048,16]{1,2,0:T(8,128)} %param.10) | copy-start | bytes 1179652
  13.3 0.7 %copy-start.4 = (f32[3,16,128]{2,1,0:T(8,128)S(1)}, f32[3,16,128]{2,1,0:T(8,128)}, u32[]{:S(2)}) copy-start(f32[3,16,128]{2,1,0:T(8,128)} %up.1) | copy-start | bytes 73732
  14.9 6.8 %collective-permute-start.7 = (f32[32,2304]{1,0:T(8,128)S(1)}, f32[32,2304]{1,0:T(8,128)S(1)}, u32[]{:S(2)}, u32[]{:S(2)}) collective-permute-start(f32[32,2304]{1,0:T(8,128)S(1)} %get-tuple-element.72), channel_id=1, source_target_pairs={{0,8},{1,17},{2,10},{3,19},{4,12},{5,21},{6,14},{7,23},{8,0},{9,25... | collective-permute-start | bytes 884744 | tf_op jit(solution)/shard_map/ppermute | solution.py:299
  18.1 3.6 %collective-permute-start.5 = (bf16[256,512]{1,0:T(8,128)(2,1)S(1)}, bf16[256,512]{1,0:T(8,128)(2,1)S(1)}, u32[]{:S(2)}, u32[]{:S(2)}) collective-permute-start(bf16[256,512]{1,0:T(8,128)(2,1)S(1)} %collective-permute-done.3.refs_0_), channel_id=1, source_target_pairs={{0,1},{1,0},{2,3},{3,2},{4,5},{5,4},{6,7},{7,6},{8,9},{9,8},{10,11... | collective-permute-start | bytes 786440 | tf_op jit(solution)/shard_map/ppermute | solution.py:268
  18.1 3.6 %collective-permute-start.6 = (bf16[256,512]{1,0:T(8,128)(2,1)S(1)}, bf16[256,512]{1,0:T(8,128)(2,1)S(1)}, u32[]{:S(2)}, u32[]{:S(2)}) collective-permute-start(bf16[256,512]{1,0:T(8,128)(2,1)S(1)} %collective-permute-done.4.refs_2_), channel_id=1, source_target_pairs={{0,1},{1,0},{2,3},{3,2},{4,5},{5,4},{6,7},{7,6},{8,9},{9,8},{10,11... | collective-permute-start | bytes 786440 | tf_op jit(solution)/shard_map/ppermute | solution.py:268
  21.8 10.1 %collective-permute-start.11 = (bf16[128,8192]{1,0:T(8,128)(2,1)S(1)}, bf16[128,8192]{1,0:T(8,128)(2,1)S(1)}, u32[]{:S(2)}, u32[]{:S(2)}) collective-permute-start(bf16[128,8192]{1,0:T(8,128)(2,1)S(1)} %copy-done), channel_id=1, source_target_pairs={{0,1},{1,0},{2,3},{3,2},{4,5},{5,4},{6,7},{7,6},{8,9},{9,8},{10,11... | collective-permute-start | bytes 6291464 | tf_op jit(solution)/shard_map/ppermute | solution.py:268
  21.9 10.0 %collective-permute-start.10 = (bf16[1024,512]{1,0:T(8,128)(2,1)S(1)}, bf16[1024,512]{1,0:T(8,128)(2,1)S(1)}, u32[]{:S(2)}, u32[]{:S(2)}) collective-permute-start(bf16[1024,512]{1,0:T(8,128)(2,1)S(1)} %copy-done.1), channel_id=1, source_target_pairs={{0,1},{1,0},{2,3},{3,2},{4,5},{5,4},{6,7},{7,6},{8,9},{9,8},{10,11... | collective-permute-start | bytes 3145736 | tf_op jit(solution)/shard_map/ppermute | solution.py:268
  22.4 15.0 %collective-permute-start.12 = (bf16[1024,512]{1,0:T(8,128)(2,1)S(1)}, bf16[1024,512]{1,0:T(8,128)(2,1)S(1)}, u32[]{:S(2)}, u32[]{:S(2)}) collective-permute-start(bf16[1024,512]{1,0:T(8,128)(2,1)S(1)} %join.3.refs_2_), channel_id=1, source_target_pairs={{0,8},{1,17},{2,10},{3,19},{4,12},{5,21},{6,14},{7,23},{8,0},{9,25... | collective-permute-start | bytes 3145736 | tf_op jit(solution)/shard_map/ppermute | solution.py:299
  23.3 8.6 %collective-permute-start.9 = (bf16[256,512]{1,0:T(8,128)(2,1)S(1)}, bf16[256,512]{1,0:T(8,128)(2,1)S(1)}, u32[]{:S(2)}, u32[]{:S(2)}) collective-permute-start(bf16[256,512]{1,0:T(8,128)(2,1)S(1)} %collective-permute-done.4.refs_2_), channel_id=1, source_target_pairs={{0,2},{1,3},{2,0},{3,1},{4,6},{5,7},{6,4},{7,5},{8,10},{9,11},{10,... | collective-permute-start | bytes 786440 | tf_op jit(solution)/shard_map/ppermute | solution.py:268
  31.9 1.5 %collective-permute-start.13 = (bf16[256,512]{1,0:T(8,128)(2,1)S(1)}, bf16[256,512]{1,0:T(8,128)(2,1)S(1)}, u32[]{:S(2)}, u32[]{:S(2)}) collective-permute-start(bf16[256,512]{1,0:T(8,128)(2,1)S(1)} %collective-permute-done.9.refs_0_), channel_id=1, source_target_pairs={{0,1},{1,0},{2,3},{3,2},{4,5},{5,4},{6,7},{7,6},{8,9},{9,8},{10,11... | collective-permute-start | bytes 786440 | tf_op jit(solution)/shard_map/ppermute | solution.py:268
  32.0 16.2 %collective-permute-start.16 = (bf16[512,512]{1,0:T(8,128)(2,1)S(1)}, bf16[512,512]{1,0:T(8,128)(2,1)S(1)}, u32[]{:S(2)}, u32[]{:S(2)}) collective-permute-start(bf16[512,512]{1,0:T(8,128)(2,1)S(1)} %far.1), channel_id=1, source_target_pairs={{0,2},{1,7},{2,0},{3,5},{4,6},{5,3},{6,4},{7,1},{8,10},{9,15},{10,... | collective-permute-start | bytes 1572872 | tf_op jit(solution)/shard_map/ppermute | solution.py:299
  33.5 15.1 %collective-permute-start.14 = (bf16[512,512]{1,0:T(8,128)(2,1)S(1)}, bf16[512,512]{1,0:T(8,128)(2,1)S(1)}, u32[]{:S(2)}, u32[]{:S(2)}) collective-permute-start(bf16[512,512]{1,0:T(8,128)(2,1)S(1)} %join.4.refs_3_), channel_id=1, source_target_pairs={{0,8},{1,17},{2,10},{3,19},{4,12},{5,21},{6,14},{7,23},{8,0},{9,25... | collective-permute-start | bytes 1572872 | tf_op jit(solution)/shard_map/ppermute | solution.py:299
  34.5 10.0 %collective-permute-start.8 = (f32[32,2304]{1,0:T(8,128)S(1)}, f32[32,2304]{1,0:T(8,128)S(1)}, u32[]{:S(2)}, u32[]{:S(2)}) collective-permute-start(f32[32,2304]{1,0:T(8,128)S(1)} %pass_on.1), channel_id=1, source_target_pairs={{0,16},{1,9},{2,18},{3,11},{4,20},{5,13},{6,22},{7,15},{8,24},{9,1... | collective-permute-start | bytes 884744 | tf_op jit(solution)/shard_map/ppermute | solution.py:299
  37.4 10.7 %collective-permute-start.15 = (bf16[256,512]{1,0:T(8,128)(2,1)S(1)}, bf16[256,512]{1,0:T(8,128)(2,1)S(1)}, u32[]{:S(2)}, u32[]{:S(2)}) collective-permute-start(bf16[256,512]{1,0:T(8,128)(2,1)S(1)} %take.1), channel_id=1, source_target_pairs={{0,16},{1,9},{2,18},{3,11},{4,20},{5,13},{6,22},{7,15},{8,24},{9,1... | collective-permute-start | bytes 786440 | tf_op jit(solution)/shard_map/ppermute | solution.py:299
  49.1 1.8 %copy-start.3 = (bf16[128,512]{1,0:T(8,128)(2,1)S(1)}, bf16[128,512]{1,0:T(8,128)(2,1)}, u32[]{:S(2)}) copy-start(bf16[128,512]{1,0:T(8,128)(2,1)} %refs_3_.1) | copy-start | bytes 393220
  49.2 1.8 %copy-start.5 = (f32[128]{0:T(128)S(1)}, f32[128]{0:T(128)}, u32[]{:S(2)}) copy-start(f32[128]{0:T(128)} %param.12) | copy-start | bytes 1540
  49.2 1.6 %collective-permute-start.17 = (f32[128,512]{1,0:T(8,128)S(1)}, f32[128,512]{1,0:T(8,128)S(1)}, u32[]{:S(2)}, u32[]{:S(2)}) collective-permute-start(f32[128,512]{1,0:T(8,128)S(1)} %get-tuple-element.96), channel_id=1, source_target_pairs={{0,1},{1,0},{2,3},{3,2},{4,5},{5,4},{6,7},{7,6},{8,9},{9,8},{10,11... | collective-permute-start | bytes 786440 | tf_op jit(solution)/shard_map/ppermute | solution.py:268
  50.8 5.3 %collective-permute-start.21 = (bf16[2304,512]{1,0:T(8,128)(2,1)S(1)}, bf16[2304,512]{1,0:T(8,128)(2,1)S(1)}, u32[]{:S(2)}, u32[]{:S(2)}) collective-permute-start(bf16[2304,512]{1,0:T(8,128)(2,1)S(1)} %join.5), channel_id=1, source_target_pairs={{0,1},{1,0},{2,3},{3,2},{4,5},{5,4},{6,7},{7,6},{8,9},{9,8},{10,11... | collective-permute-start | bytes 7077896 | tf_op jit(solution)/shard_map/ppermute | solution.py:268
  52.5 7.5 %collective-permute-start.18 = (bf16[16,2176]{1,0:T(8,128)(2,1)S(1)}, bf16[16,2176]{1,0:T(8,128)(2,1)S(1)}, u32[]{:S(2)}, u32[]{:S(2)}) collective-permute-start(bf16[16,2176]{1,0:T(8,128)(2,1)S(1)} %get-tuple-element.101), channel_id=1, source_target_pairs={{0,8},{8,0},{16,24},{24,16},{1,9},{9,1},{17,25},{25,17},{2,10},{10... | collective-permute-start | bytes 208904 | tf_op jit(solution)/shard_map/ppermute | solution.py:268
  53.6 6.5 %collective-permute-start.19 = (bf16[16,2176]{1,0:T(8,128)(2,1)S(1)}, bf16[16,2176]{1,0:T(8,128)(2,1)S(1)}, u32[]{:S(2)}, u32[]{:S(2)}) collective-permute-start(bf16[16,2176]{1,0:T(8,128)(2,1)S(1)} %get-tuple-element.102), channel_id=1, source_target_pairs={{0,16},{8,24},{16,0},{24,8},{1,17},{9,25},{17,1},{25,9},{2,18},{10... | collective-permute-start | bytes 208904 | tf_op jit(solution)/shard_map/ppermute | solution.py:268
  54.9 5.2 %collective-permute-start.20 = (bf16[16,2176]{1,0:T(8,128)(2,1)S(1)}, bf16[16,2176]{1,0:T(8,128)(2,1)S(1)}, u32[]{:S(2)}, u32[]{:S(2)}) collective-permute-start(bf16[16,2176]{1,0:T(8,128)(2,1)S(1)} %get-tuple-element.103), channel_id=1, source_target_pairs={{0,24},{8,16},{16,8},{24,0},{1,25},{9,17},{17,9},{25,1},{2,26},{10... | collective-permute-start | bytes 208904 | tf_op jit(solution)/shard_map/ppermute | solution.py:268
